TPU v7x, 128 devices: a whole 4x4x4 slice. The times are simulated.
128 devices in a mesh: dp: 32 (over y, x, core), mp: 4 (over z).
Axes of the slice: x: 4, y: 4, z: 4, core: 2. Of those that a mesh axis runs over, the one named last changes fastest.
Arguments:
- mel_audio: bfloat16 [128, 80, 2048], P('dp'), may hold values from -6 to 6
- start_noise: bfloat16 [128, 80, 1024], P('dp'), may hold values from -6 to 6
- span_start: int32 [128], replicated, may hold values from 0 to 2047, as said below
- span_length: int32 [128], replicated, may hold values from 1 to 1024, as said below
- block_route: int32 [512], replicated, may hold values from -1 to 191, as said below
- w_input: bfloat16 [160, 1024], replicated, may hold values from -0.5 to 0.5
- attn_gain: float32 [1024], replicated, may hold values from 0.1 to 1.9
- w_qkv: bfloat16 [1024, 3, 1024], P(None, None, 'mp'), may hold values from -4 to 4, as said below
- w_out: bfloat16 [1024, 1024], P('mp'), may hold values from -0.1875 to 0.1875
- final_gain: float32 [1024], replicated, may hold values from 0.1 to 1.9
- w_mel: bfloat16 [80, 1024], replicated, may hold values from -0.1875 to 0.1875
Outputs:
- infilled: float32 [128, 80, 1024], P('dp')
- worker_velocity: float32 [192, 80, 256], P('dp')
Inputs may be any that keep to these rules, and one draw needn't show every extreme that they name: Each span lies inside its utterance: span_start[u] + span_length[u] <= 2048. `span_length`: the spans cover 192 blocks of 256 frames in all (the last block of a span may be partly filled). `block_route`: live block slots name worker slots w * 6 + j of worker w, each worker slot exactly once; empty slots hold -1. No worker receives more than 1 block from the utterances of one dp index (utterances u with the same u // 4), and some worker receives exactly 1 from one. `w_qkv`: Query, key and value projections in that order along the middle dimension.
All inputs are finite; a program needn't handle non-finite values.
Results may differ from a plain program's by a relative error of at most 0.025.
Values may be sent and summed in bfloat16 or wider, within the bound.
No kernel may reach another device: no remote copies, remote signals or barrier semaphores. Data moves between devices by JAX's collectives and lax.ppermute only.
A program may use at most 128 MiB of HBM per device.

v0:
```python
import math

import jax
import jax.numpy as jnp
import numpy as np
from jax import lax
from jax.experimental import pallas as pl
from jax.experimental.pallas import tpu as pltpu
from jax.sharding import PartitionSpec as P

D = 1024
MEL = 80
HEAD_DIM = 64
HEADS = 16
BLOCK = 256
CTX = 128
BLK_UTT = 4
UTT_DEV = 4
WORK_DEV = 6
EULER = 2
FRAMES = 2048
WIN = 512
SPAN_MAX = 1024
SLOT_DEV = 16
N_MP = 4
JOBS = 4
ROWS = 176
PIECE = 48
flow_steps = 32.0
norm_eps = 1e-05
f32 = jnp.float32
bf16 = jnp.bfloat16
VMEM = pltpu.VMEM
SMEM = pltpu.SMEM
LIMIT = 56 * 1024 * 1024


def time_rows():
    half = D // 2
    freqs = np.exp(-math.log(10000.0) * np.arange(half, dtype=np.float32) / half)
    rows = np.zeros((16, D), np.float32)
    for step in range(EULER):
        angles = np.float32(1000.0 * step / flow_steps) * freqs.astype(np.float32)
        e = np.concatenate([np.sin(angles), np.cos(angles)])
        e = e - e.mean()
        rows[2 * step] = e
        rows[2 * step + 1] = e
    return rows


def high_low(rows):
    high = rows.astype(bf16).astype(f32)
    odd = lax.broadcasted_iota(jnp.int32, rows.shape, 0) % 2 == 1
    return jnp.where(odd, rows - high, high)


def fold_kernel(w_in, e_rows, gain, w_qkv, out):
    w = w_in[...].astype(f32)
    wc = w - jnp.mean(w, axis=1, keepdims=True)
    g = gain[...]
    wag = jnp.concatenate([wc * g, high_low(e_rows[...] * g)], axis=0).astype(bf16)
    for c in range(3):
        res = jnp.dot(wag, w_qkv[c], preferred_element_type=f32)
        if c == 0:
            res = res * (math.log2(math.e) / math.sqrt(HEAD_DIM))
        e_res = res[160:176]
        row = lax.broadcasted_iota(jnp.int32, e_res.shape, 0)
        first = e_res[0:1] + e_res[1:2]
        second = e_res[2:3] + e_res[3:4]
        both = jnp.where(row < 2, first, jnp.where(row < 4, second, 0.0))
        out[c, 0:160, :] = res[0:160].astype(bf16)
        out[c, 160:176, :] = high_low(both).astype(bf16)


def prep_kernel(w_in, e_rows, w_out, w_mel, gain, wa_t, wo_t, wm):
    w = w_in[...].astype(f32)
    wc = w - jnp.mean(w, axis=1, keepdims=True)
    wa = jnp.concatenate([wc, high_low(e_rows[...]), jnp.zeros((80, D), f32)], axis=0)
    wa_t[...] = wa.T[:, :ROWS].astype(bf16)
    wo_t[...] = w_out[...].astype(f32).T.astype(bf16)
    m = w_mel[...].astype(f32) * gain[...]
    high = m.astype(bf16)
    wm[0:MEL, :] = high
    wm[MEL : 2 * MEL, :] = (m - high.astype(f32)).astype(bf16)


def main_kernel(
    ids, route, starts, lengths, mel, noise, wa_t, wm,
    wp0, wp1, wp2, wp3, wo0, wo1, wo2, wo3,
    tot_out, v0, v1, v2, v3,
    job_smem, wq_s, wv_s, wk_s, wr_s, win_s, ws_s, wst_s, q_s, k_s, v_s, o_s, x_s, tot_s, stage,
):
    me = ids[0]
    m = ids[1]

    def scan(s, rank):
        dest = route[me * SLOT_DEV + s]
        live = dest >= 0
        mine = jnp.logical_and(live, (rank & 3) == m)

        @pl.when(mine)
        def _():
            job_smem[rank >> 2] = s

        return rank + live.astype(jnp.int32)

    n_live = lax.fori_loop(0, SLOT_DEV, scan, jnp.int32(0))
    n_jobs = (n_live - m + 3) >> 2

    for k, (wp, wo) in enumerate(zip((wp0, wp1, wp2, wp3), (wo0, wo1, wo2, wo3))):
        lanes = slice(256 * k, 256 * k + 256)
        pad = jnp.zeros((256 - ROWS, 256), f32)
        wq_s[lanes, :] = jnp.concatenate([wp[0].astype(f32), pad], axis=0).T.astype(bf16)[:, :ROWS]
        wv_s[lanes, :] = jnp.concatenate([wp[2].astype(f32), pad], axis=0).T.astype(bf16)[:, :ROWS]
        wk_s[:, lanes] = wp[1]
        wr_s[:, lanes] = wo[...]
    wr_s[:, 1024 : 1024 + ROWS] = wa_t[...]

    def job(q, carry):
        s = job_smem[q]
        u = s >> 2
        order = s & 3
        span = starts[me * UTT_DEV + u]
        length = lengths[me * UTT_DEV + u]
        begin = span + BLOCK * order
        count = jnp.minimum(BLOCK, length - BLOCK * order)
        first = begin - CTX
        aligned = jnp.clip((first >> 7) << 7, 0, FRAMES - 640)
        aligned = pl.multiple_of(aligned, 128)
        chunk = mel[u, :, pl.ds(aligned, 640)].astype(f32)
        shift = aligned - first
        shift = jnp.where(shift < 0, shift + 640, shift)
        chunk = pltpu.roll(chunk, shift, 1)[:, :WIN]
        pos = first + lax.broadcasted_iota(jnp.int32, (1, WIN), 1)
        valid = jnp.logical_and(pos >= 0, pos < FRAMES)
        in_span = jnp.logical_and(pos >= span, pos < span + length)
        keep = jnp.logical_and(valid, jnp.logical_not(in_span))
        context = jnp.where(keep, chunk, 0.0)
        own = lax.broadcasted_iota(jnp.int32, (1, BLOCK), 1) < count
        off = pl.multiple_of(order * BLOCK, BLOCK)
        x_s[...] = jnp.where(own, noise[u, :, pl.ds(off, BLOCK)].astype(f32), 0.0)
        tot_s[...] = jnp.zeros((MEL, BLOCK), f32)
        valid_f = valid.astype(f32)
        ones_rows = jnp.broadcast_to(valid_f, (16, WIN)).astype(bf16)

        def step(n, c2):
            xr = x_s[...].astype(bf16).astype(f32)
            side = jnp.zeros((MEL, CTX), f32)
            state = jnp.concatenate([side, xr, side], axis=1)
            flags = (lax.broadcasted_iota(jnp.int32, (16, WIN), 0) >> 1) == n
            win = jnp.concatenate([context, state, flags.astype(f32)], axis=0)
            win = jnp.where(valid, win, win[:, CTX : CTX + 1])
            win_b = win.astype(bf16)
            win_s[...] = win_b
            o_s[1024 : 1024 + ROWS, :] = win_b[:, CTX : CTX + BLOCK]
            hid = jnp.dot(wa_t[...], win_b, preferred_element_type=f32)
            var = jnp.sum(hid * hid, axis=0, keepdims=True) * (1.0 / D)
            rstd = lax.rsqrt(var + norm_eps)
            scaled = win * rstd
            ws_s[...] = scaled.astype(bf16)
            padded = jnp.concatenate([scaled, jnp.zeros((256 - ROWS, WIN), f32)], axis=0)
            wst_s[...] = padded.T.astype(bf16)[:, :ROWS]
            q_s[...] = jnp.dot(
                wq_s[...], ws_s[:, CTX : CTX + BLOCK], preferred_element_type=f32
            ).astype(bf16)
            v_win = (scaled * valid_f).astype(bf16)
            v_s[...] = jnp.dot(wv_s[...], v_win, preferred_element_type=f32).astype(bf16)
            keys = jnp.dot(wst_s[...], wk_s[...], preferred_element_type=f32).astype(bf16)
            for p in range(HEADS // 2):
                k_s[p] = keys[:, 128 * p : 128 * p + 128]

            def heads(g, c3):
                for pp in range(2):
                    p = g * 2 + pp
                    kp = k_s[p]
                    base = pl.multiple_of(p * 128, 128)
                    qp = q_s[pl.ds(base, 128), :]
                    zero = jnp.zeros((HEAD_DIM, BLOCK), bf16)
                    for j in range(2):
                        qh = qp[64 * j : 64 * j + 64]
                        qz = jnp.concatenate([qh, zero] if j == 0 else [zero, qh], axis=0)
                        sc = jnp.dot(kp, qz, preferred_element_type=f32)
                        top = jnp.max(sc, axis=0, keepdims=True)
                        pr = jnp.exp2(sc - top).astype(bf16)
                        vh = v_s[pl.ds(pl.multiple_of(base + 64 * j, 64), 64), :]
                        lhs = jnp.concatenate([vh, ones_rows], axis=0)
                        ov = jnp.dot(lhs, pr, preferred_element_type=f32)
                        o = ov[0:64] / ov[64:65]
                        o_s[pl.ds(pl.multiple_of(base + 64 * j, 64), 64), :] = o.astype(bf16)
                return c3

            lax.fori_loop(0, HEADS // 4, heads, 0)
            r = jnp.dot(wr_s[...], o_s[...], preferred_element_type=f32)
            mean = jnp.sum(r, axis=0, keepdims=True) * (1.0 / D)
            rc = r - mean
            rvar = jnp.sum(rc * rc, axis=0, keepdims=True) * (1.0 / D)
            vv = jnp.dot(wm[...], rc.astype(bf16), preferred_element_type=f32)
            vel = (vv[0:MEL] + vv[MEL : 2 * MEL]) * lax.rsqrt(rvar + norm_eps)
            vel = jnp.where(own, vel, 0.0)
            x_s[...] = x_s[...] + vel * (1.0 / flow_steps)
            tot_s[...] = tot_s[...] + vel
            velb = vel.astype(bf16)
            stage[0:MEL, :] = velb[:, 0:128]
            stage[MEL : 2 * MEL, :] = velb[:, 128:256]
            return c2

        lax.fori_loop(0, EULER, step, 0)
        totb = tot_s[...].astype(bf16)
        tot_out[q, 0:MEL, :] = totb[:, 0:128]
        tot_out[q, MEL : 2 * MEL, :] = totb[:, 128:256]
        for k, out in enumerate((v0, v1, v2, v3)):
            quarter = (m + k) & 3
            out[q] = stage[pl.ds(pl.multiple_of(quarter * PIECE, 16), PIECE), :]
        return carry

    stage[...] = jnp.zeros(stage.shape, bf16)
    lax.fori_loop(0, n_jobs, job, 0)


def pack_kernel(ids, route, a0, a1, a2, a3, out):
    me = ids[0]
    m = ids[1]

    def scan(s, rank):
        dest = route[me * SLOT_DEV + s]
        live = dest >= 0
        worker = (jnp.maximum(dest, 0) * 10923) >> 16
        source = (m - rank) & 3
        for k, a in enumerate((a0, a1, a2, a3)):

            @pl.when(jnp.logical_and(live, source == k))
            def _():
                out[worker] = a[rank >> 2]

        return rank + live.astype(jnp.int32)

    lax.fori_loop(0, SLOT_DEV, scan, jnp.int32(0))


def select_kernel(owners, got, out):
    for j in range(WORK_DEV):
        out[j] = got[owners[j]]


def span_kernel(ids, route, t0, t1, t2, t3, out):
    me = ids[0]
    m = ids[1]
    out[...] = jnp.zeros(out.shape, f32)

    def scan(s, rank):
        live = route[me * SLOT_DEV + s] >= 0
        source = (m - rank) & 3
        u = s >> 2
        off = (s & 3) * BLOCK
        for k, t in enumerate((t0, t1, t2, t3)):

            @pl.when(jnp.logical_and(live, source == k))
            def _():
                block = t[rank >> 2].astype(f32)
                out[u, :, pl.ds(pl.multiple_of(off, 128), 128)] = block[0:MEL]
                out[u, :, pl.ds(pl.multiple_of(off + 128, 128), 128)] = block[MEL : 2 * MEL]

        return rank + live.astype(jnp.int32)

    lax.fori_loop(0, SLOT_DEV, scan, jnp.int32(0))


def final_kernel(ids, b0, b1, b2, b3, out, stage):
    m = ids[1]
    for k, b in enumerate((b0, b1, b2, b3)):
        quarter = (m - k) & 3
        at = pl.multiple_of(quarter * PIECE, 16)
        for j in range(WORK_DEV):
            stage[j, pl.ds(at, PIECE), :] = b[j]
    for j in range(WORK_DEV):
        out[j, :, 0:128] = stage[j, 0:MEL, :].astype(f32)
        out[j, :, 128:256] = stage[j, MEL : 2 * MEL, :].astype(f32)


def call(kernel, outs, kinds, args, scratch=(), out_kinds=None):
    spec = lambda kind: pl.BlockSpec(memory_space=SMEM if kind == "s" else VMEM)
    return pl.pallas_call(
        kernel,
        out_shape=outs,
        in_specs=[spec(k) for k in kinds],
        out_specs=jax.tree.map(lambda _: pl.BlockSpec(memory_space=VMEM), outs),
        scratch_shapes=list(scratch),
        compiler_params=pltpu.CompilerParams(vmem_limit_bytes=LIMIT),
    )(*args)


def shape(dims, dtype):
    return jax.ShapeDtypeStruct(dims, dtype)


def to_next(value, k):
    return lax.ppermute(value, "mp", [(i, (i + k) % N_MP) for i in range(N_MP)])


def gathered(value):
    return [value] + [to_next(value, k) for k in range(1, N_MP)]


def shards(
    mel_audio, start_noise, span_start, span_length, block_route,
    w_input, attn_gain, w_qkv, w_out, final_gain, w_mel,
):
    e_rows = jnp.asarray(time_rows())
    gain = attn_gain.reshape(1, D)
    w3 = jnp.transpose(w_qkv, (1, 0, 2))
    folded = call(fold_kernel, shape((3, ROWS, 256), bf16), "vvvv", (w_input, e_rows, gain, w3))
    wp = gathered(folded)
    wa_t, wo_t, wm = call(
        prep_kernel,
        (shape((D, ROWS), bf16), shape((D, 256), bf16), shape((2 * MEL, D), bf16)),
        "vvvvv",
        (w_input, e_rows, w_out, w_mel, final_gain.reshape(1, D)),
    )
    wo = gathered(wo_t)
    ids = jnp.stack([lax.axis_index("dp"), lax.axis_index("mp")]).astype(jnp.int32)
    slot_ids = ids[0] * WORK_DEV + jnp.arange(WORK_DEV, dtype=jnp.int32)
    matches = block_route[None, :] == slot_ids[:, None]
    every = jnp.arange(block_route.shape[0], dtype=jnp.int32)
    owners = jnp.sum(jnp.where(matches, every[None, :], 0), axis=1) // SLOT_DEV

    tot, v0, v1, v2, v3 = call(
        main_kernel,
        (shape((JOBS, 2 * MEL, 128), bf16),) + (shape((JOBS, PIECE, 128), bf16),) * 4,
        "ssss" + "v" * 12,
        (ids, block_route, span_start, span_length, mel_audio, start_noise, wa_t, wm, *wp, *wo),
        scratch=[
            SMEM((JOBS,), jnp.int32),
            VMEM((D, ROWS), bf16),
            VMEM((D, ROWS), bf16),
            VMEM((ROWS, D), bf16),
            VMEM((D, D + ROWS), bf16),
            VMEM((ROWS, WIN), bf16),
            VMEM((ROWS, WIN), bf16),
            VMEM((WIN, ROWS), bf16),
            VMEM((D, BLOCK), bf16),
            VMEM((HEADS // 2, WIN, 128), bf16),
            VMEM((D, WIN), bf16),
            VMEM((D + ROWS, BLOCK), bf16),
            VMEM((MEL, BLOCK), f32),
            VMEM((MEL, BLOCK), f32),
            VMEM((4 * PIECE, 128), bf16),
        ],
    )
    pieces = [v0] + [to_next(v, k) for k, v in ((1, v1), (2, v2), (3, v3))]
    totals = gathered(tot)
    packed = call(
        pack_kernel, shape((32, PIECE, 128), bf16), "ssvvvv", (ids, block_route, *pieces)
    )
    got = lax.all_to_all(packed, "dp", 0, 0, tiled=True)
    chosen = call(select_kernel, shape((WORK_DEV, PIECE, 128), bf16), "sv", (owners, got))
    parts = gathered(chosen)
    infilled = call(
        span_kernel, shape((UTT_DEV, MEL, SPAN_MAX), f32), "ssvvvv", (ids, block_route, *totals)
    )
    velocity = call(
        final_kernel,
        shape((WORK_DEV, MEL, BLOCK), f32),
        "svvvv",
        (ids, *parts),
        scratch=[VMEM((WORK_DEV, 4 * PIECE, 128), bf16)],
    )
    return (infilled, velocity)


def solution(mesh):
    return jax.shard_map(
        shards,
        mesh=mesh,
        in_specs=(
            P("dp", None, None),
            P("dp", None, None),
            P(),
            P(),
            P(),
            P(),
            P(),
            P(None, None, "mp"),
            P("mp", None),
            P(),
            P(),
        ),
        out_specs=(P("dp", None, None), P("dp", None, None)),
        check_vma=False,
    )
```

profile of v0, /device:TPU:1, one launch (start us, length us, event | category | flops | bytes accessed | tf_op | source)
XLA Modules:
  0.0 169.0 jit_solution(13889397728598133350)
XLA Ops:
  0.6 2.8 %shard_map.132.wp0 = bf16[3,176,256]{2,1,0:T(8,128)(2,1)} custom-call(bf16[160,1024]{1,0:T(8,128)(2,1)} %w_in.3, f32[16,1024]{1,0:T(8,128)} %constant.30.clone.e_rows, f32[1,1024]{1,0:T(1,128)} %bitcast.6, bf16[3,1024,256]{2,1,0:T(8,128)(2,1)} %bitcast.5), custom_call_target="tpu_custom_call" | custom-call | tf_op jit(solution)/shard_map/pallas_call | solution.py:282
  3.5 4.6 %collective-permute-start.2 = (bf16[3,176,256]{2,1,0:T(8,128)(2,1)}, bf16[3,176,256]{2,1,0:T(8,128)(2,1)S(1)}, u32[]{:S(2)}, u32[]{:S(2)}) collective-permute-start(bf16[3,176,256]{2,1,0:T(8,128)(2,1)} %shard_map.132.wp0), channel_id=1, source_target_pairs={{0,3},{1,0},{2,1},{3,2},{4,7},{5,4},{6,5},{7,6},{8,11},{9,8},{10,9... | collective-permute-start | bytes 811016 | tf_op jit(solution)/shard_map/ppermute | solution.py:297
  8.1 2.7 %shard_map.131 = (bf16[1024,176]{1,0:T(8,128)(2,1)}, bf16[1024,256]{1,0:T(8,128)(2,1)}, bf16[160,1024]{1,0:T(8,128)(2,1)}) custom-call(bf16[160,1024]{1,0:T(8,128)(2,1)} %w_in.3, f32[16,1024]{1,0:T(8,128)} %constant.30.clone.e_rows, bf16[256,1024]{1,0:T(8,128)(2,1)} %w_out.1, bf16[80,1024]{1,0:T(8,128)(2,1)} %w_mel.1, f32[1,1024]{1,0:T(1,128)} %bitcast.7), custom_call_target="tpu_custom_call" | custom-call | tf_op jit(solution)/shard_map/pallas_call | solution.py:282
  10.8 1.3 collective-permute-start.3
  12.2 3.6 %collective-permute-start.1 = (bf16[3,176,256]{2,1,0:T(8,128)(2,1)}, bf16[3,176,256]{2,1,0:T(8,128)(2,1)S(1)}, u32[]{:S(2)}, u32[]{:S(2)}) collective-permute-start(bf16[3,176,256]{2,1,0:T(8,128)(2,1)} %shard_map.132.wp0), channel_id=1, source_target_pairs={{0,2},{1,3},{2,0},{3,1},{4,6},{5,7},{6,4},{7,5},{8,10},{9,11},{10,... | collective-permute-start | bytes 811016 | tf_op jit(solution)/shard_map/ppermute | solution.py:297
  15.8 0.7 pad_add_fusion.ids
  16.4 25.4 %collective-permute-done.1.wp2 = bf16[3,176,256]{2,1,0:T(8,128)(2,1)S(1)} collective-permute-done((bf16[3,176,256]{2,1,0:T(8,128)(2,1)}, bf16[3,176,256]{2,1,0:T(8,128)(2,1)S(1)}, u32[]{:S(2)}, u32[]{:S(2)}) %collective-permute-start.1) | collective-permute-done | bytes 270368 | tf_op jit(solution)/shard_map/ppermute | solution.py:297
  41.8 7.4 %collective-permute-done.wp1 = bf16[3,176,256]{2,1,0:T(8,128)(2,1)S(1)} collective-permute-done((bf16[3,176,256]{2,1,0:T(8,128)(2,1)}, bf16[3,176,256]{2,1,0:T(8,128)(2,1)S(1)}, u32[]{:S(2)}, u32[]{:S(2)}) %collective-permute-start) | collective-permute-done | bytes 270368 | tf_op jit(solution)/shard_map/ppermute | solution.py:297
  49.3 0.6 copy-done.6
  49.9 0.2 copy-done.1
  50.3 0.2 copy-done.3
  50.5 62.3 %shard_map.133 = (bf16[4,160,128]{2,1,0:T(8,128)(2,1)}, bf16[4,48,128]{2,1,0:T(8,128)(2,1)}, bf16[4,48,128]{2,1,0:T(8,128)(2,1)}, bf16[4,48,128]{2,1,0:T(8,128)(2,1)}, bf16[4,48,128]{2,1,0:T(8,128)(2,1)}) custom-call(s32[2]{0:T(128)} %pad_add_fusion.ids, s32[512]{0:T(512)} %route.5, s32[128]{0:T(128)} %starts.1, s32[128]{0:T(128)} %lengths.1, ...), custom_call_target="tpu_custom_call" | custom-call | tf_op jit(solution)/shard_map/pallas_call | solution.py:282
  113.0 2.6 %collective-permute-start.11 = (bf16[4,48,128]{2,1,0:T(8,128)(2,1)}, bf16[4,48,128]{2,1,0:T(8,128)(2,1)S(1)}, u32[]{:S(2)}, u32[]{:S(2)}) collective-permute-start(bf16[4,48,128]{2,1,0:T(8,128)(2,1)} %get-tuple-element.17), channel_id=1, source_target_pairs={{0,3},{1,0},{2,1},{3,2},{4,7},{5,4},{6,5},{7,6},{8,11},{9,8},{10,9... | collective-permute-start | bytes 147464 | tf_op jit(solution)/shard_map/ppermute | solution.py:297
  115.6 2.2 %collective-permute-done.9.a1 = bf16[4,48,128]{2,1,0:T(8,128)(2,1)S(1)} collective-permute-done((bf16[4,48,128]{2,1,0:T(8,128)(2,1)}, bf16[4,48,128]{2,1,0:T(8,128)(2,1)S(1)}, u32[]{:S(2)}, u32[]{:S(2)}) %collective-permute-start.9) | collective-permute-done | bytes 49184 | tf_op jit(solution)/shard_map/ppermute | solution.py:297
  117.8 0.6 collective-permute-done.11.a3
  118.4 0.6 copy-done.16
  119.0 2.2 %shard_map.135 = bf16[32,48,128]{2,1,0:T(8,128)(2,1)} custom-call(s32[2]{0:T(128)} %pad_add_fusion.ids, s32[512]{0:T(512)} %route.5, bf16[4,48,128]{2,1,0:T(8,128)(2,1)} %get-tuple-element.14.a0, bf16[4,48,128]{2,1,0:T(8,128)(2,1)} %copy-done.14, bf16[4,48,128]{2,1,0:T(8,128)(2,1)} %copy-done.15, bf16[4,48,128]{2,1,0:T(8,128)(2,1)} %copy-done.16), custom_call_target="tpu_custom_call" | custom-call | tf_op jit(solution)/shard_map/pallas_call | solution.py:282
  121.2 24.2 %all-to-all-start = ((bf16[32,48,128]{2,1,0:T(8,128)(2,1)}), bf16[32,48,128]{2,1,0:T(8,128)(2,1)S(1)}, u32[]{:S(2)}, u32[]{:S(2)}) async-start(bf16[32,48,128]{2,1,0:T(8,128)(2,1)} %shard_map.135), calls=%async_computation | async-start | bytes 786432 | tf_op jit(solution)/shard_map/all_to_all | solution.py:354
  145.6 2.2 %collective-permute-start.8 = (bf16[4,160,128]{2,1,0:T(8,128)(2,1)S(1)}, bf16[4,160,128]{2,1,0:T(8,128)(2,1)S(1)}, u32[]{:S(2)}, u32[]{:S(2)}) collective-permute-start(bf16[4,160,128]{2,1,0:T(8,128)(2,1)S(1)} %copy-done.7), channel_id=1, source_target_pairs={{0,3},{1,0},{2,1},{3,2},{4,7},{5,4},{6,5},{7,6},{8,11},{9,8},{10,9... | collective-permute-start | bytes 491528 | tf_op jit(solution)/shard_map/ppermute | solution.py:297
  147.8 0.9 collective-permute-start.7
  148.7 0.5 and_select_fusion.owners
  149.2 6.4 %all-to-all-done.got = bf16[32,48,128]{2,1,0:T(8,128)(2,1)S(1)} async-done(((bf16[32,48,128]{2,1,0:T(8,128)(2,1)}), bf16[32,48,128]{2,1,0:T(8,128)(2,1)S(1)}, u32[]{:S(2)}, u32[]{:S(2)}) %all-to-all-start) | async-done | bytes 393248 | tf_op jit(solution)/shard_map/all_to_all | solution.py:354
  155.5 0.7 copy-done
  156.3 1.6 shard_map.136.b0
  157.9 2.1 %collective-permute-start.14 = (bf16[6,48,128]{2,1,0:T(8,128)(2,1)}, bf16[6,48,128]{2,1,0:T(8,128)(2,1)S(1)}, u32[]{:S(2)}, u32[]{:S(2)}) collective-permute-start(bf16[6,48,128]{2,1,0:T(8,128)(2,1)} %shard_map.136.b0), channel_id=1, source_target_pairs={{0,3},{1,0},{2,1},{3,2},{4,7},{5,4},{6,5},{7,6},{8,11},{9,8},{10,9... | collective-permute-start | bytes 221192 | tf_op jit(solution)/shard_map/ppermute | solution.py:297
  160.0 0.9 collective-permute-start.13
  161.0 0.6 copy-done.8
  161.7 0.7 copy-done.10
  162.3 2.9 %shard_map.134 = f32[4,80,1024]{2,1,0:T(8,128)} custom-call(s32[2]{0:T(128)} %pad_add_fusion.ids, s32[512]{0:T(512)} %route.5, bf16[4,160,128]{2,1,0:T(8,128)(2,1)} %get-tuple-element.13.t0, bf16[4,160,128]{2,1,0:T(8,128)(2,1)} %copy-done.10, bf16[4,160,128]{2,1,0:T(8,128)(2,1)} %copy-done.9, bf16[4,160,128]{2,1,0:T(8,128)(2,1)} %copy-done.8), custom_call_target="tpu_custom_call" | custom-call | tf_op jit(solution)/shard_map/pallas_call | solution.py:282
  165.3 1.2 collective-permute-done.12.b1
  166.5 0.6 copy-done.13
  167.1 1.8 %shard_map.137 = f32[6,80,256]{2,1,0:T(8,128)} custom-call(s32[2]{0:T(128)} %pad_add_fusion.ids, bf16[6,48,128]{2,1,0:T(8,128)(2,1)} %shard_map.136.b0, bf16[6,48,128]{2,1,0:T(8,128)(2,1)} %copy-done.13, bf16[6,48,128]{2,1,0:T(8,128)(2,1)} %copy-done.12, bf16[6,48,128]{2,1,0:T(8,128)(2,1)} %copy-done.11), custom_call_target="tpu_custom_call" | custom-call | tf_op jit(solution)/shard_map/pallas_call | solution.py:282
  (47 shorter events, 0.8 us)
Async XLA Ops:
  3.5 12.3 %collective-permute-start.2 = (bf16[3,176,256]{2,1,0:T(8,128)(2,1)}, bf16[3,176,256]{2,1,0:T(8,128)(2,1)S(1)}, u32[]{:S(2)}, u32[]{:S(2)}) collective-permute-start(bf16[3,176,256]{2,1,0:T(8,128)(2,1)} %shard_map.132.wp0), channel_id=1, source_target_pairs={{0,3},{1,0},{2,1},{3,2},{4,7},{5,4},{6,5},{7,6},{8,11},{9,8},{10,9... | collective-permute-start | bytes 811016 | tf_op jit(solution)/shard_map/ppermute | solution.py:297
  10.7 38.5 %collective-permute-start.5 = (bf16[1024,256]{1,0:T(8,128)(2,1)}, bf16[1024,256]{1,0:T(8,128)(2,1)S(1)}, u32[]{:S(2)}, u32[]{:S(2)}) collective-permute-start(bf16[1024,256]{1,0:T(8,128)(2,1)} %get-tuple-element.12.wo0), channel_id=1, source_target_pairs={{0,3},{1,0},{2,1},{3,2},{4,7},{5,4},{6,5},{7,6},{8,11},{9,8},{10,9... | collective-permute-start | bytes 1572872 | tf_op jit(solution)/shard_map/ppermute | solution.py:297
  10.8 38.4 %collective-permute-start.4 = (bf16[1024,256]{1,0:T(8,128)(2,1)}, bf16[1024,256]{1,0:T(8,128)(2,1)S(1)}, u32[]{:S(2)}, u32[]{:S(2)}) collective-permute-start(bf16[1024,256]{1,0:T(8,128)(2,1)} %get-tuple-element.12.wo0), channel_id=1, source_target_pairs={{0,2},{1,3},{2,0},{3,1},{4,6},{5,7},{6,4},{7,5},{8,10},{9,11},{10,... | collective-permute-start | bytes 1572872 | tf_op jit(solution)/shard_map/ppermute | solution.py:297
  10.8 38.4 %collective-permute-start.3 = (bf16[1024,256]{1,0:T(8,128)(2,1)}, bf16[1024,256]{1,0:T(8,128)(2,1)S(1)}, u32[]{:S(2)}, u32[]{:S(2)}) collective-permute-start(bf16[1024,256]{1,0:T(8,128)(2,1)} %get-tuple-element.12.wo0), channel_id=1, source_target_pairs={{0,1},{1,2},{2,3},{3,0},{4,5},{5,6},{6,7},{7,4},{8,9},{9,10},{10,1... | collective-permute-start | bytes 1572872 | tf_op jit(solution)/shard_map/ppermute | solution.py:297
  12.2 29.7 %collective-permute-start.1 = (bf16[3,176,256]{2,1,0:T(8,128)(2,1)}, bf16[3,176,256]{2,1,0:T(8,128)(2,1)S(1)}, u32[]{:S(2)}, u32[]{:S(2)}) collective-permute-start(bf16[3,176,256]{2,1,0:T(8,128)(2,1)} %shard_map.132.wp0), channel_id=1, source_target_pairs={{0,2},{1,3},{2,0},{3,1},{4,6},{5,7},{6,4},{7,5},{8,10},{9,11},{10,... | collective-permute-start | bytes 811016 | tf_op jit(solution)/shard_map/ppermute | solution.py:297
  15.8 33.5 %copy-start.4 = (bf16[3,176,256]{2,1,0:T(8,128)(2,1)}, bf16[3,176,256]{2,1,0:T(8,128)(2,1)S(1)}, u32[]{:S(2)}) copy-start(bf16[3,176,256]{2,1,0:T(8,128)(2,1)S(1)} %collective-permute-done.2.wp3) | copy-start | bytes 811012
  15.8 33.5 %collective-permute-start = (bf16[3,176,256]{2,1,0:T(8,128)(2,1)}, bf16[3,176,256]{2,1,0:T(8,128)(2,1)S(1)}, u32[]{:S(2)}, u32[]{:S(2)}) collective-permute-start(bf16[3,176,256]{2,1,0:T(8,128)(2,1)} %shard_map.132.wp0), channel_id=1, source_target_pairs={{0,1},{1,2},{2,3},{3,0},{4,5},{5,6},{6,7},{7,4},{8,9},{9,10},{10,1... | collective-permute-start | bytes 811016 | tf_op jit(solution)/shard_map/ppermute | solution.py:297
  41.8 7.4 %copy-start.5 = (bf16[3,176,256]{2,1,0:T(8,128)(2,1)}, bf16[3,176,256]{2,1,0:T(8,128)(2,1)S(1)}, u32[]{:S(2)}) copy-start(bf16[3,176,256]{2,1,0:T(8,128)(2,1)S(1)} %collective-permute-done.1.wp2) | copy-start | bytes 811012
  49.2 0.7 copy-start.6
  49.2 0.9 copy-start.1
  49.2 1.1 copy-start.2
  49.3 1.2 copy-start.3
  112.8 32.6 %copy-start.17 = (s32[512]{0:T(512)S(1)}, s32[512]{0:T(512)}, u32[]{:S(2)}) copy-start(s32[512]{0:T(512)} %route.5) | copy-start | bytes 6148
  112.8 32.8 %copy-start.7 = (bf16[4,160,128]{2,1,0:T(8,128)(2,1)S(1)}, bf16[4,160,128]{2,1,0:T(8,128)(2,1)}, u32[]{:S(2)}) copy-start(bf16[4,160,128]{2,1,0:T(8,128)(2,1)} %get-tuple-element.13.t0) | copy-start | bytes 491524
  112.8 5.0 %collective-permute-start.9 = (bf16[4,48,128]{2,1,0:T(8,128)(2,1)}, bf16[4,48,128]{2,1,0:T(8,128)(2,1)S(1)}, u32[]{:S(2)}, u32[]{:S(2)}) collective-permute-start(bf16[4,48,128]{2,1,0:T(8,128)(2,1)} %get-tuple-element.15), channel_id=1, source_target_pairs={{0,1},{1,2},{2,3},{3,0},{4,5},{5,6},{6,7},{7,4},{8,9},{9,10},{10,1... | collective-permute-start | bytes 147464 | tf_op jit(solution)/shard_map/ppermute | solution.py:297
  112.9 4.9 %collective-permute-start.10 = (bf16[4,48,128]{2,1,0:T(8,128)(2,1)}, bf16[4,48,128]{2,1,0:T(8,128)(2,1)S(1)}, u32[]{:S(2)}, u32[]{:S(2)}) collective-permute-start(bf16[4,48,128]{2,1,0:T(8,128)(2,1)} %get-tuple-element.16), channel_id=1, source_target_pairs={{0,2},{1,3},{2,0},{3,1},{4,6},{5,7},{6,4},{7,5},{8,10},{9,11},{10,... | collective-permute-start | bytes 147464 | tf_op jit(solution)/shard_map/ppermute | solution.py:297
  113.0 5.4 %collective-permute-start.11 = (bf16[4,48,128]{2,1,0:T(8,128)(2,1)}, bf16[4,48,128]{2,1,0:T(8,128)(2,1)S(1)}, u32[]{:S(2)}, u32[]{:S(2)}) collective-permute-start(bf16[4,48,128]{2,1,0:T(8,128)(2,1)} %get-tuple-element.17), channel_id=1, source_target_pairs={{0,3},{1,0},{2,1},{3,2},{4,7},{5,4},{6,5},{7,6},{8,11},{9,8},{10,9... | collective-permute-start | bytes 147464 | tf_op jit(solution)/shard_map/ppermute | solution.py:297
  117.8 0.6 copy-start.15
  121.2 34.4 %all-to-all-start = ((bf16[32,48,128]{2,1,0:T(8,128)(2,1)}), bf16[32,48,128]{2,1,0:T(8,128)(2,1)S(1)}, u32[]{:S(2)}, u32[]{:S(2)}) async-start(bf16[32,48,128]{2,1,0:T(8,128)(2,1)} %shard_map.135), calls=%async_computation | async-start | bytes 786432 | tf_op jit(solution)/shard_map/all_to_all | solution.py:354
  145.6 15.4 %collective-permute-start.8 = (bf16[4,160,128]{2,1,0:T(8,128)(2,1)S(1)}, bf16[4,160,128]{2,1,0:T(8,128)(2,1)S(1)}, u32[]{:S(2)}, u32[]{:S(2)}) collective-permute-start(bf16[4,160,128]{2,1,0:T(8,128)(2,1)S(1)} %copy-done.7), channel_id=1, source_target_pairs={{0,3},{1,0},{2,1},{3,2},{4,7},{5,4},{6,5},{7,6},{8,11},{9,8},{10,9... | collective-permute-start | bytes 491528 | tf_op jit(solution)/shard_map/ppermute | solution.py:297
  147.8 13.2 %collective-permute-start.7 = (bf16[4,160,128]{2,1,0:T(8,128)(2,1)S(1)}, bf16[4,160,128]{2,1,0:T(8,128)(2,1)S(1)}, u32[]{:S(2)}, u32[]{:S(2)}) collective-permute-start(bf16[4,160,128]{2,1,0:T(8,128)(2,1)S(1)} %copy-done.7), channel_id=1, source_target_pairs={{0,2},{1,3},{2,0},{3,1},{4,6},{5,7},{6,4},{7,5},{8,10},{9,11},{10,... | collective-permute-start | bytes 491528 | tf_op jit(solution)/shard_map/ppermute | solution.py:297
  148.7 12.3 %collective-permute-start.6 = (bf16[4,160,128]{2,1,0:T(8,128)(2,1)S(1)}, bf16[4,160,128]{2,1,0:T(8,128)(2,1)S(1)}, u32[]{:S(2)}, u32[]{:S(2)}) collective-permute-start(bf16[4,160,128]{2,1,0:T(8,128)(2,1)S(1)} %copy-done.7), channel_id=1, source_target_pairs={{0,1},{1,2},{2,3},{3,0},{4,5},{5,6},{6,7},{7,4},{8,9},{9,10},{10,1... | collective-permute-start | bytes 491528 | tf_op jit(solution)/shard_map/ppermute | solution.py:297
  155.5 0.7 copy-start
  157.9 7.3 %collective-permute-start.14 = (bf16[6,48,128]{2,1,0:T(8,128)(2,1)}, bf16[6,48,128]{2,1,0:T(8,128)(2,1)S(1)}, u32[]{:S(2)}, u32[]{:S(2)}) collective-permute-start(bf16[6,48,128]{2,1,0:T(8,128)(2,1)} %shard_map.136.b0), channel_id=1, source_target_pairs={{0,3},{1,0},{2,1},{3,2},{4,7},{5,4},{6,5},{7,6},{8,11},{9,8},{10,9... | collective-permute-start | bytes 221192 | tf_op jit(solution)/shard_map/ppermute | solution.py:297
  160.0 5.2 %collective-permute-start.13 = (bf16[6,48,128]{2,1,0:T(8,128)(2,1)}, bf16[6,48,128]{2,1,0:T(8,128)(2,1)S(1)}, u32[]{:S(2)}, u32[]{:S(2)}) collective-permute-start(bf16[6,48,128]{2,1,0:T(8,128)(2,1)} %shard_map.136.b0), channel_id=1, source_target_pairs={{0,2},{1,3},{2,0},{3,1},{4,6},{5,7},{6,4},{7,5},{8,10},{9,11},{10,... | collective-permute-start | bytes 221192 | tf_op jit(solution)/shard_map/ppermute | solution.py:297
  160.9 0.7 copy-start.8
  160.9 5.5 %collective-permute-start.12 = (bf16[6,48,128]{2,1,0:T(8,128)(2,1)}, bf16[6,48,128]{2,1,0:T(8,128)(2,1)S(1)}, u32[]{:S(2)}, u32[]{:S(2)}) collective-permute-start(bf16[6,48,128]{2,1,0:T(8,128)(2,1)} %shard_map.136.b0), channel_id=1, source_target_pairs={{0,1},{1,2},{2,3},{3,0},{4,5},{5,6},{6,7},{7,4},{8,9},{9,10},{10,1... | collective-permute-start | bytes 221192 | tf_op jit(solution)/shard_map/ppermute | solution.py:297
  161.0 0.7 copy-start.9
  161.7 0.7 copy-start.10
  165.2 1.2 copy-start.11
  165.3 1.2 copy-start.12
  166.5 0.6 copy-start.13
  (2 other events, 1.2 us)
where the time goes:
time: 169 us
  Pallas kernels  76.3 us (45%)
  waiting for transfers between devices  43.2 us (26%)
  starting transfers between devices  42.7 us (25%)
  local copies, waits for them, and re-layouts  4.61 us (3%)
    pallas_call x7, Pallas kernels, call(): pl.pallas_call(kernel, out_shape=outs, in_specs=[spec(k) for k in kinds],...  76.3 us
    ppermute x15, waiting for transfers between devices, to_next(): return lax.ppermute(value, 'mp', [(i, (i + k) % N_MP) for i in range(N_MP)])  36.8 us
    all_to_all x1, starting transfers between devices, shards(): got = lax.all_to_all(packed, 'dp', 0, 0, tiled=True)  24.2 us
    ppermute x15, starting transfers between devices, to_next(): return lax.ppermute(value, 'mp', [(i, (i + k) % N_MP) for i in range(N_MP)])  18.4 us
    all_to_all x1, waiting for transfers between devices, shards(): got = lax.all_to_all(packed, 'dp', 0, 0, tiled=True)  6.36 us
    unnamed x36, local copies, waits for them, and re-layouts  4.61 us
  transfers between devices with their start and end apart: 16, of which 6 were waited for; matrix products, arithmetic and copies ran while one was open for 1% of the time, Pallas kernels for 4%

commit v1 on v0

v1 whole, which is shorter than its diff:
```python
import math

import jax
import jax.numpy as jnp
import numpy as np
from jax import lax
from jax.experimental import pallas as pl
from jax.experimental.pallas import tpu as pltpu
from jax.sharding import PartitionSpec as P

D = 1024
MEL = 80
HEAD_DIM = 64
HEADS = 16
BLOCK = 256
CTX = 128
BLK_UTT = 4
UTT_DEV = 4
WORK_DEV = 6
EULER = 2
FRAMES = 2048
WIN = 512
SPAN_MAX = 1024
SLOT_DEV = 16
N_MP = 4
JOBS = 4
ROWS = 176
PIECE = 48
flow_steps = 32.0
norm_eps = 1e-05
f32 = jnp.float32
bf16 = jnp.bfloat16
VMEM = pltpu.VMEM
SMEM = pltpu.SMEM
LIMIT = 56 * 1024 * 1024


def time_rows():
    half = D // 2
    freqs = np.exp(-math.log(10000.0) * np.arange(half, dtype=np.float32) / half)
    rows = np.zeros((16, D), np.float32)
    for step in range(EULER):
        angles = np.float32(1000.0 * step / flow_steps) * freqs.astype(np.float32)
        e = np.concatenate([np.sin(angles), np.cos(angles)])
        e = e - e.mean()
        rows[2 * step] = e
        rows[2 * step + 1] = e
    return rows


def high_low(rows):
    high = rows.astype(bf16).astype(f32)
    odd = lax.broadcasted_iota(jnp.int32, rows.shape, 0) % 2 == 1
    return jnp.where(odd, rows - high, high)


def fold_kernel(ids, w_in, e_rows, gain, w_qkv, out, half):
    w = w_in[...].astype(f32)
    wc = w - jnp.mean(w, axis=1, keepdims=True)
    g = gain[...]
    wag = jnp.concatenate([wc * g, high_low(e_rows[...] * g)], axis=0).astype(bf16)
    for c in range(3):
        res = jnp.dot(wag, w_qkv[c], preferred_element_type=f32)
        if c == 0:
            res = res * (math.log2(math.e) / math.sqrt(HEAD_DIM))
        e_res = res[160:176]
        row = lax.broadcasted_iota(jnp.int32, e_res.shape, 0)
        first = e_res[0:1] + e_res[1:2]
        second = e_res[2:3] + e_res[3:4]
        both = jnp.where(row < 2, first, jnp.where(row < 4, second, 0.0))
        out[c, 0:160, :] = res[0:160].astype(bf16)
        out[c, 160:176, :] = high_low(both).astype(bf16)
        half[c] = jnp.where((ids[0] & 1) == 0, out[c, :, 0:128], out[c, :, 128:256])


def prep_kernel(ids, w_in, e_rows, w_out, w_mel, gain, wa_t, gram, wo_t, half, wm):
    w = w_in[...].astype(f32)
    wc = w - jnp.mean(w, axis=1, keepdims=True)
    wa = jnp.concatenate([wc, high_low(e_rows[...]), jnp.zeros((80, D), f32)], axis=0)
    wa_t[...] = wa.T[:, :ROWS].astype(bf16)
    wab = wa.astype(bf16)
    g = lax.dot_general(wab, wab, (((1,), (1,)), ((), ())), preferred_element_type=f32)
    g = g[0:ROWS, 0:ROWS] * (1.0 / D)
    high = g.astype(bf16)
    gram[0:ROWS, :] = high
    gram[ROWS : 2 * ROWS, :] = (g - high.astype(f32)).astype(bf16)
    o = w_out[...].astype(f32)
    o = o - jnp.mean(o, axis=1, keepdims=True)
    wo_t[...] = o.T.astype(bf16)
    half[...] = jnp.where((ids[0] & 1) == 0, wo_t[:, 0:128], wo_t[:, 128:256])
    wm[...] = (w_mel[...].astype(f32) * gain[...]).astype(bf16)


def find_jobs(ids, route, job_smem):
    base = (ids[0] >> 1) * (2 * SLOT_DEV)
    seat = (ids[0] & 1) * N_MP + ids[1]

    def scan(s, rank):
        live = route[base + s] >= 0

        @pl.when(jnp.logical_and(live, (rank & 7) == seat))
        def _():
            job_smem[rank >> 3] = s

        return rank + live.astype(jnp.int32)

    n_live = lax.fori_loop(0, 2 * SLOT_DEV, scan, jnp.int32(0))
    return (n_live - seat + 7) >> 3


def place(ids, starts, lengths, s):
    u = (s >> 2) & 3
    order = s & 3
    utter = (ids[0] >> 1) * (2 * UTT_DEV) + (s >> 2)
    span = starts[utter]
    length = lengths[utter]
    return u, order, span, length


def own_mask(order, length):
    count = length - BLOCK * order
    return lax.broadcasted_iota(jnp.int32, (1, BLOCK), 1) < count


def load_context(ids, s, u, order, span, length, mel_a, mel_b, chunk_s):
    first = span + BLOCK * order - CTX
    aligned = pl.multiple_of(jnp.clip((first >> 7) << 7, 0, FRAMES - 640), 128)
    here = (s >> 4) == (ids[0] & 1)

    @pl.when(here)
    def _():
        chunk_s[...] = mel_a[u, :, pl.ds(aligned, 640)]

    @pl.when(jnp.logical_not(here))
    def _():
        chunk_s[...] = mel_b[u, :, pl.ds(aligned, 640)]

    shift = aligned - first
    shift = jnp.where(shift < 0, shift + 640, shift)
    chunk = pltpu.roll(chunk_s[...].astype(f32), shift, 1)[:, :WIN]
    pos = first + lax.broadcasted_iota(jnp.int32, (1, WIN), 1)
    valid = jnp.logical_and(pos >= 0, pos < FRAMES)
    in_span = jnp.logical_and(pos >= span, pos < span + length)
    keep = jnp.logical_and(valid, jnp.logical_not(in_span))
    return jnp.where(keep, chunk, 0.0), valid.astype(f32)


def load_noise(ids, s, u, order, own, noise_a, noise_b, x_s):
    off = pl.multiple_of(order * BLOCK, BLOCK)
    here = (s >> 4) == (ids[0] & 1)

    @pl.when(here)
    def _():
        x_s[...] = jnp.where(own, noise_a[u, :, pl.ds(off, BLOCK)].astype(f32), 0.0)

    @pl.when(jnp.logical_not(here))
    def _():
        x_s[...] = jnp.where(own, noise_b[u, :, pl.ds(off, BLOCK)].astype(f32), 0.0)


def attend(n, context, valid, x, weights, work, o_out):
    gram, wq_s, wv_s, wk_s = weights
    k_s, q_s, v_s = work
    xr = x.astype(bf16).astype(f32)
    side = jnp.zeros((MEL, CTX), f32)
    state = jnp.concatenate([side, xr, side], axis=1)
    flags = (lax.broadcasted_iota(jnp.int32, (16, WIN), 0) >> 1) == n
    win = jnp.concatenate([context, state, flags.astype(f32)], axis=0)
    win = jnp.where(valid > 0.0, win, win[:, CTX : CTX + 1])
    win_b = win.astype(bf16)
    o_out[1024 : 1024 + ROWS, :] = win_b[:, CTX : CTX + BLOCK]
    gw = jnp.dot(gram[...], win_b, preferred_element_type=f32)
    var = jnp.sum(win * (gw[0:ROWS] + gw[ROWS : 2 * ROWS]), axis=0, keepdims=True)
    rstd = lax.rsqrt(jnp.maximum(var, 0.0) + norm_eps)
    scaled = win * rstd
    scaled_b = scaled.astype(bf16)
    v_win = (scaled * valid).astype(bf16)
    padded = jnp.concatenate([scaled, jnp.zeros((256 - ROWS, WIN), f32)], axis=0)
    win_t = padded.T.astype(bf16)[:, :ROWS]
    q_s[...] = jnp.dot(
        wq_s[...], scaled_b[:, CTX : CTX + BLOCK], preferred_element_type=f32
    ).astype(bf16)
    keys = jnp.dot(win_t, wk_s[...], preferred_element_type=f32).astype(bf16)
    for p in range(4):
        k_s[p] = keys[:, 256 * p : 256 * p + 256]
    v_s[...] = jnp.dot(wv_s[...], v_win, preferred_element_type=f32).astype(bf16)
    ones_rows = jnp.broadcast_to(valid, (16, WIN)).astype(bf16)
    zero = jnp.zeros((HEAD_DIM, BLOCK), bf16)

    def heads(half, carry):
        for quad in range(2):
            g = half * 2 + quad
            base = pl.multiple_of(g * 256, 256)
            qq = q_s[pl.ds(base, 256), :]
            columns = []
            for j in range(4):
                rows = [qq[64 * j : 64 * j + 64] if t == j else zero for t in range(4)]
                columns.append(jnp.concatenate(rows, axis=0))
            sc = jnp.dot(k_s[g], jnp.concatenate(columns, axis=1), preferred_element_type=f32)
            top = jnp.max(sc, axis=0, keepdims=True)
            pr = jnp.exp2(sc - top).astype(bf16)
            for j in range(4):
                at = pl.multiple_of(base + 64 * j, 64)
                lhs = jnp.concatenate([v_s[pl.ds(at, 64), :], ones_rows], axis=0)
                ov = jnp.dot(lhs, pr[:, 256 * j : 256 * j + 256], preferred_element_type=f32)
                o_out[pl.ds(at, 64), :] = (ov[0:64] / ov[64:65]).astype(bf16)
        return carry

    lax.fori_loop(0, 2, heads, 0)


def velocity_of(wr_s, o, own):
    r = jnp.dot(wr_s[...], o[...], preferred_element_type=f32)
    body = r[0:D]
    var = jnp.sum(body * body, axis=0, keepdims=True) * (1.0 / D)
    return jnp.where(own, r[D : D + MEL] * lax.rsqrt(var + norm_eps), 0.0)


def first_kernel(
    ids, route, starts, lengths, mel_a, mel_b, noise_a, noise_b, gram,
    wp0, hp1, sp1, hp2, sp2, hp3, sp3,
    wq_s, wv_s, wk_s, o_out,
    job_smem, k_s, q_s, v_s, x_s, chunk_s, o_s,
):
    n_jobs = find_jobs(ids, route, job_smem)
    at = 0
    for wp in (wp0, hp1, sp1, hp2, sp2, hp3, sp3):
        width = wp.shape[2]
        lanes = slice(at, at + width)
        pad = jnp.zeros((256 - ROWS, width), f32)
        wq_s[lanes, :] = jnp.concatenate([wp[0].astype(f32), pad], axis=0).T.astype(bf16)[:, :ROWS]
        wv_s[lanes, :] = jnp.concatenate([wp[2].astype(f32), pad], axis=0).T.astype(bf16)[:, :ROWS]
        wk_s[:, lanes] = wp[1]
        at += width

    def job(q, carry):
        s = job_smem[q]
        u, order, span, length = place(ids, starts, lengths, s)
        own = own_mask(order, length)
        context, valid = load_context(ids, s, u, order, span, length, mel_a, mel_b, chunk_s)
        load_noise(ids, s, u, order, own, noise_a, noise_b, x_s)
        attend(0, context, valid, x_s[...], (gram, wq_s, wv_s, wk_s), (k_s, q_s, v_s), o_s)
        o_out[q] = o_s[...]
        return carry

    lax.fori_loop(0, n_jobs, job, 0)


def second_kernel(
    ids, route, starts, lengths, mel_a, mel_b, noise_a, noise_b, gram,
    wq_s, wv_s, wk_s, o_in, wa_t, wm,
    wo0, ho1, so1, ho2, so2, ho3, so3,
    tot_out, v0, v1, v2, v3,
    job_smem, k_s, q_s, v_s, x_s, chunk_s, o_s, wr_s, stage,
):
    m = ids[1]
    n_jobs = find_jobs(ids, route, job_smem)
    at = 0
    for wo in (wo0, ho1, so1, ho2, so2, ho3, so3):
        width = wo.shape[1]
        wr_s[0:D, at : at + width] = wo[...]
        at += width
    wr_s[0:D, 1024 : 1024 + ROWS] = wa_t[...]
    wr_s[D : D + MEL, :] = jnp.dot(wm[...], wr_s[0:D, :], preferred_element_type=f32).astype(bf16)
    stage[...] = jnp.zeros(stage.shape, bf16)

    def job(q, carry):
        s = job_smem[q]
        u, order, span, length = place(ids, starts, lengths, s)
        own = own_mask(order, length)
        context, valid = load_context(ids, s, u, order, span, length, mel_a, mel_b, chunk_s)
        load_noise(ids, s, u, order, own, noise_a, noise_b, x_s)
        first = velocity_of(wr_s, o_in.at[q], own)
        x = x_s[...] + first * (1.0 / flow_steps)
        attend(1, context, valid, x, (gram, wq_s, wv_s, wk_s), (k_s, q_s, v_s), o_s)
        last = velocity_of(wr_s, o_s, own)
        total = (first + last).astype(bf16)
        tot_out[q, 0:MEL, :] = total[:, 0:128]
        tot_out[q, MEL : 2 * MEL, :] = total[:, 128:256]
        vel = last.astype(bf16)
        stage[0:MEL, :] = vel[:, 0:128]
        stage[MEL : 2 * MEL, :] = vel[:, 128:256]
        for k, out in enumerate((v0, v1, v2, v3)):
            quarter = (m + k) & 3
            out[q] = stage[pl.ds(pl.multiple_of(quarter * PIECE, 16), PIECE), :]
        return carry

    lax.fori_loop(0, n_jobs, job, 0)


def each_own_block(ids, route, arrays, use):
    m = ids[1]
    core = ids[0] & 1
    base = (ids[0] >> 1) * (2 * SLOT_DEV)

    def scan(s, rank):
        dest = route[base + s]
        live = dest >= 0
        mine = jnp.logical_and(live, (s >> 4) == core)
        k = (m - rank) & 3
        away = ((rank >> 2) & 1) ^ core
        source = away * 4 + k
        for i, a in enumerate(arrays):

            @pl.when(jnp.logical_and(mine, source == i))
            def _():
                use(s & 15, dest, a, rank >> 3)

        return rank + live.astype(jnp.int32)

    lax.fori_loop(0, 2 * SLOT_DEV, scan, jnp.int32(0))


def pack_kernel(ids, route, a0, a1, a2, a3, b0, b1, b2, b3, out):
    def use(s, dest, a, q):
        out[(dest * 10923) >> 16] = a[q]

    each_own_block(ids, route, (a0, a1, a2, a3, b0, b1, b2, b3), use)


def select_kernel(owners, got, out):
    for j in range(WORK_DEV):
        out[j] = got[owners[j]]


def span_kernel(ids, route, a0, a1, a2, a3, b0, b1, b2, b3, out):
    out[...] = jnp.zeros(out.shape, f32)

    def use(s, dest, a, q):
        block = a[q].astype(f32)
        off = (s & 3) * BLOCK
        out[s >> 2, :, pl.ds(pl.multiple_of(off, 128), 128)] = block[0:MEL]
        out[s >> 2, :, pl.ds(pl.multiple_of(off + 128, 128), 128)] = block[MEL : 2 * MEL]

    each_own_block(ids, route, (a0, a1, a2, a3, b0, b1, b2, b3), use)


def final_kernel(ids, b0, b1, b2, b3, out, stage):
    m = ids[1]
    for k, b in enumerate((b0, b1, b2, b3)):
        quarter = (m - k) & 3
        at = pl.multiple_of(quarter * PIECE, 16)
        for j in range(WORK_DEV):
            stage[j, pl.ds(at, PIECE), :] = b[j]
    for j in range(WORK_DEV):
        out[j, :, 0:128] = stage[j, 0:MEL, :].astype(f32)
        out[j, :, 128:256] = stage[j, MEL : 2 * MEL, :].astype(f32)


def call(kernel, outs, kinds, args, scratch=(), out_kinds=None):
    spec = lambda kind: pl.BlockSpec(memory_space=SMEM if kind == "s" else VMEM)
    return pl.pallas_call(
        kernel,
        out_shape=outs,
        in_specs=[spec(k) for k in kinds],
        out_specs=jax.tree.map(lambda _: pl.BlockSpec(memory_space=VMEM), outs),
        scratch_shapes=list(scratch),
        compiler_params=pltpu.CompilerParams(vmem_limit_bytes=LIMIT),
    )(*args)


def shape(dims, dtype):
    return jax.ShapeDtypeStruct(dims, dtype)


def to_next(value, k):
    return lax.ppermute(value, "mp", [(i, (i + k) % N_MP) for i in range(N_MP)])


def to_other(value):
    size = lax.axis_size("dp")
    return lax.ppermute(value, "dp", [(i, i ^ 1) for i in range(size)])


def gathered(value):
    return [value] + [to_next(value, k) for k in range(1, N_MP)]


def gathered_halves(whole, half):
    got = [to_next(half, k) for k in range(1, N_MP)]
    out = [whole]
    for value in got:
        out += [value, to_other(value)]
    return out


def run_first(ids, plan, audio, gram, wp):
    return call(
        first_kernel,
        (
            shape((D, ROWS), bf16),
            shape((D, ROWS), bf16),
            shape((ROWS, D), bf16),
            shape((JOBS, D + ROWS, BLOCK), bf16),
        ),
        "ssss" + "v" * 12,
        (ids, *plan, *audio, gram, *wp),
        scratch=work_shapes(),
    )


def work_shapes():
    return [
        SMEM((JOBS,), jnp.int32),
        VMEM((4, WIN, 256), bf16),
        VMEM((D, BLOCK), bf16),
        VMEM((D, WIN), bf16),
        VMEM((MEL, BLOCK), f32),
        VMEM((MEL, 640), bf16),
        VMEM((D + ROWS, BLOCK), bf16),
    ]


def run_second(ids, plan, audio, gram, first, wa_t, wm, wo):
    return call(
        second_kernel,
        (shape((JOBS, 2 * MEL, 128), bf16),) + (shape((JOBS, PIECE, 128), bf16),) * 4,
        "ssss" + "v" * 18,
        (ids, *plan, *audio, gram, *first, wa_t, wm, *wo),
        scratch=work_shapes() + [VMEM((D + MEL, D + ROWS), bf16), VMEM((4 * PIECE, 128), bf16)],
    )


def shards(
    mel_audio, start_noise, span_start, span_length, block_route,
    w_input, attn_gain, w_qkv, w_out, final_gain, w_mel,
):
    e_rows = jnp.asarray(time_rows())
    ids = jnp.stack([lax.axis_index("dp"), lax.axis_index("mp")]).astype(jnp.int32)
    plan = (block_route, span_start, span_length)
    w3 = jnp.transpose(w_qkv, (1, 0, 2))
    whole, half = call(
        fold_kernel,
        (shape((3, ROWS, 256), bf16), shape((3, ROWS, 128), bf16)),
        "svvvv",
        (ids, w_input, e_rows, attn_gain.reshape(1, D), w3),
    )
    wp = gathered_halves(whole, half)
    audio = (mel_audio, to_other(mel_audio), start_noise, to_other(start_noise))
    wa_t, gram, wo_t, wo_half, wm = call(
        prep_kernel,
        (
            shape((D, ROWS), bf16),
            shape((2 * ROWS, ROWS), bf16),
            shape((D, 256), bf16),
            shape((D, 128), bf16),
            shape((MEL, D), bf16),
        ),
        "svvvvv",
        (ids, w_input, e_rows, w_out, w_mel, final_gain.reshape(1, D)),
    )
    wo = gathered_halves(wo_t, wo_half)
    slot_ids = ids[0] * WORK_DEV + jnp.arange(WORK_DEV, dtype=jnp.int32)
    matches = block_route[None, :] == slot_ids[:, None]
    every = jnp.arange(block_route.shape[0], dtype=jnp.int32)
    owners = jnp.sum(jnp.where(matches, every[None, :], 0), axis=1) // SLOT_DEV

    first = run_first(ids, plan, audio, gram, wp)
    tot, v0, v1, v2, v3 = run_second(ids, plan, audio, gram, first, wa_t, wm, wo)
    pieces = [v0] + [to_next(v, k) for k, v in ((1, v1), (2, v2), (3, v3))]
    pieces += [to_other(v) for v in pieces]
    totals = gathered(tot)
    totals += [to_other(t) for t in totals]
    packed = call(
        pack_kernel, shape((32, PIECE, 128), bf16), "ss" + "v" * 8, (ids, block_route, *pieces)
    )
    got = lax.all_to_all(packed, "dp", 0, 0, tiled=True)
    chosen = call(select_kernel, shape((WORK_DEV, PIECE, 128), bf16), "sv", (owners, got))
    parts = gathered(chosen)
    infilled = call(
        span_kernel,
        shape((UTT_DEV, MEL, SPAN_MAX), f32),
        "ss" + "v" * 8,
        (ids, block_route, *totals),
    )
    velocity = call(
        final_kernel,
        shape((WORK_DEV, MEL, BLOCK), f32),
        "svvvv",
        (ids, *parts),
        scratch=[VMEM((WORK_DEV, 4 * PIECE, 128), bf16)],
    )
    return (infilled, velocity)


def solution(mesh):
    return jax.shard_map(
        shards,
        mesh=mesh,
        in_specs=(
            P("dp", None, None),
            P("dp", None, None),
            P(),
            P(),
            P(),
            P(),
            P(),
            P(None, None, "mp"),
            P("mp", None),
            P(),
            P(),
        ),
        out_specs=(P("dp", None, None), P("dp", None, None)),
        check_vma=False,
    )
```

time: 169 us -> 129 us (0.76)
  Pallas kernels: 76.3 us -> 40.5 us
  waiting for transfers between devices: 43.2 us -> 15.7 us
  starting transfers between devices: 42.7 us -> 64 us
  local copies, waits for them, and re-layouts: 4.61 us -> 6.6 us
    pallas_call x7 -> x8, Pallas kernels: 76.3 us -> 40.5 us  [call(): pl.pallas_call(kernel, out_shape=outs, in_specs=[spec(k) for k in kinds],...]
    ppermute x15, waiting for transfers between devices: 36.8 us -> 6.89 us  [to_next(): return lax.ppermute(value, 'mp', [(i, (i + k) % N_MP) for i in range(N_MP)])]
    ppermute x0 -> x16, starting transfers between devices: none -> 25.4 us  [to_other(): return lax.ppermute(value, 'dp', [(i, i ^ 1) for i in range(size)])]
    all_to_all x1, starting transfers between devices: 24.2 us -> 18.5 us  [shards(): got = lax.all_to_all(packed, 'dp', 0, 0, tiled=True)]
    unnamed x36 -> x70, local copies, waits for them, and re-layouts: 4.61 us -> 6.6 us
    all_to_all x1, waiting for transfers between devices: 6.36 us -> 8.33 us  [shards(): got = lax.all_to_all(packed, 'dp', 0, 0, tiled=True)]
    ppermute x15, starting transfers between devices: 18.4 us -> 20.1 us  [to_next(): return lax.ppermute(value, 'mp', [(i, (i + k) % N_MP) for i in range(N_MP)])]
  transfers between devices with their start and end apart: 16 -> 32, of which waited for: 6 -> 6; matrix products, arithmetic and copies ran while one was open for 1% -> 1% of each run, Pallas kernels for 4% -> 19%
where the time goes in v1:
time: 129 us
  starting transfers between devices  64 us (50%)
  Pallas kernels  40.5 us (31%)
  waiting for transfers between devices  15.7 us (12%)
  local copies, waits for them, and re-layouts  6.6 us (5%)
  other arithmetic  1.35 us (1%)
    pallas_call x8, Pallas kernels, call(): pl.pallas_call(kernel, out_shape=outs, in_specs=[spec(k) for k in kinds],...  40.5 us
    ppermute x16, starting transfers between devices, to_other(): return lax.ppermute(value, 'dp', [(i, i ^ 1) for i in range(size)])  25.4 us
    ppermute x15, starting transfers between devices, to_next(): return lax.ppermute(value, 'mp', [(i, (i + k) % N_MP) for i in range(N_MP)])  20.1 us
    all_to_all x1, starting transfers between devices, shards(): got = lax.all_to_all(packed, 'dp', 0, 0, tiled=True)  18.5 us
    all_to_all x1, waiting for transfers between devices, shards(): got = lax.all_to_all(packed, 'dp', 0, 0, tiled=True)  8.33 us
    ppermute x15, waiting for transfers between devices, to_next(): return lax.ppermute(value, 'mp', [(i, (i + k) % N_MP) for i in range(N_MP)])  6.89 us
    unnamed x70, local copies, waits for them, and re-layouts  6.6 us
  transfers between devices with their start and end apart: 32, of which 6 were waited for; matrix products, arithmetic and copies ran while one was open for 1% of the time, Pallas kernels for 19%

profile of v1, /device:TPU:1, one launch (start us, length us, event | category | flops | bytes accessed | tf_op | source)
XLA Modules:
  0.0 129.2 jit_solution(11743069542765382549)
XLA Ops:
  0.6 1.5 %collective-permute-start = (bf16[4,80,2048]{2,1,0:T(8,128)(2,1)}, bf16[4,80,2048]{2,1,0:T(8,128)(2,1)S(1)}, u32[]{:S(2)}, u32[]{:S(2)}) collective-permute-start(bf16[4,80,2048]{2,1,0:T(8,128)(2,1)} %mel_a.3), channel_id=1, source_target_pairs={{0,4},{4,0},{8,12},{12,8},{16,20},{20,16},{24,28},{28,24},{32,36},... | collective-permute-start | bytes 3932168 | tf_op jit(solution)/shard_map/ppermute | solution.py:372
  2.8 3.0 %shard_map.132 = (bf16[3,176,256]{2,1,0:T(8,128)(2,1)}, bf16[3,176,128]{2,1,0:T(8,128)(2,1)}) custom-call(s32[2]{0:T(128)} %pad_add_fusion.ids, bf16[160,1024]{1,0:T(8,128)(2,1)} %w_in.3, f32[16,1024]{1,0:T(8,128)} %constant.30.clone.e_rows, f32[1,1024]{1,0:T(1,128)} %bitcast.6, bf16[3,1024,256]{2,1,0:T(8,128)(2,1)} %bitcast.5), custom_call_target="tpu_custom_call" | custom-call | tf_op jit(solution)/shard_map/pallas_call | solution.py:352
  5.8 1.7 %collective-permute-start.2 = (bf16[3,176,128]{2,1,0:T(8,128)(2,1)}, bf16[3,176,128]{2,1,0:T(8,128)(2,1)S(1)}, u32[]{:S(2)}, u32[]{:S(2)}) collective-permute-start(bf16[3,176,128]{2,1,0:T(8,128)(2,1)} %get-tuple-element.20), channel_id=1, source_target_pairs={{0,1},{1,2},{2,3},{3,0},{4,5},{5,6},{6,7},{7,4},{8,9},{9,10},{10,1... | collective-permute-start | bytes 405512 | tf_op jit(solution)/shard_map/ppermute | solution.py:367
  7.5 3.3 %collective-permute-start.4 = (bf16[3,176,128]{2,1,0:T(8,128)(2,1)}, bf16[3,176,128]{2,1,0:T(8,128)(2,1)S(1)}, u32[]{:S(2)}, u32[]{:S(2)}) collective-permute-start(bf16[3,176,128]{2,1,0:T(8,128)(2,1)} %get-tuple-element.20), channel_id=1, source_target_pairs={{0,2},{1,3},{2,0},{3,1},{4,6},{5,7},{6,4},{7,5},{8,10},{9,11},{10,... | collective-permute-start | bytes 405512 | tf_op jit(solution)/shard_map/ppermute | solution.py:367
  10.8 0.7 collective-permute-start.6
  11.5 2.9 %shard_map.131 = (bf16[1024,176]{1,0:T(8,128)(2,1)}, bf16[352,176]{1,0:T(8,128)(2,1)}, bf16[1024,256]{1,0:T(8,128)(2,1)}, bf16[1024,128]{1,0:T(8,128)(2,1)}, bf16[80,1024]{1,0:T(8,128)(2,1)}) custom-call(s32[2]{0:T(128)} %pad_add_fusion.ids, bf16[160,1024]{1,0:T(8,128)(2,1)} %w_in.3, f32[16,1024]{1,0:T(8,128)} %constant.30.clone.e_rows, ...), custom_call_target="tpu_custom_call" | custom-call | tf_op jit(solution)/shard_map/pallas_call | solution.py:352
  14.9 2.7 %collective-permute-start.12 = (bf16[1024,128]{1,0:T(8,128)(2,1)}, bf16[1024,128]{1,0:T(8,128)(2,1)S(1)}, u32[]{:S(2)}, u32[]{:S(2)}) collective-permute-start(bf16[1024,128]{1,0:T(8,128)(2,1)} %get-tuple-element.28), channel_id=1, source_target_pairs={{0,3},{1,0},{2,1},{3,2},{4,7},{5,4},{6,5},{7,6},{8,11},{9,8},{10,9... | collective-permute-start | bytes 786440 | tf_op jit(solution)/shard_map/ppermute | solution.py:367
  17.7 1.4 %collective-permute-start.1 = (bf16[4,80,1024]{2,1,0:T(8,128)(2,1)S(1)}, bf16[4,80,1024]{2,1,0:T(8,128)(2,1)S(1)}, u32[]{:S(2)}, u32[]{:S(2)}) collective-permute-start(bf16[4,80,1024]{2,1,0:T(8,128)(2,1)S(1)} %copy-done.1), channel_id=1, source_target_pairs={{0,4},{4,0},{8,12},{12,8},{16,20},{20,16},{24,28},{28,24},{32,36},... | collective-permute-start | bytes 1966088 | tf_op jit(solution)/shard_map/ppermute | solution.py:372
  19.1 4.0 %collective-permute-done.10.ho2 = bf16[1024,128]{1,0:T(8,128)(2,1)S(1)} collective-permute-done((bf16[1024,128]{1,0:T(8,128)(2,1)}, bf16[1024,128]{1,0:T(8,128)(2,1)S(1)}, u32[]{:S(2)}, u32[]{:S(2)}) %collective-permute-start.10) | collective-permute-done | bytes 262176 | tf_op jit(solution)/shard_map/ppermute | solution.py:367
  23.1 3.1 %collective-permute-start.3 = (bf16[3,176,128]{2,1,0:T(8,128)(2,1)S(1)}, bf16[3,176,128]{2,1,0:T(8,128)(2,1)S(1)}, u32[]{:S(2)}, u32[]{:S(2)}) collective-permute-start(bf16[3,176,128]{2,1,0:T(8,128)(2,1)S(1)} %collective-permute-done.2.hp1), channel_id=1, source_target_pairs={{0,4},{4,0},{8,12},{12,8},{16,20},{20,16},{24,28},{28,24},{32,36},... | collective-permute-start | bytes 405512 | tf_op jit(solution)/shard_map/ppermute | solution.py:372
  26.2 2.1 %collective-permute-done.12.ho3 = bf16[1024,128]{1,0:T(8,128)(2,1)S(1)} collective-permute-done((bf16[1024,128]{1,0:T(8,128)(2,1)}, bf16[1024,128]{1,0:T(8,128)(2,1)S(1)}, u32[]{:S(2)}, u32[]{:S(2)}) %collective-permute-start.12) | collective-permute-done | bytes 262176 | tf_op jit(solution)/shard_map/ppermute | solution.py:367
  28.3 0.8 collective-permute-start.5
  29.1 0.7 collective-permute-done.8.ho1
  33.1 9.5 %shard_map.133 = (bf16[1024,176]{1,0:T(8,128)(2,1)}, bf16[1024,176]{1,0:T(8,128)(2,1)}, bf16[176,1024]{1,0:T(8,128)(2,1)}, bf16[4,1200,256]{2,1,0:T(8,128)(2,1)}) custom-call(s32[2]{0:T(128)} %pad_add_fusion.ids, s32[512]{0:T(512)} %route.7, s32[128]{0:T(128)} %starts.3, s32[128]{0:T(128)} %lengths.3, bf16[4,80,2048]{2,1,0:T(8,128)(2,1)} %mel_a.3, ...), custom_call_target="tpu_custom_call" | custom-call | tf_op jit(solution)/shard_map/pallas_call | solution.py:352
  43.5 13.7 %shard_map.134 = (bf16[4,160,128]{2,1,0:T(8,128)(2,1)}, bf16[4,48,128]{2,1,0:T(8,128)(2,1)}, bf16[4,48,128]{2,1,0:T(8,128)(2,1)}, bf16[4,48,128]{2,1,0:T(8,128)(2,1)}, bf16[4,48,128]{2,1,0:T(8,128)(2,1)}) custom-call(s32[2]{0:T(128)} %pad_add_fusion.ids, s32[512]{0:T(512)} %route.7, s32[128]{0:T(128)} %starts.3, s32[128]{0:T(128)} %lengths.3, ...), custom_call_target="tpu_custom_call" | custom-call | tf_op jit(solution)/shard_map/pallas_call | solution.py:352
  57.5 2.1 %collective-permute-start.22 = (bf16[4,48,128]{2,1,0:T(8,128)(2,1)}, bf16[4,48,128]{2,1,0:T(8,128)(2,1)S(1)}, u32[]{:S(2)}, u32[]{:S(2)}) collective-permute-start(bf16[4,48,128]{2,1,0:T(8,128)(2,1)} %get-tuple-element.32), channel_id=1, source_target_pairs={{0,2},{1,3},{2,0},{3,1},{4,6},{5,7},{6,4},{7,5},{8,10},{9,11},{10,... | collective-permute-start | bytes 147464 | tf_op jit(solution)/shard_map/ppermute | solution.py:367
  59.6 1.3 %collective-permute-start.23 = (bf16[4,48,128]{2,1,0:T(8,128)(2,1)}, bf16[4,48,128]{2,1,0:T(8,128)(2,1)S(1)}, u32[]{:S(2)}, u32[]{:S(2)}) collective-permute-start(bf16[4,48,128]{2,1,0:T(8,128)(2,1)} %get-tuple-element.33), channel_id=1, source_target_pairs={{0,3},{1,0},{2,1},{3,2},{4,7},{5,4},{6,5},{7,6},{8,11},{9,8},{10,9... | collective-permute-start | bytes 147464 | tf_op jit(solution)/shard_map/ppermute | solution.py:367
  60.9 13.2 %collective-permute-start.24 = (bf16[4,48,128]{2,1,0:T(8,128)(2,1)}, bf16[4,48,128]{2,1,0:T(8,128)(2,1)S(1)}, u32[]{:S(2)}, u32[]{:S(2)}) collective-permute-start(bf16[4,48,128]{2,1,0:T(8,128)(2,1)} %get-tuple-element.30.a0), channel_id=1, source_target_pairs={{0,4},{4,0},{8,12},{12,8},{16,20},{20,16},{24,28},{28,24},{32,36},... | collective-permute-start | bytes 147464 | tf_op jit(solution)/shard_map/ppermute | solution.py:372
  74.1 0.8 collective-permute-start.25
  74.9 1.0 collective-permute-start.26
  75.9 0.9 collective-permute-start.27
  76.8 0.7 collective-permute-start.14
  77.6 3.0 %collective-permute-start.15 = (bf16[4,160,128]{2,1,0:T(8,128)(2,1)}, bf16[4,160,128]{2,1,0:T(8,128)(2,1)S(1)}, u32[]{:S(2)}, u32[]{:S(2)}) collective-permute-start(bf16[4,160,128]{2,1,0:T(8,128)(2,1)} %get-tuple-element.29.a0), channel_id=1, source_target_pairs={{0,2},{1,3},{2,0},{3,1},{4,6},{5,7},{6,4},{7,5},{8,10},{9,11},{10,... | collective-permute-start | bytes 491528 | tf_op jit(solution)/shard_map/ppermute | solution.py:367
  81.8 3.6 %shard_map.136 = bf16[32,48,128]{2,1,0:T(8,128)(2,1)} custom-call(s32[2]{0:T(128)} %pad_add_fusion.ids, s32[512]{0:T(512)} %route.7, bf16[4,48,128]{2,1,0:T(8,128)(2,1)} %get-tuple-element.30.a0, bf16[4,48,128]{2,1,0:T(8,128)(2,1)} %copy-done.28, bf16[4,48,128]{2,1,0:T(8,128)(2,1)} %copy-done.29, bf16[4,48,128]{2,1,0:T(8,128)(2,1)} %copy-done.30, ...), custom_call_target="tpu_custom_call" | custom-call | tf_op jit(solution)/shard_map/pallas_call | solution.py:352
  85.3 18.5 %all-to-all-start = ((bf16[32,48,128]{2,1,0:T(8,128)(2,1)}), bf16[32,48,128]{2,1,0:T(8,128)(2,1)S(1)}, u32[]{:S(2)}, u32[]{:S(2)}) async-start(bf16[32,48,128]{2,1,0:T(8,128)(2,1)} %shard_map.136), calls=%async_computation | async-start | bytes 786432 | tf_op jit(solution)/shard_map/all_to_all | solution.py:467
  105.7 8.3 %all-to-all-done.got = bf16[32,48,128]{2,1,0:T(8,128)(2,1)S(1)} async-done(((bf16[32,48,128]{2,1,0:T(8,128)(2,1)}), bf16[32,48,128]{2,1,0:T(8,128)(2,1)S(1)}, u32[]{:S(2)}, u32[]{:S(2)}) %all-to-all-start) | async-done | bytes 393248 | tf_op jit(solution)/shard_map/all_to_all | solution.py:467
  114.0 0.7 copy-done.3
  114.8 1.6 %shard_map.137.b0 = bf16[6,48,128]{2,1,0:T(8,128)(2,1)} custom-call(s32[6]{0:T(128)} %and_select_fusion.owners, bf16[32,48,128]{2,1,0:T(8,128)(2,1)} %copy-done.3), custom_call_target="tpu_custom_call" | custom-call | tf_op jit(solution)/shard_map/pallas_call | solution.py:352
  116.4 1.4 %collective-permute-start.28 = (bf16[6,48,128]{2,1,0:T(8,128)(2,1)}, bf16[6,48,128]{2,1,0:T(8,128)(2,1)S(1)}, u32[]{:S(2)}, u32[]{:S(2)}) collective-permute-start(bf16[6,48,128]{2,1,0:T(8,128)(2,1)} %shard_map.137.b0), channel_id=1, source_target_pairs={{0,1},{1,2},{2,3},{3,0},{4,5},{5,6},{6,7},{7,4},{8,9},{9,10},{10,1... | collective-permute-start | bytes 221192 | tf_op jit(solution)/shard_map/ppermute | solution.py:367
  117.8 2.5 %collective-permute-start.30 = (bf16[6,48,128]{2,1,0:T(8,128)(2,1)}, bf16[6,48,128]{2,1,0:T(8,128)(2,1)S(1)}, u32[]{:S(2)}, u32[]{:S(2)}) collective-permute-start(bf16[6,48,128]{2,1,0:T(8,128)(2,1)} %shard_map.137.b0), channel_id=1, source_target_pairs={{0,3},{1,0},{2,1},{3,2},{4,7},{5,4},{6,5},{7,6},{8,11},{9,8},{10,9... | collective-permute-start | bytes 221192 | tf_op jit(solution)/shard_map/ppermute | solution.py:367
  121.6 4.4 %shard_map.135 = f32[4,80,1024]{2,1,0:T(8,128)} custom-call(s32[2]{0:T(128)} %pad_add_fusion.ids, s32[512]{0:T(512)} %route.7, bf16[4,160,128]{2,1,0:T(8,128)(2,1)} %get-tuple-element.29.a0, bf16[4,160,128]{2,1,0:T(8,128)(2,1)} %copy-done.11, bf16[4,160,128]{2,1,0:T(8,128)(2,1)} %copy-done.12, bf16[4,160,128]{2,1,0:T(8,128)(2,1)} %copy-done.13, ...), custom_call_target="tpu_custom_call" | custom-call | tf_op jit(solution)/shard_map/pallas_call | solution.py:352
  127.3 1.8 %shard_map.138 = f32[6,80,256]{2,1,0:T(8,128)} custom-call(s32[2]{0:T(128)} %pad_add_fusion.ids, bf16[6,48,128]{2,1,0:T(8,128)(2,1)} %shard_map.137.b0, bf16[6,48,128]{2,1,0:T(8,128)(2,1)} %copy-done.24, bf16[6,48,128]{2,1,0:T(8,128)(2,1)} %copy-done.25, bf16[6,48,128]{2,1,0:T(8,128)(2,1)} %copy-done.26), custom_call_target="tpu_custom_call" | custom-call | tf_op jit(solution)/shard_map/pallas_call | solution.py:352
  (114 shorter events, 11.2 us)
Async XLA Ops:
  0.6 31.2 %collective-permute-start = (bf16[4,80,2048]{2,1,0:T(8,128)(2,1)}, bf16[4,80,2048]{2,1,0:T(8,128)(2,1)S(1)}, u32[]{:S(2)}, u32[]{:S(2)}) collective-permute-start(bf16[4,80,2048]{2,1,0:T(8,128)(2,1)} %mel_a.3), channel_id=1, source_target_pairs={{0,4},{4,0},{8,12},{12,8},{16,20},{20,16},{24,28},{28,24},{32,36},... | collective-permute-start | bytes 3932168 | tf_op jit(solution)/shard_map/ppermute | solution.py:372
  5.8 9.1 %collective-permute-start.2 = (bf16[3,176,128]{2,1,0:T(8,128)(2,1)}, bf16[3,176,128]{2,1,0:T(8,128)(2,1)S(1)}, u32[]{:S(2)}, u32[]{:S(2)}) collective-permute-start(bf16[3,176,128]{2,1,0:T(8,128)(2,1)} %get-tuple-element.20), channel_id=1, source_target_pairs={{0,1},{1,2},{2,3},{3,0},{4,5},{5,6},{6,7},{7,4},{8,9},{9,10},{10,1... | collective-permute-start | bytes 405512 | tf_op jit(solution)/shard_map/ppermute | solution.py:367
  7.5 10.2 %collective-permute-start.4 = (bf16[3,176,128]{2,1,0:T(8,128)(2,1)}, bf16[3,176,128]{2,1,0:T(8,128)(2,1)S(1)}, u32[]{:S(2)}, u32[]{:S(2)}) collective-permute-start(bf16[3,176,128]{2,1,0:T(8,128)(2,1)} %get-tuple-element.20), channel_id=1, source_target_pairs={{0,2},{1,3},{2,0},{3,1},{4,6},{5,7},{6,4},{7,5},{8,10},{9,11},{10,... | collective-permute-start | bytes 405512 | tf_op jit(solution)/shard_map/ppermute | solution.py:367
  10.8 6.9 %collective-permute-start.6 = (bf16[3,176,128]{2,1,0:T(8,128)(2,1)}, bf16[3,176,128]{2,1,0:T(8,128)(2,1)S(1)}, u32[]{:S(2)}, u32[]{:S(2)}) collective-permute-start(bf16[3,176,128]{2,1,0:T(8,128)(2,1)} %get-tuple-element.20), channel_id=1, source_target_pairs={{0,3},{1,0},{2,1},{3,2},{4,7},{5,4},{6,5},{7,6},{8,11},{9,8},{10,9... | collective-permute-start | bytes 405512 | tf_op jit(solution)/shard_map/ppermute | solution.py:367
  14.4 8.7 %collective-permute-start.10 = (bf16[1024,128]{1,0:T(8,128)(2,1)}, bf16[1024,128]{1,0:T(8,128)(2,1)S(1)}, u32[]{:S(2)}, u32[]{:S(2)}) collective-permute-start(bf16[1024,128]{1,0:T(8,128)(2,1)} %get-tuple-element.28), channel_id=1, source_target_pairs={{0,2},{1,3},{2,0},{3,1},{4,6},{5,7},{6,4},{7,5},{8,10},{9,11},{10,... | collective-permute-start | bytes 786440 | tf_op jit(solution)/shard_map/ppermute | solution.py:367
  14.9 13.4 %collective-permute-start.12 = (bf16[1024,128]{1,0:T(8,128)(2,1)}, bf16[1024,128]{1,0:T(8,128)(2,1)S(1)}, u32[]{:S(2)}, u32[]{:S(2)}) collective-permute-start(bf16[1024,128]{1,0:T(8,128)(2,1)} %get-tuple-element.28), channel_id=1, source_target_pairs={{0,3},{1,0},{2,1},{3,2},{4,7},{5,4},{6,5},{7,6},{8,11},{9,8},{10,9... | collective-permute-start | bytes 786440 | tf_op jit(solution)/shard_map/ppermute | solution.py:367
  17.6 12.2 %collective-permute-start.8 = (bf16[1024,128]{1,0:T(8,128)(2,1)}, bf16[1024,128]{1,0:T(8,128)(2,1)S(1)}, u32[]{:S(2)}, u32[]{:S(2)}) collective-permute-start(bf16[1024,128]{1,0:T(8,128)(2,1)} %get-tuple-element.28), channel_id=1, source_target_pairs={{0,1},{1,2},{2,3},{3,0},{4,5},{5,6},{6,7},{7,4},{8,9},{9,10},{10,1... | collective-permute-start | bytes 786440 | tf_op jit(solution)/shard_map/ppermute | solution.py:367
  17.7 14.2 %collective-permute-start.1 = (bf16[4,80,1024]{2,1,0:T(8,128)(2,1)S(1)}, bf16[4,80,1024]{2,1,0:T(8,128)(2,1)S(1)}, u32[]{:S(2)}, u32[]{:S(2)}) collective-permute-start(bf16[4,80,1024]{2,1,0:T(8,128)(2,1)S(1)} %copy-done.1), channel_id=1, source_target_pairs={{0,4},{4,0},{8,12},{12,8},{16,20},{20,16},{24,28},{28,24},{32,36},... | collective-permute-start | bytes 1966088 | tf_op jit(solution)/shard_map/ppermute | solution.py:372
  23.1 7.4 %collective-permute-start.3 = (bf16[3,176,128]{2,1,0:T(8,128)(2,1)S(1)}, bf16[3,176,128]{2,1,0:T(8,128)(2,1)S(1)}, u32[]{:S(2)}, u32[]{:S(2)}) collective-permute-start(bf16[3,176,128]{2,1,0:T(8,128)(2,1)S(1)} %collective-permute-done.2.hp1), channel_id=1, source_target_pairs={{0,4},{4,0},{8,12},{12,8},{16,20},{20,16},{24,28},{28,24},{32,36},... | collective-permute-start | bytes 405512 | tf_op jit(solution)/shard_map/ppermute | solution.py:372
  28.3 2.3 %collective-permute-start.5 = (bf16[3,176,128]{2,1,0:T(8,128)(2,1)S(1)}, bf16[3,176,128]{2,1,0:T(8,128)(2,1)S(1)}, u32[]{:S(2)}, u32[]{:S(2)}) collective-permute-start(bf16[3,176,128]{2,1,0:T(8,128)(2,1)S(1)} %collective-permute-done.4.hp2), channel_id=1, source_target_pairs={{0,4},{4,0},{8,12},{12,8},{16,20},{20,16},{24,28},{28,24},{32,36},... | collective-permute-start | bytes 405512 | tf_op jit(solution)/shard_map/ppermute | solution.py:372
  29.8 1.6 %collective-permute-start.7 = (bf16[3,176,128]{2,1,0:T(8,128)(2,1)S(1)}, bf16[3,176,128]{2,1,0:T(8,128)(2,1)S(1)}, u32[]{:S(2)}, u32[]{:S(2)}) collective-permute-start(bf16[3,176,128]{2,1,0:T(8,128)(2,1)S(1)} %collective-permute-done.6.hp3), channel_id=1, source_target_pairs={{0,4},{4,0},{8,12},{12,8},{16,20},{20,16},{24,28},{28,24},{32,36},... | collective-permute-start | bytes 405512 | tf_op jit(solution)/shard_map/ppermute | solution.py:372
  30.5 12.1 %collective-permute-start.11 = (bf16[1024,128]{1,0:T(8,128)(2,1)S(1)}, bf16[1024,128]{1,0:T(8,128)(2,1)S(1)}, u32[]{:S(2)}, u32[]{:S(2)}) collective-permute-start(bf16[1024,128]{1,0:T(8,128)(2,1)S(1)} %collective-permute-done.10.ho2), channel_id=1, source_target_pairs={{0,4},{4,0},{8,12},{12,8},{16,20},{20,16},{24,28},{28,24},{32,36},... | collective-permute-start | bytes 786440 | tf_op jit(solution)/shard_map/ppermute | solution.py:372
  30.6 12.0 %collective-permute-start.13 = (bf16[1024,128]{1,0:T(8,128)(2,1)S(1)}, bf16[1024,128]{1,0:T(8,128)(2,1)S(1)}, u32[]{:S(2)}, u32[]{:S(2)}) collective-permute-start(bf16[1024,128]{1,0:T(8,128)(2,1)S(1)} %collective-permute-done.12.ho3), channel_id=1, source_target_pairs={{0,4},{4,0},{8,12},{12,8},{16,20},{20,16},{24,28},{28,24},{32,36},... | collective-permute-start | bytes 786440 | tf_op jit(solution)/shard_map/ppermute | solution.py:372
  31.5 11.2 %collective-permute-start.9 = (bf16[1024,128]{1,0:T(8,128)(2,1)S(1)}, bf16[1024,128]{1,0:T(8,128)(2,1)S(1)}, u32[]{:S(2)}, u32[]{:S(2)}) collective-permute-start(bf16[1024,128]{1,0:T(8,128)(2,1)S(1)} %collective-permute-done.8.ho1), channel_id=1, source_target_pairs={{0,4},{4,0},{8,12},{12,8},{16,20},{20,16},{24,28},{28,24},{32,36},... | collective-permute-start | bytes 786440 | tf_op jit(solution)/shard_map/ppermute | solution.py:372
  57.2 16.9 %collective-permute-start.21 = (bf16[4,48,128]{2,1,0:T(8,128)(2,1)}, bf16[4,48,128]{2,1,0:T(8,128)(2,1)S(1)}, u32[]{:S(2)}, u32[]{:S(2)}) collective-permute-start(bf16[4,48,128]{2,1,0:T(8,128)(2,1)} %get-tuple-element.31), channel_id=1, source_target_pairs={{0,1},{1,2},{2,3},{3,0},{4,5},{5,6},{6,7},{7,4},{8,9},{9,10},{10,1... | collective-permute-start | bytes 147464 | tf_op jit(solution)/shard_map/ppermute | solution.py:367
  57.5 17.4 %collective-permute-start.22 = (bf16[4,48,128]{2,1,0:T(8,128)(2,1)}, bf16[4,48,128]{2,1,0:T(8,128)(2,1)S(1)}, u32[]{:S(2)}, u32[]{:S(2)}) collective-permute-start(bf16[4,48,128]{2,1,0:T(8,128)(2,1)} %get-tuple-element.32), channel_id=1, source_target_pairs={{0,2},{1,3},{2,0},{3,1},{4,6},{5,7},{6,4},{7,5},{8,10},{9,11},{10,... | collective-permute-start | bytes 147464 | tf_op jit(solution)/shard_map/ppermute | solution.py:367
  59.6 16.3 %collective-permute-start.23 = (bf16[4,48,128]{2,1,0:T(8,128)(2,1)}, bf16[4,48,128]{2,1,0:T(8,128)(2,1)S(1)}, u32[]{:S(2)}, u32[]{:S(2)}) collective-permute-start(bf16[4,48,128]{2,1,0:T(8,128)(2,1)} %get-tuple-element.33), channel_id=1, source_target_pairs={{0,3},{1,0},{2,1},{3,2},{4,7},{5,4},{6,5},{7,6},{8,11},{9,8},{10,9... | collective-permute-start | bytes 147464 | tf_op jit(solution)/shard_map/ppermute | solution.py:367
  60.9 16.6 %collective-permute-start.24 = (bf16[4,48,128]{2,1,0:T(8,128)(2,1)}, bf16[4,48,128]{2,1,0:T(8,128)(2,1)S(1)}, u32[]{:S(2)}, u32[]{:S(2)}) collective-permute-start(bf16[4,48,128]{2,1,0:T(8,128)(2,1)} %get-tuple-element.30.a0), channel_id=1, source_target_pairs={{0,4},{4,0},{8,12},{12,8},{16,20},{20,16},{24,28},{28,24},{32,36},... | collective-permute-start | bytes 147464 | tf_op jit(solution)/shard_map/ppermute | solution.py:372
  74.1 6.4 %collective-permute-start.25 = (bf16[4,48,128]{2,1,0:T(8,128)(2,1)S(1)}, bf16[4,48,128]{2,1,0:T(8,128)(2,1)S(1)}, u32[]{:S(2)}, u32[]{:S(2)}) collective-permute-start(bf16[4,48,128]{2,1,0:T(8,128)(2,1)S(1)} %collective-permute-done.21.a1), channel_id=1, source_target_pairs={{0,4},{4,0},{8,12},{12,8},{16,20},{20,16},{24,28},{28,24},{32,36},... | collective-permute-start | bytes 147464 | tf_op jit(solution)/shard_map/ppermute | solution.py:372
  74.9 5.6 %collective-permute-start.26 = (bf16[4,48,128]{2,1,0:T(8,128)(2,1)S(1)}, bf16[4,48,128]{2,1,0:T(8,128)(2,1)S(1)}, u32[]{:S(2)}, u32[]{:S(2)}) collective-permute-start(bf16[4,48,128]{2,1,0:T(8,128)(2,1)S(1)} %collective-permute-done.22.a2), channel_id=1, source_target_pairs={{0,4},{4,0},{8,12},{12,8},{16,20},{20,16},{24,28},{28,24},{32,36},... | collective-permute-start | bytes 147464 | tf_op jit(solution)/shard_map/ppermute | solution.py:372
  75.9 4.6 %collective-permute-start.27 = (bf16[4,48,128]{2,1,0:T(8,128)(2,1)S(1)}, bf16[4,48,128]{2,1,0:T(8,128)(2,1)S(1)}, u32[]{:S(2)}, u32[]{:S(2)}) collective-permute-start(bf16[4,48,128]{2,1,0:T(8,128)(2,1)S(1)} %collective-permute-done.23.a3), channel_id=1, source_target_pairs={{0,4},{4,0},{8,12},{12,8},{16,20},{20,16},{24,28},{28,24},{32,36},... | collective-permute-start | bytes 147464 | tf_op jit(solution)/shard_map/ppermute | solution.py:372
  76.8 27.6 %collective-permute-start.14 = (bf16[4,160,128]{2,1,0:T(8,128)(2,1)}, bf16[4,160,128]{2,1,0:T(8,128)(2,1)S(1)}, u32[]{:S(2)}, u32[]{:S(2)}) collective-permute-start(bf16[4,160,128]{2,1,0:T(8,128)(2,1)} %get-tuple-element.29.a0), channel_id=1, source_target_pairs={{0,1},{1,2},{2,3},{3,0},{4,5},{5,6},{6,7},{7,4},{8,9},{9,10},{10,1... | collective-permute-start | bytes 491528 | tf_op jit(solution)/shard_map/ppermute | solution.py:367
  77.6 27.1 %collective-permute-start.15 = (bf16[4,160,128]{2,1,0:T(8,128)(2,1)}, bf16[4,160,128]{2,1,0:T(8,128)(2,1)S(1)}, u32[]{:S(2)}, u32[]{:S(2)}) collective-permute-start(bf16[4,160,128]{2,1,0:T(8,128)(2,1)} %get-tuple-element.29.a0), channel_id=1, source_target_pairs={{0,2},{1,3},{2,0},{3,1},{4,6},{5,7},{6,4},{7,5},{8,10},{9,11},{10,... | collective-permute-start | bytes 491528 | tf_op jit(solution)/shard_map/ppermute | solution.py:367
  80.5 24.4 %collective-permute-start.16 = (bf16[4,160,128]{2,1,0:T(8,128)(2,1)}, bf16[4,160,128]{2,1,0:T(8,128)(2,1)S(1)}, u32[]{:S(2)}, u32[]{:S(2)}) collective-permute-start(bf16[4,160,128]{2,1,0:T(8,128)(2,1)} %get-tuple-element.29.a0), channel_id=1, source_target_pairs={{0,3},{1,0},{2,1},{3,2},{4,7},{5,4},{6,5},{7,6},{8,11},{9,8},{10,9... | collective-permute-start | bytes 491528 | tf_op jit(solution)/shard_map/ppermute | solution.py:367
  85.3 28.7 %all-to-all-start = ((bf16[32,48,128]{2,1,0:T(8,128)(2,1)}), bf16[32,48,128]{2,1,0:T(8,128)(2,1)S(1)}, u32[]{:S(2)}, u32[]{:S(2)}) async-start(bf16[32,48,128]{2,1,0:T(8,128)(2,1)} %shard_map.136), calls=%async_computation | async-start | bytes 786432 | tf_op jit(solution)/shard_map/all_to_all | solution.py:467
  104.1 13.7 %collective-permute-start.17 = (bf16[4,160,128]{2,1,0:T(8,128)(2,1)S(1)}, bf16[4,160,128]{2,1,0:T(8,128)(2,1)S(1)}, u32[]{:S(2)}, u32[]{:S(2)}) collective-permute-start(bf16[4,160,128]{2,1,0:T(8,128)(2,1)S(1)} %copy-done.10), channel_id=1, source_target_pairs={{0,4},{4,0},{8,12},{12,8},{16,20},{20,16},{24,28},{28,24},{32,36},... | collective-permute-start | bytes 491528 | tf_op jit(solution)/shard_map/ppermute | solution.py:372
  104.4 13.4 %collective-permute-start.18 = (bf16[4,160,128]{2,1,0:T(8,128)(2,1)S(1)}, bf16[4,160,128]{2,1,0:T(8,128)(2,1)S(1)}, u32[]{:S(2)}, u32[]{:S(2)}) collective-permute-start(bf16[4,160,128]{2,1,0:T(8,128)(2,1)S(1)} %collective-permute-done.14.a1), channel_id=1, source_target_pairs={{0,4},{4,0},{8,12},{12,8},{16,20},{20,16},{24,28},{28,24},{32,36},... | collective-permute-start | bytes 491528 | tf_op jit(solution)/shard_map/ppermute | solution.py:372
  104.7 15.6 %collective-permute-start.19 = (bf16[4,160,128]{2,1,0:T(8,128)(2,1)S(1)}, bf16[4,160,128]{2,1,0:T(8,128)(2,1)S(1)}, u32[]{:S(2)}, u32[]{:S(2)}) collective-permute-start(bf16[4,160,128]{2,1,0:T(8,128)(2,1)S(1)} %collective-permute-done.15.a2), channel_id=1, source_target_pairs={{0,4},{4,0},{8,12},{12,8},{16,20},{20,16},{24,28},{28,24},{32,36},... | collective-permute-start | bytes 491528 | tf_op jit(solution)/shard_map/ppermute | solution.py:372
  104.9 15.4 %collective-permute-start.20 = (bf16[4,160,128]{2,1,0:T(8,128)(2,1)S(1)}, bf16[4,160,128]{2,1,0:T(8,128)(2,1)S(1)}, u32[]{:S(2)}, u32[]{:S(2)}) collective-permute-start(bf16[4,160,128]{2,1,0:T(8,128)(2,1)S(1)} %collective-permute-done.16.a3), channel_id=1, source_target_pairs={{0,4},{4,0},{8,12},{12,8},{16,20},{20,16},{24,28},{28,24},{32,36},... | collective-permute-start | bytes 491528 | tf_op jit(solution)/shard_map/ppermute | solution.py:372
  116.4 9.6 %collective-permute-start.28 = (bf16[6,48,128]{2,1,0:T(8,128)(2,1)}, bf16[6,48,128]{2,1,0:T(8,128)(2,1)S(1)}, u32[]{:S(2)}, u32[]{:S(2)}) collective-permute-start(bf16[6,48,128]{2,1,0:T(8,128)(2,1)} %shard_map.137.b0), channel_id=1, source_target_pairs={{0,1},{1,2},{2,3},{3,0},{4,5},{5,6},{6,7},{7,4},{8,9},{9,10},{10,1... | collective-permute-start | bytes 221192 | tf_op jit(solution)/shard_map/ppermute | solution.py:367
  117.8 8.3 %collective-permute-start.29 = (bf16[6,48,128]{2,1,0:T(8,128)(2,1)}, bf16[6,48,128]{2,1,0:T(8,128)(2,1)S(1)}, u32[]{:S(2)}, u32[]{:S(2)}) collective-permute-start(bf16[6,48,128]{2,1,0:T(8,128)(2,1)} %shard_map.137.b0), channel_id=1, source_target_pairs={{0,2},{1,3},{2,0},{3,1},{4,6},{5,7},{6,4},{7,5},{8,10},{9,11},{10,... | collective-permute-start | bytes 221192 | tf_op jit(solution)/shard_map/ppermute | solution.py:367
  117.8 8.3 %collective-permute-start.30 = (bf16[6,48,128]{2,1,0:T(8,128)(2,1)}, bf16[6,48,128]{2,1,0:T(8,128)(2,1)S(1)}, u32[]{:S(2)}, u32[]{:S(2)}) collective-permute-start(bf16[6,48,128]{2,1,0:T(8,128)(2,1)} %shard_map.137.b0), channel_id=1, source_target_pairs={{0,3},{1,0},{2,1},{3,2},{4,7},{5,4},{6,5},{7,6},{8,11},{9,8},{10,9... | collective-permute-start | bytes 221192 | tf_op jit(solution)/shard_map/ppermute | solution.py:367
  (35 other events, 286.2 us)

commit v2 on v1

v2 whole, which is shorter than its diff:
```python
import math

import jax
import jax.numpy as jnp
import numpy as np
from jax import lax
from jax.experimental import pallas as pl
from jax.experimental.pallas import tpu as pltpu
from jax.sharding import PartitionSpec as P

D = 1024
MEL = 80
HEAD_DIM = 64
HEADS = 16
BLOCK = 256
CTX = 128
BLK_UTT = 4
UTT_DEV = 4
WORK_DEV = 6
EULER = 2
FRAMES = 2048
WIN = 512
SPAN_MAX = 1024
SLOT_DEV = 16
N_MP = 4
JOBS = 4
ROWS = 176
PIECE = 48
flow_steps = 32.0
norm_eps = 1e-05
f32 = jnp.float32
bf16 = jnp.bfloat16
VMEM = pltpu.VMEM
SMEM = pltpu.SMEM
MAIN_LIMIT = 44
SLOT_AT, JOB_AT, COUNT_AT, OWNER_AT, TABLE = 32, 64, 68, 72, 80


def time_rows():
    half = D // 2
    freqs = np.exp(-math.log(10000.0) * np.arange(half, dtype=np.float32) / half)
    rows = np.zeros((16, D), np.float32)
    for step in range(EULER):
        angles = np.float32(1000.0 * step / flow_steps) * freqs.astype(np.float32)
        e = np.concatenate([np.sin(angles), np.cos(angles)])
        e = e - e.mean()
        rows[2 * step] = e
        rows[2 * step + 1] = e
    return rows


def high_low(rows):
    high = rows.astype(bf16).astype(f32)
    odd = lax.broadcasted_iota(jnp.int32, rows.shape, 0) % 2 == 1
    return jnp.where(odd, rows - high, high)


def fold_kernel(w_in, e_rows, gain, w_qkv, out, half):
    core = lax.axis_index("dp") & 1
    w = w_in[...].astype(f32)
    wc = w - jnp.mean(w, axis=1, keepdims=True)
    g = gain[...]
    wag = jnp.concatenate([wc * g, high_low(e_rows[...] * g)], axis=0).astype(bf16)
    for c in range(3):
        res = jnp.dot(wag, w_qkv[c], preferred_element_type=f32)
        if c == 0:
            res = res * (math.log2(math.e) / math.sqrt(HEAD_DIM))
        e_res = res[160:176]
        row = lax.broadcasted_iota(jnp.int32, e_res.shape, 0)
        first = e_res[0:1] + e_res[1:2]
        second = e_res[2:3] + e_res[3:4]
        both = jnp.where(row < 2, first, jnp.where(row < 4, second, 0.0))
        out[c, 0:160, :] = res[0:160].astype(bf16)
        out[c, 160:176, :] = high_low(both).astype(bf16)
        half[c] = jnp.where(core == 0, out[c, :, 0:128], out[c, :, 128:256])


def prep_kernel(w_in, e_rows, w_out, w_mel, gain, wa_t, gram, wo_t, half, wm):
    w = w_in[...].astype(f32)
    wc = w - jnp.mean(w, axis=1, keepdims=True)
    wa = jnp.concatenate([wc, high_low(e_rows[...]), jnp.zeros((80, D), f32)], axis=0)
    wa_t[...] = wa.T[:, :ROWS].astype(bf16)
    wab = wa.astype(bf16)
    g = lax.dot_general(wab, wab, (((1,), (1,)), ((), ())), preferred_element_type=f32)
    g = g[0:ROWS, 0:ROWS] * (1.0 / D)
    high = g.astype(bf16)
    gram[0:ROWS, :] = high
    gram[ROWS : 2 * ROWS, :] = (g - high.astype(f32)).astype(bf16)
    core = lax.axis_index("dp") & 1
    o = w_out[...].astype(f32)
    o = o - jnp.mean(o, axis=1, keepdims=True)
    wo_t[...] = o.T.astype(bf16)
    half[...] = jnp.where(core == 0, wo_t[:, 0:128], wo_t[:, 128:256])
    wm[...] = (w_mel[...].astype(f32) * gain[...]).astype(bf16)


def plan_kernel(
    route, starts, lengths, mel_a, mel_b, noise_a, noise_b, gram,
    table, context_out, noise_out, valid_out, scaled_out, values_out, keys_out, own_out,
    chunk_s, x_s,
):
    dp = lax.axis_index("dp")
    m = lax.axis_index("mp")
    core = dp & 1
    base = (dp >> 1) * (2 * SLOT_DEV)
    seat = core * N_MP + m
    for i in range(TABLE):
        table[i] = -1

    def scan(s, rank):
        dest = route[base + s]
        live = dest >= 0
        q = rank >> 3

        @pl.when(jnp.logical_and(live, (rank & 7) == seat))
        def _():
            table[JOB_AT + q] = s

        @pl.when(jnp.logical_and(live, (s >> 4) == core))
        def _():
            away = ((rank >> 2) & 1) ^ core
            entry = (away * 4 + ((m - rank) & 3)) * JOBS + q
            table[entry] = (dest * 10923) >> 16
            table[SLOT_AT + entry] = s & 15

        return rank + live.astype(jnp.int32)

    n_live = lax.fori_loop(0, 2 * SLOT_DEV, scan, jnp.int32(0))
    n_jobs = (n_live - seat + 7) >> 3
    table[COUNT_AT] = n_jobs

    def owner(g, carry):
        j = route[g] - dp * WORK_DEV

        @pl.when(jnp.logical_and(j >= 0, j < WORK_DEV))
        def _():
            table[OWNER_AT + j] = g >> 4

        return carry

    lax.fori_loop(0, 32 * SLOT_DEV, owner, 0)

    def job(q, carry):
        s = table[JOB_AT + q]
        u = (s >> 2) & 3
        order = s & 3
        utter = (dp >> 1) * (2 * UTT_DEV) + (s >> 2)
        span = starts[utter]
        length = lengths[utter]
        first = span + BLOCK * order - CTX
        aligned = pl.multiple_of(jnp.clip((first >> 7) << 7, 0, FRAMES - 640), 128)
        off = pl.multiple_of(order * BLOCK, BLOCK)
        here = (s >> 4) == core

        @pl.when(here)
        def _():
            chunk_s[...] = mel_a[u, :, pl.ds(aligned, 640)]
            x_s[...] = noise_a[u, :, pl.ds(off, BLOCK)]

        @pl.when(jnp.logical_not(here))
        def _():
            chunk_s[...] = mel_b[u, :, pl.ds(aligned, 640)]
            x_s[...] = noise_b[u, :, pl.ds(off, BLOCK)]

        own = lax.broadcasted_iota(jnp.int32, (1, BLOCK), 1) < length - BLOCK * order
        x = jnp.where(own, x_s[...].astype(f32), 0.0)
        noise_out[q] = x.astype(bf16)
        shift = aligned - first
        shift = jnp.where(shift < 0, shift + 640, shift)
        chunk = pltpu.roll(chunk_s[...].astype(f32), shift, 1)[:, :WIN]
        pos = first + lax.broadcasted_iota(jnp.int32, (1, WIN), 1)
        valid = jnp.logical_and(pos >= 0, pos < FRAMES)
        in_span = jnp.logical_and(pos >= span, pos < span + length)
        keep = jnp.logical_and(valid, jnp.logical_not(in_span))
        context = jnp.where(keep, chunk, 0.0)
        context_out[q] = context.astype(bf16)
        valid = valid.astype(f32)
        in_block = jnp.logical_and(pos >= first + CTX, jnp.logical_and(pos < first + CTX + BLOCK, in_span))
        row = lax.broadcasted_iota(jnp.int32, (8, WIN), 0)
        valid_out[q] = jnp.where(row == 0, valid, in_block.astype(f32))
        window(0, context, valid, x, gram, scaled_out.at[q], values_out.at[q], keys_out.at[q], own_out.at[q])
        return carry

    lax.fori_loop(0, n_jobs, job, 0)


def window(n, context, valid, x, gram, scaled_out, values_out, keys_out, own_out):
    side = jnp.zeros((MEL, CTX), f32)
    state = jnp.concatenate([side, x.astype(bf16).astype(f32), side], axis=1)
    flags = (lax.broadcasted_iota(jnp.int32, (16, WIN), 0) >> 1) == n
    win = jnp.concatenate([context, state, flags.astype(f32)], axis=0)
    win = jnp.where(valid > 0.0, win, win[:, CTX : CTX + 1])
    win_b = win.astype(bf16)
    own_out[...] = win_b[:, CTX : CTX + BLOCK]
    gw = jnp.dot(gram[...], win_b, preferred_element_type=f32)
    var = jnp.sum(win * (gw[0:ROWS] + gw[ROWS : 2 * ROWS]), axis=0, keepdims=True)
    scaled = win * lax.rsqrt(jnp.maximum(var, 0.0) + norm_eps)
    scaled_out[...] = scaled[:, CTX : CTX + BLOCK].astype(bf16)
    values_out[...] = (scaled * valid).astype(bf16)
    padded = jnp.concatenate([scaled, jnp.zeros((256 - ROWS, WIN), f32)], axis=0)
    keys_out[...] = padded.T.astype(bf16)[:, :ROWS]


def attend(scaled, values, win_t, valid, weights, work, o_out):
    wq_s, wv_s, wk_s = weights
    k_s, q_s, v_s = work
    q_s[...] = jnp.dot(wq_s[...], scaled[...], preferred_element_type=f32).astype(bf16)
    keys = jnp.dot(win_t[...], wk_s[...], preferred_element_type=f32).astype(bf16)
    for p in range(4):
        k_s[p] = keys[:, 256 * p : 256 * p + 256]
    v_s[...] = jnp.dot(wv_s[...], values[...], preferred_element_type=f32).astype(bf16)
    ones_rows = jnp.broadcast_to(valid, (16, WIN)).astype(bf16)
    zero = jnp.zeros((HEAD_DIM, BLOCK), bf16)
    for g in range(4):
        columns = []
        for j in range(4):
            at = 256 * g + 64 * j
            rows = [q_s[at : at + 64, :] if t == j else zero for t in range(4)]
            columns.append(jnp.concatenate(rows, axis=0))
        sc = jnp.dot(k_s[g], jnp.concatenate(columns, axis=1), preferred_element_type=f32)
        top = jnp.max(sc, axis=0, keepdims=True)
        pr = jnp.exp2(sc - top).astype(bf16)
        for j in range(4):
            at = 256 * g + 64 * j
            lhs = jnp.concatenate([v_s[at : at + 64, :], ones_rows], axis=0)
            ov = jnp.dot(lhs, pr[:, 256 * j : 256 * j + 256], preferred_element_type=f32)
            o_out[at : at + 64, :] = (ov[0:64] / ov[64:65]).astype(bf16)


def velocity_of(wr_s, o, own):
    r = jnp.dot(wr_s[...], o[...], preferred_element_type=f32)
    body = r[0:D]
    var = jnp.sum(body * body, axis=0, keepdims=True) * (1.0 / D)
    return jnp.where(own, r[D : D + MEL] * lax.rsqrt(var + norm_eps), 0.0)


def first_kernel(
    table, valid, scaled, values, keys, own_win,
    wp0, hp1, sp1, hp2, sp2, hp3, sp3,
    wq_s, wv_s, wk_s, o_out,
    k_s, q_s, v_s,
):
    at = 0
    for wp in (wp0, hp1, sp1, hp2, sp2, hp3, sp3):
        width = wp.shape[2]
        lanes = slice(at, at + width)
        pad = jnp.zeros((256 - ROWS, width), f32)
        wq_s[lanes, :] = jnp.concatenate([wp[0].astype(f32), pad], axis=0).T.astype(bf16)[:, :ROWS]
        wv_s[lanes, :] = jnp.concatenate([wp[2].astype(f32), pad], axis=0).T.astype(bf16)[:, :ROWS]
        wk_s[:, lanes] = wp[1]
        at += width

    def job(q, carry):
        o = o_out.at[q]
        o[1024 : 1024 + ROWS, :] = own_win[q]
        attend(
            scaled.at[q], values.at[q], keys.at[q], valid[q, 0:1, :],
            (wq_s, wv_s, wk_s), (k_s, q_s, v_s), o,
        )
        return carry

    lax.fori_loop(0, table[COUNT_AT], job, 0)


def second_kernel(
    table, context, noise, valid, gram, wq_s, wv_s, wk_s, o_in, wa_t, wm,
    wo0, ho1, so1, ho2, so2, ho3, so3,
    tot_out, v0, v1, v2, v3,
    k_s, q_s, v_s, o_s, wr_s, stage, scaled_s, values_s, keys_s,
):
    m = lax.axis_index("mp")
    at = 0
    for wo in (wo0, ho1, so1, ho2, so2, ho3, so3):
        width = wo.shape[1]
        wr_s[0:D, at : at + width] = wo[...]
        at += width
    wr_s[0:D, 1024 : 1024 + ROWS] = wa_t[...]
    wr_s[D : D + MEL, :] = jnp.dot(wm[...], wr_s[0:D, :], preferred_element_type=f32).astype(bf16)
    stage[...] = jnp.zeros(stage.shape, bf16)

    def job(q, carry):
        masks = valid[q]
        own = masks[1:2, CTX : CTX + BLOCK] > 0.0
        usable = masks[0:1, :]
        first = velocity_of(wr_s, o_in.at[q], own)
        x = noise[q].astype(f32) + first * (1.0 / flow_steps)
        window(
            1, context[q].astype(f32), usable, x, gram,
            scaled_s, values_s, keys_s, o_s.at[1024 : 1024 + ROWS, :],
        )
        attend(
            scaled_s, values_s, keys_s, usable, (wq_s, wv_s, wk_s), (k_s, q_s, v_s), o_s
        )
        last = velocity_of(wr_s, o_s, own)
        total = (first + last).astype(bf16)
        tot_out[q, 0:MEL, :] = total[:, 0:128]
        tot_out[q, MEL : 2 * MEL, :] = total[:, 128:256]
        vel = last.astype(bf16)
        stage[0:MEL, :] = vel[:, 0:128]
        stage[MEL : 2 * MEL, :] = vel[:, 128:256]
        for k, out in enumerate((v0, v1, v2, v3)):
            quarter = (m + k) & 3
            out[q] = stage[pl.ds(pl.multiple_of(quarter * PIECE, 16), PIECE), :]
        return carry

    lax.fori_loop(0, table[COUNT_AT], job, 0)


def pack_kernel(table, a0, a1, a2, a3, b0, b1, b2, b3, out, sems):
    def each(act):
        for i, a in enumerate((a0, a1, a2, a3, b0, b1, b2, b3)):
            for q in range(JOBS):
                entry = i * JOBS + q
                worker = table[entry]

                @pl.when(worker >= 0)
                def _():
                    act(pltpu.make_async_copy(a.at[q], out.at[worker], sems.at[entry]))

    each(lambda copy: copy.start())
    each(lambda copy: copy.wait())


def select_kernel(table, got, out, sems):
    copies = [
        pltpu.make_async_copy(got.at[table[OWNER_AT + j]], out.at[j], sems.at[j])
        for j in range(WORK_DEV)
    ]
    for copy in copies:
        copy.start()
    for copy in copies:
        copy.wait()


def span_kernel(table, a0, a1, a2, a3, b0, b1, b2, b3, out):
    out[...] = jnp.zeros(out.shape, f32)
    for i, a in enumerate((a0, a1, a2, a3, b0, b1, b2, b3)):
        for q in range(JOBS):
            s = table[SLOT_AT + i * JOBS + q]

            @pl.when(s >= 0)
            def _():
                block = a[q].astype(f32)
                off = (s & 3) * BLOCK
                out[s >> 2, :, pl.ds(pl.multiple_of(off, 128), 128)] = block[0:MEL]
                out[s >> 2, :, pl.ds(pl.multiple_of(off + 128, 128), 128)] = block[MEL : 2 * MEL]


def final_kernel(b0, b1, b2, b3, out, stage):
    m = lax.axis_index("mp")
    for k, b in enumerate((b0, b1, b2, b3)):
        quarter = (m - k) & 3
        at = pl.multiple_of(quarter * PIECE, 16)
        for j in range(WORK_DEV):
            stage[j, pl.ds(at, PIECE), :] = b[j]
    for j in range(WORK_DEV):
        out[j, :, 0:128] = stage[j, 0:MEL, :].astype(f32)
        out[j, :, 128:256] = stage[j, MEL : 2 * MEL, :].astype(f32)


def call(kernel, outs, kinds, args, scratch=(), out_kinds=None, limit=24):
    spaces = {"s": SMEM, "v": VMEM, "h": pl.ANY}
    spec = lambda kind: pl.BlockSpec(memory_space=spaces[kind])
    many = isinstance(outs, tuple)
    out_kinds = out_kinds or "v" * (len(outs) if many else 1)
    out_specs = tuple(spec(k) for k in out_kinds)
    return pl.pallas_call(
        kernel,
        out_shape=outs,
        in_specs=[spec(k) for k in kinds],
        out_specs=out_specs if many else out_specs[0],
        scratch_shapes=list(scratch),
        compiler_params=pltpu.CompilerParams(vmem_limit_bytes=limit * 1024 * 1024),
    )(*args)


def shape(dims, dtype):
    return jax.ShapeDtypeStruct(dims, dtype)


def to_next(value, k):
    return lax.ppermute(value, "mp", [(i, (i + k) % N_MP) for i in range(N_MP)])


def to_other(value):
    size = lax.axis_size("dp")
    return lax.ppermute(value, "dp", [(i, i ^ 1) for i in range(size)])


def gathered(value):
    return [value] + [to_next(value, k) for k in range(1, N_MP)]


def after(value, *others):
    return lax.optimization_barrier((value, *others))[0]


def run_plan(plan, audio, gram):
    return call(
        plan_kernel,
        (
            shape((TABLE,), jnp.int32),
            shape((JOBS, MEL, WIN), bf16),
            shape((JOBS, MEL, BLOCK), bf16),
            shape((JOBS, 8, WIN), f32),
            shape((JOBS, ROWS, BLOCK), bf16),
            shape((JOBS, ROWS, WIN), bf16),
            shape((JOBS, WIN, ROWS), bf16),
            shape((JOBS, ROWS, BLOCK), bf16),
        ),
        "sss" + "v" * 5,
        (*plan, *audio, gram),
        scratch=[VMEM((MEL, 640), bf16), VMEM((MEL, BLOCK), bf16)],
        out_kinds="s" + "v" * 7,
    )


def run_first(table, windows, wp):
    return call(
        first_kernel,
        (
            shape((D, ROWS), bf16),
            shape((D, ROWS), bf16),
            shape((ROWS, D), bf16),
            shape((JOBS, D + ROWS, BLOCK), bf16),
        ),
        "s" + "v" * 12,
        (table, *windows, *wp),
        scratch=work_shapes(),
        limit=MAIN_LIMIT,
    )


def work_shapes():
    return [VMEM((4, WIN, 256), bf16), VMEM((D, BLOCK), bf16), VMEM((D, WIN), bf16)]


def run_second(table, context, noise, valid, gram, first, wa_t, wm, wo):
    return call(
        second_kernel,
        (shape((JOBS, 2 * MEL, 128), bf16),) + (shape((JOBS, PIECE, 128), bf16),) * 4,
        "s" + "v" * 17,
        (table, context, noise, valid, gram, *first, wa_t, wm, *wo),
        scratch=work_shapes()
        + [
            VMEM((D + ROWS, BLOCK), bf16),
            VMEM((D + MEL, D + ROWS), bf16),
            VMEM((4 * PIECE, 128), bf16),
            VMEM((ROWS, BLOCK), bf16),
            VMEM((ROWS, WIN), bf16),
            VMEM((WIN, ROWS), bf16),
        ],
        limit=MAIN_LIMIT,
    )


def shards(
    mel_audio, start_noise, span_start, span_length, block_route,
    w_input, attn_gain, w_qkv, w_out, final_gain, w_mel,
):
    e_rows = jnp.asarray(time_rows())
    plan = (block_route, span_start, span_length)
    w3 = jnp.transpose(w_qkv, (1, 0, 2))
    whole, half = call(
        fold_kernel,
        (shape((3, ROWS, 256), bf16), shape((3, ROWS, 128), bf16)),
        "vvvv",
        (w_input, e_rows, attn_gain.reshape(1, D), w3),
    )
    halves = gathered(half)[1:]
    audio = (mel_audio, to_other(mel_audio), start_noise, to_other(start_noise))
    wa_t, gram, wo_t, wo_half, wm = call(
        prep_kernel,
        (
            shape((D, ROWS), bf16),
            shape((2 * ROWS, ROWS), bf16),
            shape((D, 256), bf16),
            shape((D, 128), bf16),
            shape((MEL, D), bf16),
        ),
        "vvvvv",
        (w_input, e_rows, after(w_out, half), w_mel, final_gain.reshape(1, D)),
    )
    out_halves = gathered(wo_half)[1:]
    table, context, noise, valid, scaled, values, keys, own_win = run_plan(plan, audio, gram)
    wp = [whole]
    for h in halves:
        wp += [h, to_other(h)]
    first = run_first(table, (valid, scaled, values, keys, own_win), wp)
    out_halves = lax.optimization_barrier((*out_halves, first[3]))
    first = (*first[:3], out_halves[-1])
    wo = [wo_t]
    for h in out_halves[:-1]:
        wo += [h, to_other(h)]
    tot, v0, v1, v2, v3 = run_second(table, context, noise, valid, gram, first, wa_t, wm, wo)
    pieces = [v0] + [to_next(v, k) for k, v in ((1, v1), (2, v2), (3, v3))]
    pieces += [to_other(v) for v in pieces]
    packed = call(
        pack_kernel,
        shape((32, PIECE, 128), bf16),
        "s" + "h" * 8,
        (table, *pieces),
        scratch=[pltpu.SemaphoreType.DMA((8 * JOBS,))],
        out_kinds="h",
    )
    got = lax.all_to_all(packed, "dp", 0, 0, tiled=True)
    totals = gathered(after(tot, packed))
    totals += [to_other(t) for t in totals]
    infilled = call(
        span_kernel, shape((UTT_DEV, MEL, SPAN_MAX), f32), "s" + "v" * 8, (table, *totals)
    )
    chosen = call(
        select_kernel,
        shape((WORK_DEV, PIECE, 128), bf16),
        "sh",
        (table, got),
        scratch=[pltpu.SemaphoreType.DMA((WORK_DEV,))],
        out_kinds="h",
    )
    parts = gathered(chosen)
    velocity = call(
        final_kernel,
        shape((WORK_DEV, MEL, BLOCK), f32),
        "vvvv",
        tuple(parts),
        scratch=[VMEM((WORK_DEV, 4 * PIECE, 128), bf16)],
    )
    return (infilled, velocity)


def solution(mesh):
    return jax.shard_map(
        shards,
        mesh=mesh,
        in_specs=(
            P("dp", None, None),
            P("dp", None, None),
            P(),
            P(),
            P(),
            P(),
            P(),
            P(None, None, "mp"),
            P("mp", None),
            P(),
            P(),
        ),
        out_specs=(P("dp", None, None), P("dp", None, None)),
        check_vma=False,
    )
```

time: 129 us -> 102 us (0.79)
  starting transfers between devices: 64 us -> 36.1 us
  Pallas kernels: 40.5 us -> 45.9 us
  waiting for transfers between devices: 15.7 us -> 12.2 us
  other arithmetic: 1.35 us -> 0 us
    all_to_all x1, starting transfers between devices: 18.5 us -> 3.79 us  [shards(): got = lax.all_to_all(packed, 'dp', 0, 0, tiled=True)]
    ppermute x16, starting transfers between devices: 25.4 us -> 12 us  [to_other(): return lax.ppermute(value, 'dp', [(i, i ^ 1) for i in range(size)])]
    all_to_all x1, waiting for transfers between devices: 8.33 us -> 0.01 us  [shards(): got = lax.all_to_all(packed, 'dp', 0, 0, tiled=True)]
    pallas_call x8 -> x9, Pallas kernels: 40.5 us -> 45.9 us  [call(): pl.pallas_call(kernel, out_shape=outs, in_specs=[spec(k) for k in kinds],...]
    ppermute x15, waiting for transfers between devices: 6.89 us -> 9.83 us  [to_next(): return lax.ppermute(value, 'mp', [(i, (i + k) % N_MP) for i in range(N_MP)])]
    ppermute x16, waiting for transfers between devices: 0.51 us -> 2.41 us  [to_other(): return lax.ppermute(value, 'dp', [(i, i ^ 1) for i in range(size)])]
    unnamed x70 -> x24, local copies, waits for them, and re-layouts: 6.6 us -> 5.88 us
  transfers between devices with their start and end apart: 32 -> 32, of which waited for: 6 -> 11; matrix products, arithmetic and copies ran while one was open for 1% -> 0% of each run, Pallas kernels for 19% -> 22%
where the time goes in v2:
time: 102 us; the launch traced here: 101 us
  Pallas kernels  45.9 us (45%)
  starting transfers between devices  36.1 us (35%)
  waiting for transfers between devices  12.2 us (12%)
  local copies, waits for them, and re-layouts  5.88 us (6%)
    pallas_call x9, Pallas kernels, call(): pl.pallas_call(kernel, out_shape=outs, in_specs=[spec(k) for k in kinds],...  45.9 us
    ppermute x15, starting transfers between devices, to_next(): return lax.ppermute(value, 'mp', [(i, (i + k) % N_MP) for i in range(N_MP)])  20.3 us
    ppermute x16, starting transfers between devices, to_other(): return lax.ppermute(value, 'dp', [(i, i ^ 1) for i in range(size)])  12 us
    ppermute x15, waiting for transfers between devices, to_next(): return lax.ppermute(value, 'mp', [(i, (i + k) % N_MP) for i in range(N_MP)])  9.83 us
    unnamed x24, local copies, waits for them, and re-layouts  5.88 us
    all_to_all x1, starting transfers between devices, shards(): got = lax.all_to_all(packed, 'dp', 0, 0, tiled=True)  3.79 us
    ppermute x16, waiting for transfers between devices, to_other(): return lax.ppermute(value, 'dp', [(i, i ^ 1) for i in range(size)])  2.41 us
  transfers between devices with their start and end apart: 32, of which 11 were waited for; matrix products, arithmetic and copies ran while one was open for 0% of the time, Pallas kernels for 22%

profile of v2, /device:TPU:1, one launch (start us, length us, event | category | flops | bytes accessed | tf_op | source)
XLA Modules:
  0.0 100.9 jit_solution(10351552866569332504)
XLA Ops:
  0.6 1.5 %collective-permute-start = (bf16[4,80,2048]{2,1,0:T(8,128)(2,1)}, bf16[4,80,2048]{2,1,0:T(8,128)(2,1)S(1)}, u32[]{:S(2)}, u32[]{:S(2)}) collective-permute-start(bf16[4,80,2048]{2,1,0:T(8,128)(2,1)} %mel_a.1), channel_id=1, source_target_pairs={{0,4},{4,0},{8,12},{12,8},{16,20},{20,16},{24,28},{28,24},{32,36},... | collective-permute-start | bytes 3932168 | tf_op jit(solution)/shard_map/ppermute | solution.py:387
  2.2 1.4 %copy-done = bf16[1024,3,256]{2,0,1:T(8,128)(2,1)S(1)} copy-done((bf16[1024,3,256]{2,0,1:T(8,128)(2,1)S(1)}, bf16[1024,3,256]{2,0,1:T(8,128)(2,1)}, u32[]{:S(2)}) %copy-start) | copy-done | bytes 1572888
  3.6 1.0 copy-done.2
  4.6 0.8 copy-done.5
  6.8 1.8 %collective-permute-start.2 = (bf16[3,176,128]{2,1,0:T(8,128)(2,1)S(1)}, bf16[3,176,128]{2,1,0:T(8,128)(2,1)S(1)}, u32[]{:S(2)}, u32[]{:S(2)}) collective-permute-start(bf16[3,176,128]{2,1,0:T(8,128)(2,1)S(1)} %get-tuple-element.32), channel_id=1, source_target_pairs={{0,1},{1,2},{2,3},{3,0},{4,5},{5,6},{6,7},{7,4},{8,9},{9,10},{10,1... | collective-permute-start | bytes 405512 | tf_op jit(solution)/shard_map/ppermute | solution.py:382
  8.6 3.3 %collective-permute-start.4 = (bf16[3,176,128]{2,1,0:T(8,128)(2,1)S(1)}, bf16[3,176,128]{2,1,0:T(8,128)(2,1)S(1)}, u32[]{:S(2)}, u32[]{:S(2)}) collective-permute-start(bf16[3,176,128]{2,1,0:T(8,128)(2,1)S(1)} %get-tuple-element.32), channel_id=1, source_target_pairs={{0,2},{1,3},{2,0},{3,1},{4,6},{5,7},{6,4},{7,5},{8,10},{9,11},{10,... | collective-permute-start | bytes 405512 | tf_op jit(solution)/shard_map/ppermute | solution.py:382
  11.8 0.7 collective-permute-start.6
  12.6 1.7 %collective-permute-done.2.hp1 = bf16[3,176,128]{2,1,0:T(8,128)(2,1)S(1)} collective-permute-done((bf16[3,176,128]{2,1,0:T(8,128)(2,1)S(1)}, bf16[3,176,128]{2,1,0:T(8,128)(2,1)S(1)}, u32[]{:S(2)}, u32[]{:S(2)}) %collective-permute-start.2) | collective-permute-done | bytes 135200 | tf_op jit(solution)/shard_map/ppermute | solution.py:382
  14.3 0.9 collective-permute-start.3
  15.2 1.0 %copy-done.4 = bf16[256,1024]{1,0:T(8,128)(2,1)S(1)} copy-done((bf16[256,1024]{1,0:T(8,128)(2,1)S(1)}, bf16[256,1024]{1,0:T(8,128)(2,1)}, u32[]{:S(2)}) %copy-start.4) | copy-done | bytes 524312
  16.3 0.9 copy-done.6
  18.0 3.4 %collective-permute-start.9 = (bf16[1024,128]{1,0:T(8,128)(2,1)S(1)}, bf16[1024,128]{1,0:T(8,128)(2,1)S(1)}, u32[]{:S(2)}, u32[]{:S(2)}) collective-permute-start(bf16[1024,128]{1,0:T(8,128)(2,1)S(1)} %get-tuple-element.47), channel_id=1, source_target_pairs={{0,2},{1,3},{2,0},{3,1},{4,6},{5,7},{6,4},{7,5},{8,10},{9,11},{10,... | collective-permute-start | bytes 786440 | tf_op jit(solution)/shard_map/ppermute | solution.py:382
  21.8 1.4 %collective-permute-start.5 = (bf16[3,176,128]{2,1,0:T(8,128)(2,1)S(1)}, bf16[3,176,128]{2,1,0:T(8,128)(2,1)S(1)}, u32[]{:S(2)}, u32[]{:S(2)}) collective-permute-start(bf16[3,176,128]{2,1,0:T(8,128)(2,1)S(1)} %collective-permute-done.4.hp2), channel_id=1, source_target_pairs={{0,4},{4,0},{8,12},{12,8},{16,20},{20,16},{24,28},{28,24},{32,36},... | collective-permute-start | bytes 405512 | tf_op jit(solution)/shard_map/ppermute | solution.py:387
  23.3 6.7 %shard_map.133 = (s32[80]{0:T(128)S(1)}, bf16[4,80,512]{2,1,0:T(8,128)(2,1)S(1)}, bf16[4,80,256]{2,1,0:T(8,128)(2,1)S(1)}, f32[4,8,512]{2,1,0:T(8,128)S(1)}, bf1...) custom-call(s32[512]{0:T(512)S(1)} %copy-done.9, ...), custom_call_target="tpu_custom_call" | custom-call | tf_op jit(solution)/shard_map/pallas_call | solution.py:367
  30.1 11.6 %shard_map.134 = (bf16[1024,176]{1,0:T(8,128)(2,1)S(1)}, bf16[1024,176]{1,0:T(8,128)(2,1)S(1)}, bf16[176,1024]{1,0:T(8,128)(2,1)S(1)}, bf16[4,1200,256]{2,1,0:T(8,128)(2,1)S(1)}) custom-call(s32[80]{0:T(128)S(1)} %get-tuple-element.35.table, f32[4,8,512]{2,1,0:T(8,128)S(1)} %get-tuple-element.38.valid, bf16[4,176,256]{2,1,0:T(8,128)(2,1)S(1)} %get-tuple-element.39.scaled, ...), custom_call_target="tpu_custom_call" | custom-call | tf_op jit(solution)/shard_map/pallas_call | solution.py:367
  44.1 21.3 %shard_map.135 = (bf16[4,160,128]{2,1,0:T(8,128)(2,1)S(1)}, bf16[4,48,128]{2,1,0:T(8,128)(2,1)S(1)}, bf16[4,48,128]{2,1,0:T(8,128)(2,1)S(1)}, bf16[4,48,128]{2,1,0:T(8,128)(2,1)S(1)}, bf16[4,48,128]{2,1,0:T(8,128)(2,1)S(1)}) custom-call(s32[80]{0:T(128)S(1)} %get-tuple-element.35.table, bf16[4,80,512]{2,1,0:T(8,128)(2,1)S(1)} %get-tuple-element.36.context, ...), custom_call_target="tpu_custom_call" | custom-call | tf_op jit(solution)/shard_map/pallas_call | solution.py:367
  66.1 2.5 %collective-permute-start.16 = (bf16[4,48,128]{2,1,0:T(8,128)(2,1)S(1)}, bf16[4,48,128]{2,1,0:T(8,128)(2,1)S(1)}, u32[]{:S(2)}, u32[]{:S(2)}) collective-permute-start(bf16[4,48,128]{2,1,0:T(8,128)(2,1)S(1)} %get-tuple-element.60), channel_id=1, source_target_pairs={{0,3},{1,0},{2,1},{3,2},{4,7},{5,4},{6,5},{7,6},{8,11},{9,8},{10,9... | collective-permute-start | bytes 147464 | tf_op jit(solution)/shard_map/ppermute | solution.py:382
  68.5 2.2 %collective-permute-start.17 = (bf16[4,48,128]{2,1,0:T(8,128)(2,1)S(1)}, bf16[4,48,128]{2,1,0:T(8,128)(2,1)S(1)}, u32[]{:S(2)}, u32[]{:S(2)}) collective-permute-start(bf16[4,48,128]{2,1,0:T(8,128)(2,1)S(1)} %get-tuple-element.57.a0), channel_id=1, source_target_pairs={{0,4},{4,0},{8,12},{12,8},{16,20},{20,16},{24,28},{28,24},{32,36},... | collective-permute-start | bytes 147464 | tf_op jit(solution)/shard_map/ppermute | solution.py:387
  70.7 1.0 collective-permute-start.18
  73.5 1.5 %shard_map.136 = bf16[32,48,128]{2,1,0:T(8,128)(2,1)} custom-call(s32[80]{0:T(128)S(1)} %get-tuple-element.35.table, bf16[4,48,128]{2,1,0:T(8,128)(2,1)S(1)} %get-tuple-element.57.a0, bf16[4,48,128]{2,1,0:T(8,128)(2,1)S(1)} %collective-permute-done.14.a1, bf16[4,48,128]{2,1,0:T(8,128)(2,1)S(1)} %collective-permute-done.15.a2, ...), custom_call_target="tpu_custom_call" | custom-call | tf_op jit(solution)/shard_map/pallas_call | solution.py:367
  75.0 3.8 %all-to-all-start = ((bf16[32,48,128]{2,1,0:T(8,128)(2,1)}), bf16[32,48,128]{2,1,0:T(8,128)(2,1)S(1)}, u32[]{:S(2)}, u32[]{:S(2)}) async-start(bf16[32,48,128]{2,1,0:T(8,128)(2,1)} %shard_map.136), calls=%async_computation | async-start | bytes 786432 | tf_op jit(solution)/shard_map/all_to_all | solution.py:506
  78.8 1.4 %collective-permute-start.21 = (bf16[4,160,128]{2,1,0:T(8,128)(2,1)S(1)}, bf16[4,160,128]{2,1,0:T(8,128)(2,1)S(1)}, u32[]{:S(2)}, u32[]{:S(2)}) collective-permute-start(bf16[4,160,128]{2,1,0:T(8,128)(2,1)S(1)} %get-tuple-element.61.a0), channel_id=1, source_target_pairs={{0,1},{1,2},{2,3},{3,0},{4,5},{5,6},{6,7},{7,4},{8,9},{9,10},{10,1... | collective-permute-start | bytes 491528 | tf_op jit(solution)/shard_map/ppermute | solution.py:382
  80.3 3.0 %collective-permute-start.22 = (bf16[4,160,128]{2,1,0:T(8,128)(2,1)S(1)}, bf16[4,160,128]{2,1,0:T(8,128)(2,1)S(1)}, u32[]{:S(2)}, u32[]{:S(2)}) collective-permute-start(bf16[4,160,128]{2,1,0:T(8,128)(2,1)S(1)} %get-tuple-element.61.a0), channel_id=1, source_target_pairs={{0,2},{1,3},{2,0},{3,1},{4,6},{5,7},{6,4},{7,5},{8,10},{9,11},{10,... | collective-permute-start | bytes 491528 | tf_op jit(solution)/shard_map/ppermute | solution.py:382
  83.3 0.9 collective-permute-start.24
  84.2 2.2 %collective-permute-done.21.a1 = bf16[4,160,128]{2,1,0:T(8,128)(2,1)S(1)} collective-permute-done((bf16[4,160,128]{2,1,0:T(8,128)(2,1)S(1)}, bf16[4,160,128]{2,1,0:T(8,128)(2,1)S(1)}, u32[]{:S(2)}, u32[]{:S(2)}) %collective-permute-start.21) | collective-permute-done | bytes 163872 | tf_op jit(solution)/shard_map/ppermute | solution.py:382
  86.4 0.9 collective-permute-start.25
  87.3 3.5 %collective-permute-done.22.a2 = bf16[4,160,128]{2,1,0:T(8,128)(2,1)S(1)} collective-permute-done((bf16[4,160,128]{2,1,0:T(8,128)(2,1)S(1)}, bf16[4,160,128]{2,1,0:T(8,128)(2,1)S(1)}, u32[]{:S(2)}, u32[]{:S(2)}) %collective-permute-start.22) | collective-permute-done | bytes 163872 | tf_op jit(solution)/shard_map/ppermute | solution.py:382
  90.8 1.2 %collective-permute-start.26 = (bf16[4,160,128]{2,1,0:T(8,128)(2,1)S(1)}, bf16[4,160,128]{2,1,0:T(8,128)(2,1)S(1)}, u32[]{:S(2)}, u32[]{:S(2)}) collective-permute-start(bf16[4,160,128]{2,1,0:T(8,128)(2,1)S(1)} %collective-permute-done.22.a2), channel_id=1, source_target_pairs={{0,4},{4,0},{8,12},{12,8},{16,20},{20,16},{24,28},{28,24},{32,36},... | collective-permute-start | bytes 491528 | tf_op jit(solution)/shard_map/ppermute | solution.py:387
  93.0 2.8 %collective-permute-start.29 = (bf16[6,48,128]{2,1,0:T(8,128)(2,1)S(1)}, bf16[6,48,128]{2,1,0:T(8,128)(2,1)S(1)}, u32[]{:S(2)}, u32[]{:S(2)}) collective-permute-start(bf16[6,48,128]{2,1,0:T(8,128)(2,1)S(1)} %shard_map.138.b0), channel_id=1, source_target_pairs={{0,2},{1,3},{2,0},{3,1},{4,6},{5,7},{6,4},{7,5},{8,10},{9,11},{10,... | collective-permute-start | bytes 221192 | tf_op jit(solution)/shard_map/ppermute | solution.py:382
  95.8 2.0 %shard_map.137 = f32[4,80,1024]{2,1,0:T(8,128)} custom-call(s32[80]{0:T(128)S(1)} %get-tuple-element.35.table, bf16[4,160,128]{2,1,0:T(8,128)(2,1)S(1)} %get-tuple-element.61.a0, bf16[4,160,128]{2,1,0:T(8,128)(2,1)S(1)} %collective-permute-done.21.a1, bf16[4,160,128]{2,1,0:T(8,128)(2,1)S(1)} %collective-permute-done.22.a2, ...), custom_call_target="tpu_custom_call" | custom-call | tf_op jit(solution)/shard_map/pallas_call | solution.py:367
  97.8 2.0 %collective-permute-done.29.b2 = bf16[6,48,128]{2,1,0:T(8,128)(2,1)S(1)} collective-permute-done((bf16[6,48,128]{2,1,0:T(8,128)(2,1)S(1)}, bf16[6,48,128]{2,1,0:T(8,128)(2,1)S(1)}, u32[]{:S(2)}, u32[]{:S(2)}) %collective-permute-start.29) | collective-permute-done | bytes 73760 | tf_op jit(solution)/shard_map/ppermute | solution.py:382
  100.1 0.8 shard_map.139
  (65 shorter events, 8.9 us)
Async XLA Ops:
  0.6 22.6 %collective-permute-start = (bf16[4,80,2048]{2,1,0:T(8,128)(2,1)}, bf16[4,80,2048]{2,1,0:T(8,128)(2,1)S(1)}, u32[]{:S(2)}, u32[]{:S(2)}) collective-permute-start(bf16[4,80,2048]{2,1,0:T(8,128)(2,1)} %mel_a.1), channel_id=1, source_target_pairs={{0,4},{4,0},{8,12},{12,8},{16,20},{20,16},{24,28},{28,24},{32,36},... | collective-permute-start | bytes 3932168 | tf_op jit(solution)/shard_map/ppermute | solution.py:387
  2.1 19.6 %collective-permute-start.1 = (bf16[4,80,1024]{2,1,0:T(8,128)(2,1)}, bf16[4,80,1024]{2,1,0:T(8,128)(2,1)S(1)}, u32[]{:S(2)}, u32[]{:S(2)}) collective-permute-start(bf16[4,80,1024]{2,1,0:T(8,128)(2,1)} %noise_a.1), channel_id=1, source_target_pairs={{0,4},{4,0},{8,12},{12,8},{16,20},{20,16},{24,28},{28,24},{32,36},... | collective-permute-start | bytes 1966088 | tf_op jit(solution)/shard_map/ppermute | solution.py:387
  6.8 7.5 %collective-permute-start.2 = (bf16[3,176,128]{2,1,0:T(8,128)(2,1)S(1)}, bf16[3,176,128]{2,1,0:T(8,128)(2,1)S(1)}, u32[]{:S(2)}, u32[]{:S(2)}) collective-permute-start(bf16[3,176,128]{2,1,0:T(8,128)(2,1)S(1)} %get-tuple-element.32), channel_id=1, source_target_pairs={{0,1},{1,2},{2,3},{3,0},{4,5},{5,6},{6,7},{7,4},{8,9},{9,10},{10,1... | collective-permute-start | bytes 405512 | tf_op jit(solution)/shard_map/ppermute | solution.py:382
  8.6 9.4 %collective-permute-start.4 = (bf16[3,176,128]{2,1,0:T(8,128)(2,1)S(1)}, bf16[3,176,128]{2,1,0:T(8,128)(2,1)S(1)}, u32[]{:S(2)}, u32[]{:S(2)}) collective-permute-start(bf16[3,176,128]{2,1,0:T(8,128)(2,1)S(1)} %get-tuple-element.32), channel_id=1, source_target_pairs={{0,2},{1,3},{2,0},{3,1},{4,6},{5,7},{6,4},{7,5},{8,10},{9,11},{10,... | collective-permute-start | bytes 405512 | tf_op jit(solution)/shard_map/ppermute | solution.py:382
  11.8 6.2 %collective-permute-start.6 = (bf16[3,176,128]{2,1,0:T(8,128)(2,1)S(1)}, bf16[3,176,128]{2,1,0:T(8,128)(2,1)S(1)}, u32[]{:S(2)}, u32[]{:S(2)}) collective-permute-start(bf16[3,176,128]{2,1,0:T(8,128)(2,1)S(1)} %get-tuple-element.32), channel_id=1, source_target_pairs={{0,3},{1,0},{2,1},{3,2},{4,7},{5,4},{6,5},{7,6},{8,11},{9,8},{10,9... | collective-permute-start | bytes 405512 | tf_op jit(solution)/shard_map/ppermute | solution.py:382
  14.3 7.2 %collective-permute-start.3 = (bf16[3,176,128]{2,1,0:T(8,128)(2,1)S(1)}, bf16[3,176,128]{2,1,0:T(8,128)(2,1)S(1)}, u32[]{:S(2)}, u32[]{:S(2)}) collective-permute-start(bf16[3,176,128]{2,1,0:T(8,128)(2,1)S(1)} %collective-permute-done.2.hp1), channel_id=1, source_target_pairs={{0,4},{4,0},{8,12},{12,8},{16,20},{20,16},{24,28},{28,24},{32,36},... | collective-permute-start | bytes 405512 | tf_op jit(solution)/shard_map/ppermute | solution.py:387
  18.0 23.6 %collective-permute-start.8 = (bf16[1024,128]{1,0:T(8,128)(2,1)S(1)}, bf16[1024,128]{1,0:T(8,128)(2,1)S(1)}, u32[]{:S(2)}, u32[]{:S(2)}) collective-permute-start(bf16[1024,128]{1,0:T(8,128)(2,1)S(1)} %get-tuple-element.47), channel_id=1, source_target_pairs={{0,1},{1,2},{2,3},{3,0},{4,5},{5,6},{6,7},{7,4},{8,9},{9,10},{10,1... | collective-permute-start | bytes 786440 | tf_op jit(solution)/shard_map/ppermute | solution.py:382
  18.0 23.6 %collective-permute-start.9 = (bf16[1024,128]{1,0:T(8,128)(2,1)S(1)}, bf16[1024,128]{1,0:T(8,128)(2,1)S(1)}, u32[]{:S(2)}, u32[]{:S(2)}) collective-permute-start(bf16[1024,128]{1,0:T(8,128)(2,1)S(1)} %get-tuple-element.47), channel_id=1, source_target_pairs={{0,2},{1,3},{2,0},{3,1},{4,6},{5,7},{6,4},{7,5},{8,10},{9,11},{10,... | collective-permute-start | bytes 786440 | tf_op jit(solution)/shard_map/ppermute | solution.py:382
  21.5 20.2 %collective-permute-start.10 = (bf16[1024,128]{1,0:T(8,128)(2,1)S(1)}, bf16[1024,128]{1,0:T(8,128)(2,1)S(1)}, u32[]{:S(2)}, u32[]{:S(2)}) collective-permute-start(bf16[1024,128]{1,0:T(8,128)(2,1)S(1)} %get-tuple-element.47), channel_id=1, source_target_pairs={{0,3},{1,0},{2,1},{3,2},{4,7},{5,4},{6,5},{7,6},{8,11},{9,8},{10,9... | collective-permute-start | bytes 786440 | tf_op jit(solution)/shard_map/ppermute | solution.py:382
  21.8 8.3 %collective-permute-start.5 = (bf16[3,176,128]{2,1,0:T(8,128)(2,1)S(1)}, bf16[3,176,128]{2,1,0:T(8,128)(2,1)S(1)}, u32[]{:S(2)}, u32[]{:S(2)}) collective-permute-start(bf16[3,176,128]{2,1,0:T(8,128)(2,1)S(1)} %collective-permute-done.4.hp2), channel_id=1, source_target_pairs={{0,4},{4,0},{8,12},{12,8},{16,20},{20,16},{24,28},{28,24},{32,36},... | collective-permute-start | bytes 405512 | tf_op jit(solution)/shard_map/ppermute | solution.py:387
  23.2 6.9 %collective-permute-start.7 = (bf16[3,176,128]{2,1,0:T(8,128)(2,1)S(1)}, bf16[3,176,128]{2,1,0:T(8,128)(2,1)S(1)}, u32[]{:S(2)}, u32[]{:S(2)}) collective-permute-start(bf16[3,176,128]{2,1,0:T(8,128)(2,1)S(1)} %collective-permute-done.6.hp3), channel_id=1, source_target_pairs={{0,4},{4,0},{8,12},{12,8},{16,20},{20,16},{24,28},{28,24},{32,36},... | collective-permute-start | bytes 405512 | tf_op jit(solution)/shard_map/ppermute | solution.py:387
  41.7 1.7 %collective-permute-start.11 = (bf16[1024,128]{1,0:T(8,128)(2,1)S(1)}, bf16[1024,128]{1,0:T(8,128)(2,1)S(1)}, u32[]{:S(2)}, u32[]{:S(2)}) collective-permute-start(bf16[1024,128]{1,0:T(8,128)(2,1)S(1)} %collective-permute-done.8.ho1), channel_id=1, source_target_pairs={{0,4},{4,0},{8,12},{12,8},{16,20},{20,16},{24,28},{28,24},{32,36},... | collective-permute-start | bytes 786440 | tf_op jit(solution)/shard_map/ppermute | solution.py:387
  42.2 1.5 %collective-permute-start.12 = (bf16[1024,128]{1,0:T(8,128)(2,1)S(1)}, bf16[1024,128]{1,0:T(8,128)(2,1)S(1)}, u32[]{:S(2)}, u32[]{:S(2)}) collective-permute-start(bf16[1024,128]{1,0:T(8,128)(2,1)S(1)} %collective-permute-done.9.ho2), channel_id=1, source_target_pairs={{0,4},{4,0},{8,12},{12,8},{16,20},{20,16},{24,28},{28,24},{32,36},... | collective-permute-start | bytes 786440 | tf_op jit(solution)/shard_map/ppermute | solution.py:387
  42.3 1.8 %collective-permute-start.13 = (bf16[1024,128]{1,0:T(8,128)(2,1)S(1)}, bf16[1024,128]{1,0:T(8,128)(2,1)S(1)}, u32[]{:S(2)}, u32[]{:S(2)}) collective-permute-start(bf16[1024,128]{1,0:T(8,128)(2,1)S(1)} %collective-permute-done.10.ho3), channel_id=1, source_target_pairs={{0,4},{4,0},{8,12},{12,8},{16,20},{20,16},{24,28},{28,24},{32,36},... | collective-permute-start | bytes 786440 | tf_op jit(solution)/shard_map/ppermute | solution.py:387
  65.4 5.3 %collective-permute-start.14 = (bf16[4,48,128]{2,1,0:T(8,128)(2,1)S(1)}, bf16[4,48,128]{2,1,0:T(8,128)(2,1)S(1)}, u32[]{:S(2)}, u32[]{:S(2)}) collective-permute-start(bf16[4,48,128]{2,1,0:T(8,128)(2,1)S(1)} %get-tuple-element.58), channel_id=1, source_target_pairs={{0,1},{1,2},{2,3},{3,0},{4,5},{5,6},{6,7},{7,4},{8,9},{9,10},{10,1... | collective-permute-start | bytes 147464 | tf_op jit(solution)/shard_map/ppermute | solution.py:382
  66.1 5.6 %collective-permute-start.15 = (bf16[4,48,128]{2,1,0:T(8,128)(2,1)S(1)}, bf16[4,48,128]{2,1,0:T(8,128)(2,1)S(1)}, u32[]{:S(2)}, u32[]{:S(2)}) collective-permute-start(bf16[4,48,128]{2,1,0:T(8,128)(2,1)S(1)} %get-tuple-element.59), channel_id=1, source_target_pairs={{0,2},{1,3},{2,0},{3,1},{4,6},{5,7},{6,4},{7,5},{8,10},{9,11},{10,... | collective-permute-start | bytes 147464 | tf_op jit(solution)/shard_map/ppermute | solution.py:382
  66.1 6.2 %collective-permute-start.16 = (bf16[4,48,128]{2,1,0:T(8,128)(2,1)S(1)}, bf16[4,48,128]{2,1,0:T(8,128)(2,1)S(1)}, u32[]{:S(2)}, u32[]{:S(2)}) collective-permute-start(bf16[4,48,128]{2,1,0:T(8,128)(2,1)S(1)} %get-tuple-element.60), channel_id=1, source_target_pairs={{0,3},{1,0},{2,1},{3,2},{4,7},{5,4},{6,5},{7,6},{8,11},{9,8},{10,9... | collective-permute-start | bytes 147464 | tf_op jit(solution)/shard_map/ppermute | solution.py:382
  68.5 4.0 %collective-permute-start.17 = (bf16[4,48,128]{2,1,0:T(8,128)(2,1)S(1)}, bf16[4,48,128]{2,1,0:T(8,128)(2,1)S(1)}, u32[]{:S(2)}, u32[]{:S(2)}) collective-permute-start(bf16[4,48,128]{2,1,0:T(8,128)(2,1)S(1)} %get-tuple-element.57.a0), channel_id=1, source_target_pairs={{0,4},{4,0},{8,12},{12,8},{16,20},{20,16},{24,28},{28,24},{32,36},... | collective-permute-start | bytes 147464 | tf_op jit(solution)/shard_map/ppermute | solution.py:387
  70.7 1.8 %collective-permute-start.18 = (bf16[4,48,128]{2,1,0:T(8,128)(2,1)S(1)}, bf16[4,48,128]{2,1,0:T(8,128)(2,1)S(1)}, u32[]{:S(2)}, u32[]{:S(2)}) collective-permute-start(bf16[4,48,128]{2,1,0:T(8,128)(2,1)S(1)} %collective-permute-done.14.a1), channel_id=1, source_target_pairs={{0,4},{4,0},{8,12},{12,8},{16,20},{20,16},{24,28},{28,24},{32,36},... | collective-permute-start | bytes 147464 | tf_op jit(solution)/shard_map/ppermute | solution.py:387
  71.7 1.5 %collective-permute-start.19 = (bf16[4,48,128]{2,1,0:T(8,128)(2,1)S(1)}, bf16[4,48,128]{2,1,0:T(8,128)(2,1)S(1)}, u32[]{:S(2)}, u32[]{:S(2)}) collective-permute-start(bf16[4,48,128]{2,1,0:T(8,128)(2,1)S(1)} %collective-permute-done.15.a2), channel_id=1, source_target_pairs={{0,4},{4,0},{8,12},{12,8},{16,20},{20,16},{24,28},{28,24},{32,36},... | collective-permute-start | bytes 147464 | tf_op jit(solution)/shard_map/ppermute | solution.py:387
  72.3 1.2 %collective-permute-start.20 = (bf16[4,48,128]{2,1,0:T(8,128)(2,1)S(1)}, bf16[4,48,128]{2,1,0:T(8,128)(2,1)S(1)}, u32[]{:S(2)}, u32[]{:S(2)}) collective-permute-start(bf16[4,48,128]{2,1,0:T(8,128)(2,1)S(1)} %collective-permute-done.16.a3), channel_id=1, source_target_pairs={{0,4},{4,0},{8,12},{12,8},{16,20},{20,16},{24,28},{28,24},{32,36},... | collective-permute-start | bytes 147464 | tf_op jit(solution)/shard_map/ppermute | solution.py:387
  75.0 16.9 %all-to-all-start = ((bf16[32,48,128]{2,1,0:T(8,128)(2,1)}), bf16[32,48,128]{2,1,0:T(8,128)(2,1)S(1)}, u32[]{:S(2)}, u32[]{:S(2)}) async-start(bf16[32,48,128]{2,1,0:T(8,128)(2,1)} %shard_map.136), calls=%async_computation | async-start | bytes 786432 | tf_op jit(solution)/shard_map/all_to_all | solution.py:506
  78.8 7.6 %collective-permute-start.21 = (bf16[4,160,128]{2,1,0:T(8,128)(2,1)S(1)}, bf16[4,160,128]{2,1,0:T(8,128)(2,1)S(1)}, u32[]{:S(2)}, u32[]{:S(2)}) collective-permute-start(bf16[4,160,128]{2,1,0:T(8,128)(2,1)S(1)} %get-tuple-element.61.a0), channel_id=1, source_target_pairs={{0,1},{1,2},{2,3},{3,0},{4,5},{5,6},{6,7},{7,4},{8,9},{9,10},{10,1... | collective-permute-start | bytes 491528 | tf_op jit(solution)/shard_map/ppermute | solution.py:382
  80.3 10.5 %collective-permute-start.22 = (bf16[4,160,128]{2,1,0:T(8,128)(2,1)S(1)}, bf16[4,160,128]{2,1,0:T(8,128)(2,1)S(1)}, u32[]{:S(2)}, u32[]{:S(2)}) collective-permute-start(bf16[4,160,128]{2,1,0:T(8,128)(2,1)S(1)} %get-tuple-element.61.a0), channel_id=1, source_target_pairs={{0,2},{1,3},{2,0},{3,1},{4,6},{5,7},{6,4},{7,5},{8,10},{9,11},{10,... | collective-permute-start | bytes 491528 | tf_op jit(solution)/shard_map/ppermute | solution.py:382
  83.3 8.7 %collective-permute-start.23 = (bf16[4,160,128]{2,1,0:T(8,128)(2,1)S(1)}, bf16[4,160,128]{2,1,0:T(8,128)(2,1)S(1)}, u32[]{:S(2)}, u32[]{:S(2)}) collective-permute-start(bf16[4,160,128]{2,1,0:T(8,128)(2,1)S(1)} %get-tuple-element.61.a0), channel_id=1, source_target_pairs={{0,3},{1,0},{2,1},{3,2},{4,7},{5,4},{6,5},{7,6},{8,11},{9,8},{10,9... | collective-permute-start | bytes 491528 | tf_op jit(solution)/shard_map/ppermute | solution.py:382
  83.3 9.7 %collective-permute-start.24 = (bf16[4,160,128]{2,1,0:T(8,128)(2,1)S(1)}, bf16[4,160,128]{2,1,0:T(8,128)(2,1)S(1)}, u32[]{:S(2)}, u32[]{:S(2)}) collective-permute-start(bf16[4,160,128]{2,1,0:T(8,128)(2,1)S(1)} %get-tuple-element.61.a0), channel_id=1, source_target_pairs={{0,4},{4,0},{8,12},{12,8},{16,20},{20,16},{24,28},{28,24},{32,36},... | collective-permute-start | bytes 491528 | tf_op jit(solution)/shard_map/ppermute | solution.py:387
  86.4 9.4 %collective-permute-start.25 = (bf16[4,160,128]{2,1,0:T(8,128)(2,1)S(1)}, bf16[4,160,128]{2,1,0:T(8,128)(2,1)S(1)}, u32[]{:S(2)}, u32[]{:S(2)}) collective-permute-start(bf16[4,160,128]{2,1,0:T(8,128)(2,1)S(1)} %collective-permute-done.21.a1), channel_id=1, source_target_pairs={{0,4},{4,0},{8,12},{12,8},{16,20},{20,16},{24,28},{28,24},{32,36},... | collective-permute-start | bytes 491528 | tf_op jit(solution)/shard_map/ppermute | solution.py:387
  90.8 5.0 %collective-permute-start.26 = (bf16[4,160,128]{2,1,0:T(8,128)(2,1)S(1)}, bf16[4,160,128]{2,1,0:T(8,128)(2,1)S(1)}, u32[]{:S(2)}, u32[]{:S(2)}) collective-permute-start(bf16[4,160,128]{2,1,0:T(8,128)(2,1)S(1)} %collective-permute-done.22.a2), channel_id=1, source_target_pairs={{0,4},{4,0},{8,12},{12,8},{16,20},{20,16},{24,28},{28,24},{32,36},... | collective-permute-start | bytes 491528 | tf_op jit(solution)/shard_map/ppermute | solution.py:387
  92.0 3.9 %collective-permute-start.27 = (bf16[4,160,128]{2,1,0:T(8,128)(2,1)S(1)}, bf16[4,160,128]{2,1,0:T(8,128)(2,1)S(1)}, u32[]{:S(2)}, u32[]{:S(2)}) collective-permute-start(bf16[4,160,128]{2,1,0:T(8,128)(2,1)S(1)} %collective-permute-done.23.a3), channel_id=1, source_target_pairs={{0,4},{4,0},{8,12},{12,8},{16,20},{20,16},{24,28},{28,24},{32,36},... | collective-permute-start | bytes 491528 | tf_op jit(solution)/shard_map/ppermute | solution.py:387
  92.7 5.1 %collective-permute-start.28 = (bf16[6,48,128]{2,1,0:T(8,128)(2,1)S(1)}, bf16[6,48,128]{2,1,0:T(8,128)(2,1)S(1)}, u32[]{:S(2)}, u32[]{:S(2)}) collective-permute-start(bf16[6,48,128]{2,1,0:T(8,128)(2,1)S(1)} %shard_map.138.b0), channel_id=1, source_target_pairs={{0,1},{1,2},{2,3},{3,0},{4,5},{5,6},{6,7},{7,4},{8,9},{9,10},{10,1... | collective-permute-start | bytes 221192 | tf_op jit(solution)/shard_map/ppermute | solution.py:382
  93.0 6.8 %collective-permute-start.29 = (bf16[6,48,128]{2,1,0:T(8,128)(2,1)S(1)}, bf16[6,48,128]{2,1,0:T(8,128)(2,1)S(1)}, u32[]{:S(2)}, u32[]{:S(2)}) collective-permute-start(bf16[6,48,128]{2,1,0:T(8,128)(2,1)S(1)} %shard_map.138.b0), channel_id=1, source_target_pairs={{0,2},{1,3},{2,0},{3,1},{4,6},{5,7},{6,4},{7,5},{8,10},{9,11},{10,... | collective-permute-start | bytes 221192 | tf_op jit(solution)/shard_map/ppermute | solution.py:382
  95.8 4.3 %collective-permute-start.30 = (bf16[6,48,128]{2,1,0:T(8,128)(2,1)S(1)}, bf16[6,48,128]{2,1,0:T(8,128)(2,1)S(1)}, u32[]{:S(2)}, u32[]{:S(2)}) collective-permute-start(bf16[6,48,128]{2,1,0:T(8,128)(2,1)S(1)} %shard_map.138.b0), channel_id=1, source_target_pairs={{0,3},{1,0},{2,1},{3,2},{4,7},{5,4},{6,5},{7,6},{8,11},{9,8},{10,9... | collective-permute-start | bytes 221192 | tf_op jit(solution)/shard_map/ppermute | solution.py:382
  (12 other events, 100.7 us)

commit v3 on v2

--- a/solution.py
+++ b/solution.py
@@ -26,6 +26,7 @@
 JOBS = 4
 ROWS = 176
 PIECE = 48
+SENT = PIECE + 2 * MEL
 flow_steps = 32.0
 norm_eps = 1e-05
 f32 = jnp.float32
@@ -55,13 +56,21 @@
     return jnp.where(odd, rows - high, high)
 
 
-def fold_kernel(w_in, e_rows, gain, w_qkv, out, half):
+def fold_kernel(w_in_h, e_rows_h, gain_h, w_qkv_h, out, half, w_in, e_rows, gain, w_qkv, sems):
+    pairs = [(w_in_h, w_in), (e_rows_h, e_rows), (gain_h, gain)]
+    pairs += [(w_qkv_h.at[c], w_qkv.at[c]) for c in range(3)]
+    copies = [pltpu.make_async_copy(a, b, sems.at[i]) for i, (a, b) in enumerate(pairs)]
+    for copy in copies:
+        copy.start()
+    for copy in copies[0:3]:
+        copy.wait()
     core = lax.axis_index("dp") & 1
     w = w_in[...].astype(f32)
     wc = w - jnp.mean(w, axis=1, keepdims=True)
     g = gain[...]
     wag = jnp.concatenate([wc * g, high_low(e_rows[...] * g)], axis=0).astype(bf16)
     for c in range(3):
+        copies[3 + c].wait()
         res = jnp.dot(wag, w_qkv[c], preferred_element_type=f32)
         if c == 0:
             res = res * (math.log2(math.e) / math.sqrt(HEAD_DIM))
@@ -75,33 +84,36 @@
         half[c] = jnp.where(core == 0, out[c, :, 0:128], out[c, :, 128:256])
 
 
-def prep_kernel(w_in, e_rows, w_out, w_mel, gain, wa_t, gram, wo_t, half, wm):
+def prep_kernel(w_in, e_rows, w_out, w_mel, gain, wa_t, wo_t, half, wm):
     w = w_in[...].astype(f32)
     wc = w - jnp.mean(w, axis=1, keepdims=True)
     wa = jnp.concatenate([wc, high_low(e_rows[...]), jnp.zeros((80, D), f32)], axis=0)
     wa_t[...] = wa.T[:, :ROWS].astype(bf16)
+    core = lax.axis_index("dp") & 1
+    o = w_out[...].astype(f32)
+    o = o - jnp.mean(o, axis=1, keepdims=True)
+    wo_t[...] = o.T.astype(bf16)
+    half[...] = jnp.where(core == 0, wo_t[:, 0:128], wo_t[:, 128:256])
+    wm[...] = (w_mel[...].astype(f32) * gain[...]).astype(bf16)
+
+
+def plan_kernel(
+    route, starts, lengths, mel_a, mel_b, noise_a, noise_b, w_in, e_rows, route_v,
+    table, gram, context_out, noise_out, valid_out, scaled_out, values_out, keys_out, own_out,
+    chunk_s, x_s,
+):
+    dp = lax.axis_index("dp")
+    m = lax.axis_index("mp")
+    core = dp & 1
+    w = w_in[...].astype(f32)
+    wc = w - jnp.mean(w, axis=1, keepdims=True)
+    wa = jnp.concatenate([wc, high_low(e_rows[...]), jnp.zeros((80, D), f32)], axis=0)
     wab = wa.astype(bf16)
     g = lax.dot_general(wab, wab, (((1,), (1,)), ((), ())), preferred_element_type=f32)
     g = g[0:ROWS, 0:ROWS] * (1.0 / D)
     high = g.astype(bf16)
     gram[0:ROWS, :] = high
     gram[ROWS : 2 * ROWS, :] = (g - high.astype(f32)).astype(bf16)
-    core = lax.axis_index("dp") & 1
-    o = w_out[...].astype(f32)
-    o = o - jnp.mean(o, axis=1, keepdims=True)
-    wo_t[...] = o.T.astype(bf16)
-    half[...] = jnp.where(core == 0, wo_t[:, 0:128], wo_t[:, 128:256])
-    wm[...] = (w_mel[...].astype(f32) * gain[...]).astype(bf16)
-
-
-def plan_kernel(
-    route, starts, lengths, mel_a, mel_b, noise_a, noise_b, gram,
-    table, context_out, noise_out, valid_out, scaled_out, values_out, keys_out, own_out,
-    chunk_s, x_s,
-):
-    dp = lax.axis_index("dp")
-    m = lax.axis_index("mp")
-    core = dp & 1
     base = (dp >> 1) * (2 * SLOT_DEV)
     seat = core * N_MP + m
     for i in range(TABLE):
@@ -129,16 +141,14 @@
     n_jobs = (n_live - seat + 7) >> 3
     table[COUNT_AT] = n_jobs
 
-    def owner(g, carry):
-        j = route[g] - dp * WORK_DEV
-
-        @pl.when(jnp.logical_and(j >= 0, j < WORK_DEV))
-        def _():
-            table[OWNER_AT + j] = g >> 4
-
-        return carry
-
-    lax.fori_loop(0, 32 * SLOT_DEV, owner, 0)
+    places = route_v[...]
+    owner = (
+        lax.broadcasted_iota(jnp.int32, places.shape, 0) * places.shape[1]
+        + lax.broadcasted_iota(jnp.int32, places.shape, 1)
+    ) >> 4
+    for j in range(WORK_DEV):
+        found = jnp.where(places == dp * WORK_DEV + j, owner, 0)
+        table[OWNER_AT + j] = jnp.sum(found)
 
     def job(q, carry):
         s = table[JOB_AT + q]
@@ -211,13 +221,20 @@
     v_s[...] = jnp.dot(wv_s[...], values[...], preferred_element_type=f32).astype(bf16)
     ones_rows = jnp.broadcast_to(valid, (16, WIN)).astype(bf16)
     zero = jnp.zeros((HEAD_DIM, BLOCK), bf16)
-    for g in range(4):
+
+    def score(g):
         columns = []
         for j in range(4):
             at = 256 * g + 64 * j
             rows = [q_s[at : at + 64, :] if t == j else zero for t in range(4)]
             columns.append(jnp.concatenate(rows, axis=0))
-        sc = jnp.dot(k_s[g], jnp.concatenate(columns, axis=1), preferred_element_type=f32)
+        return jnp.dot(k_s[g], jnp.concatenate(columns, axis=1), preferred_element_type=f32)
+
+    ahead = score(0)
+    for g in range(4):
+        sc = ahead
+        if g < 3:
+            ahead = score(g + 1)
         top = jnp.max(sc, axis=0, keepdims=True)
         pr = jnp.exp2(sc - top).astype(bf16)
         for j in range(4):
@@ -228,10 +245,14 @@
 
 
 def velocity_of(wr_s, o, own):
-    r = jnp.dot(wr_s[...], o[...], preferred_element_type=f32)
-    body = r[0:D]
-    var = jnp.sum(body * body, axis=0, keepdims=True) * (1.0 / D)
-    return jnp.where(own, r[D : D + MEL] * lax.rsqrt(var + norm_eps), 0.0)
+    v = jnp.dot(wr_s[D : D + MEL, :], o[...], preferred_element_type=f32)
+    squares = jnp.zeros((8, BLOCK), f32)
+    part = D // 4
+    for i in range(4):
+        r = jnp.dot(wr_s[part * i : part * i + part, :], o[...], preferred_element_type=f32)
+        squares = squares + jnp.sum((r * r).reshape(part // 8, 8, BLOCK), axis=0)
+    var = jnp.sum(squares, axis=0, keepdims=True) * (1.0 / D)
+    return jnp.where(own, v * lax.rsqrt(var + norm_eps), 0.0)
 
 
 def first_kernel(
@@ -265,7 +286,7 @@
 def second_kernel(
     table, context, noise, valid, gram, wq_s, wv_s, wk_s, o_in, wa_t, wm,
     wo0, ho1, so1, ho2, so2, ho3, so3,
-    tot_out, v0, v1, v2, v3,
+    v0, v1, v2, v3,
     k_s, q_s, v_s, o_s, wr_s, stage, scaled_s, values_s, keys_s,
 ):
     m = lax.axis_index("mp")
@@ -293,14 +314,14 @@
         )
         last = velocity_of(wr_s, o_s, own)
         total = (first + last).astype(bf16)
-        tot_out[q, 0:MEL, :] = total[:, 0:128]
-        tot_out[q, MEL : 2 * MEL, :] = total[:, 128:256]
         vel = last.astype(bf16)
         stage[0:MEL, :] = vel[:, 0:128]
         stage[MEL : 2 * MEL, :] = vel[:, 128:256]
         for k, out in enumerate((v0, v1, v2, v3)):
             quarter = (m + k) & 3
-            out[q] = stage[pl.ds(pl.multiple_of(quarter * PIECE, 16), PIECE), :]
+            out[q, 0:PIECE, :] = stage[pl.ds(pl.multiple_of(quarter * PIECE, 16), PIECE), :]
+            out[q, PIECE : PIECE + MEL, :] = total[:, 0:128]
+            out[q, PIECE + MEL : SENT, :] = total[:, 128:256]
         return carry
 
     lax.fori_loop(0, table[COUNT_AT], job, 0)
@@ -315,7 +336,7 @@
 
                 @pl.when(worker >= 0)
                 def _():
-                    act(pltpu.make_async_copy(a.at[q], out.at[worker], sems.at[entry]))
+                    act(pltpu.make_async_copy(a.at[q, 0:PIECE], out.at[worker], sems.at[entry]))
 
     each(lambda copy: copy.start())
     each(lambda copy: copy.wait())
@@ -340,7 +361,7 @@
 
             @pl.when(s >= 0)
             def _():
-                block = a[q].astype(f32)
+                block = a[q, PIECE:SENT, :].astype(f32)
                 off = (s & 3) * BLOCK
                 out[s >> 2, :, pl.ds(pl.multiple_of(off, 128), 128)] = block[0:MEL]
                 out[s >> 2, :, pl.ds(pl.multiple_of(off + 128, 128), 128)] = block[MEL : 2 * MEL]
@@ -395,11 +416,12 @@
     return lax.optimization_barrier((value, *others))[0]
 
 
-def run_plan(plan, audio, gram):
+def run_plan(plan, audio, w_input, e_rows):
     return call(
         plan_kernel,
         (
             shape((TABLE,), jnp.int32),
+            shape((2 * ROWS, ROWS), bf16),
             shape((JOBS, MEL, WIN), bf16),
             shape((JOBS, MEL, BLOCK), bf16),
             shape((JOBS, 8, WIN), f32),
@@ -408,10 +430,10 @@
             shape((JOBS, WIN, ROWS), bf16),
             shape((JOBS, ROWS, BLOCK), bf16),
         ),
-        "sss" + "v" * 5,
-        (*plan, *audio, gram),
+        "sss" + "v" * 7,
+        (*plan, *audio, w_input, e_rows, plan[0].reshape(4, 128)),
         scratch=[VMEM((MEL, 640), bf16), VMEM((MEL, BLOCK), bf16)],
-        out_kinds="s" + "v" * 7,
+        out_kinds="s" + "v" * 8,
     )
 
 
@@ -438,7 +460,7 @@
 def run_second(table, context, noise, valid, gram, first, wa_t, wm, wo):
     return call(
         second_kernel,
-        (shape((JOBS, 2 * MEL, 128), bf16),) + (shape((JOBS, PIECE, 128), bf16),) * 4,
+        (shape((JOBS, SENT, 128), bf16),) * 4,
         "s" + "v" * 17,
         (table, context, noise, valid, gram, *first, wa_t, wm, *wo),
         scratch=work_shapes()
@@ -464,25 +486,36 @@
     whole, half = call(
         fold_kernel,
         (shape((3, ROWS, 256), bf16), shape((3, ROWS, 128), bf16)),
-        "vvvv",
+        "hhhh",
         (w_input, e_rows, attn_gain.reshape(1, D), w3),
+        scratch=[
+            VMEM((2 * MEL, D), bf16),
+            VMEM((16, D), f32),
+            VMEM((1, D), f32),
+            VMEM((3, D, 256), bf16),
+            pltpu.SemaphoreType.DMA((6,)),
+        ],
+        limit=60,
     )
     halves = gathered(half)[1:]
-    audio = (mel_audio, to_other(mel_audio), start_noise, to_other(start_noise))
-    wa_t, gram, wo_t, wo_half, wm = call(
+    mel_late, noise_late = after(mel_audio, half), after(start_noise, half)
+    audio = (mel_audio, to_other(mel_late), start_noise, to_other(noise_late))
+    table, gram, context, noise, valid, scaled, values, keys, own_win = run_plan(
+        plan, audio, w_input, e_rows
+    )
+    wa_t, wo_t, wo_half, wm = call(
         prep_kernel,
         (
             shape((D, ROWS), bf16),
-            shape((2 * ROWS, ROWS), bf16),
             shape((D, 256), bf16),
             shape((D, 128), bf16),
             shape((MEL, D), bf16),
         ),
         "vvvvv",
-        (w_input, e_rows, after(w_out, half), w_mel, final_gain.reshape(1, D)),
+        (w_input, e_rows, after(w_out, table), w_mel, final_gain.reshape(1, D)),
     )
     out_halves = gathered(wo_half)[1:]
-    table, context, noise, valid, scaled, values, keys, own_win = run_plan(plan, audio, gram)
+    *halves, _ = lax.optimization_barrier((*halves, wo_half))
     wp = [whole]
     for h in halves:
         wp += [h, to_other(h)]
@@ -492,7 +525,7 @@
     wo = [wo_t]
     for h in out_halves[:-1]:
         wo += [h, to_other(h)]
-    tot, v0, v1, v2, v3 = run_second(table, context, noise, valid, gram, first, wa_t, wm, wo)
+    v0, v1, v2, v3 = run_second(table, context, noise, valid, gram, first, wa_t, wm, wo)
     pieces = [v0] + [to_next(v, k) for k, v in ((1, v1), (2, v2), (3, v3))]
     pieces += [to_other(v) for v in pieces]
     packed = call(
@@ -504,11 +537,10 @@
         out_kinds="h",
     )
     got = lax.all_to_all(packed, "dp", 0, 0, tiled=True)
-    totals = gathered(after(tot, packed))
-    totals += [to_other(t) for t in totals]
     infilled = call(
-        span_kernel, shape((UTT_DEV, MEL, SPAN_MAX), f32), "s" + "v" * 8, (table, *totals)
-    )
+        span_kernel, shape((UTT_DEV, MEL, SPAN_MAX), f32), "s" + "v" * 8, (table, *pieces)
+    )
+    table, infilled = lax.optimization_barrier((table, infilled))
     chosen = call(
         select_kernel,
         shape((WORK_DEV, PIECE, 128), bf16),

time: 102 us -> 94.5 us (0.926)
  Pallas kernels: 45.9 us -> 22.3 us
  starting transfers between devices: 36.1 us -> 47.6 us
  waiting for transfers between devices: 12.2 us -> 21.6 us
  local copies, waits for them, and re-layouts: 5.88 us -> 1.13 us
    pallas_call x9, Pallas kernels: 45.9 us -> 22.3 us  [call(): pl.pallas_call(kernel, out_shape=outs, in_specs=[spec(k) for k in kinds],...]
    all_to_all x1, starting transfers between devices: 3.79 us -> 12.9 us  [shards(): got = lax.all_to_all(packed, 'dp', 0, 0, tiled=True)]
    all_to_all x1, waiting for transfers between devices: 0.01 us -> 8.21 us  [shards(): got = lax.all_to_all(packed, 'dp', 0, 0, tiled=True)]
    ppermute x16 -> x12, starting transfers between devices: 12 us -> 17.2 us  [to_other(): return lax.ppermute(value, 'dp', [(i, i ^ 1) for i in range(size)])]
    unnamed x24 -> x22, local copies, waits for them, and re-layouts: 5.88 us -> 1.13 us
    ppermute x15 -> x12, starting transfers between devices: 20.3 us -> 17.5 us  [to_next(): return lax.ppermute(value, 'mp', [(i, (i + k) % N_MP) for i in range(N_MP)])]
    ppermute x16 -> x12, waiting for transfers between devices: 2.41 us -> 3.85 us  [to_other(): return lax.ppermute(value, 'dp', [(i, i ^ 1) for i in range(size)])]
    ppermute x15 -> x12, waiting for transfers between devices: 9.83 us -> 9.52 us  [to_next(): return lax.ppermute(value, 'mp', [(i, (i + k) % N_MP) for i in range(N_MP)])]
  transfers between devices with their start and end apart: 32 -> 25, of which waited for: 11 -> 14; matrix products, arithmetic and copies ran while one was open for 0% -> 0% of each run, Pallas kernels for 22% -> 10%
where the time goes in v3:
time: 94.5 us; the launch traced here: 93.4 us
  starting transfers between devices  47.6 us (50%)
  Pallas kernels  22.3 us (24%)
  waiting for transfers between devices  21.6 us (23%)
  local copies, waits for them, and re-layouts  1.13 us (1%)
    pallas_call x9, Pallas kernels, call(): pl.pallas_call(kernel, out_shape=outs, in_specs=[spec(k) for k in kinds],...  22.3 us
    ppermute x12, starting transfers between devices, to_next(): return lax.ppermute(value, 'mp', [(i, (i + k) % N_MP) for i in range(N_MP)])  17.5 us
    ppermute x12, starting transfers between devices, to_other(): return lax.ppermute(value, 'dp', [(i, i ^ 1) for i in range(size)])  17.2 us
    all_to_all x1, starting transfers between devices, shards(): got = lax.all_to_all(packed, 'dp', 0, 0, tiled=True)  12.9 us
    ppermute x12, waiting for transfers between devices, to_next(): return lax.ppermute(value, 'mp', [(i, (i + k) % N_MP) for i in range(N_MP)])  9.52 us
    all_to_all x1, waiting for transfers between devices, shards(): got = lax.all_to_all(packed, 'dp', 0, 0, tiled=True)  8.21 us
    ppermute x12, waiting for transfers between devices, to_other(): return lax.ppermute(value, 'dp', [(i, i ^ 1) for i in range(size)])  3.85 us
  transfers between devices with their start and end apart: 25, of which 14 were waited for; matrix products, arithmetic and copies ran while one was open for 0% of the time, Pallas kernels for 10%

profile of v3, /device:TPU:1, one launch (start us, length us, event | category | flops | bytes accessed | tf_op | source)
XLA Modules:
  0.0 93.4 jit_solution(9756468131101611068)
XLA Ops:
  0.7 3.1 %shard_map.131 = (bf16[3,176,256]{2,1,0:T(8,128)(2,1)}, bf16[3,176,128]{2,1,0:T(8,128)(2,1)}) custom-call(bf16[160,1024]{1,0:T(8,128)(2,1)} %w_in.3, f32[16,1024]{1,0:T(8,128)} %constant.2.clone.e_rows_h.e_rows, f32[1,1024]{1,0:T(1,128)} %bitcast.7, bf16[3,1024,256]{2,1,0:T(8,128)(2,1)} %bitcast.6), custom_call_target="tpu_custom_call" | custom-call | tf_op jit(solution)/shard_map/pallas_call | solution.py:388
  3.8 1.5 %collective-permute-start = (bf16[4,80,2048]{2,1,0:T(8,128)(2,1)S(1)}, bf16[4,80,2048]{2,1,0:T(8,128)(2,1)S(1)}, u32[]{:S(2)}, u32[]{:S(2)}) collective-permute-start(bf16[4,80,2048]{2,1,0:T(8,128)(2,1)S(1)} %copy-done.1), channel_id=1, source_target_pairs={{0,4},{4,0},{8,12},{12,8},{16,20},{20,16},{24,28},{28,24},{32,36},... | collective-permute-start | bytes 3932168 | tf_op jit(solution)/shard_map/ppermute | solution.py:408
  5.4 1.7 %collective-permute-start.2 = (bf16[3,176,128]{2,1,0:T(8,128)(2,1)}, bf16[3,176,128]{2,1,0:T(8,128)(2,1)S(1)}, u32[]{:S(2)}, u32[]{:S(2)}) collective-permute-start(bf16[3,176,128]{2,1,0:T(8,128)(2,1)} %get-tuple-element.37), channel_id=1, source_target_pairs={{0,1},{1,2},{2,3},{3,0},{4,5},{5,6},{6,7},{7,4},{8,9},{9,10},{10,1... | collective-permute-start | bytes 405512 | tf_op jit(solution)/shard_map/ppermute | solution.py:403
  7.1 3.3 %collective-permute-start.3 = (bf16[3,176,128]{2,1,0:T(8,128)(2,1)}, bf16[3,176,128]{2,1,0:T(8,128)(2,1)S(1)}, u32[]{:S(2)}, u32[]{:S(2)}) collective-permute-start(bf16[3,176,128]{2,1,0:T(8,128)(2,1)} %get-tuple-element.37), channel_id=1, source_target_pairs={{0,2},{1,3},{2,0},{3,1},{4,6},{5,7},{6,4},{7,5},{8,10},{9,11},{10,... | collective-permute-start | bytes 405512 | tf_op jit(solution)/shard_map/ppermute | solution.py:403
  10.5 0.7 collective-permute-start.4
  11.2 1.1 %copy-done.2 = bf16[4,80,1024]{2,1,0:T(8,128)(2,1)S(1)} copy-done((bf16[4,80,1024]{2,1,0:T(8,128)(2,1)S(1)}, bf16[4,80,1024]{2,1,0:T(8,128)(2,1)}, u32[]{:S(2)}) %copy-start.2) | copy-done | bytes 655384
  12.3 2.8 %shard_map.132 = (s32[80]{0:T(128)S(1)}, bf16[352,176]{1,0:T(8,128)(2,1)S(1)}, bf16[4,80,512]{2,1,0:T(8,128)(2,1)S(1)}, bf16[4,80,256]{2,1,0:T(8,128)(2,1)S(1)},...) custom-call(s32[512]{0:T(512)S(1)} %copy-done.7, ...), custom_call_target="tpu_custom_call" | custom-call | tf_op jit(solution)/shard_map/pallas_call | solution.py:388
  15.8 1.0 %collective-permute-done.3.hp2 = bf16[3,176,128]{2,1,0:T(8,128)(2,1)S(1)} collective-permute-done((bf16[3,176,128]{2,1,0:T(8,128)(2,1)}, bf16[3,176,128]{2,1,0:T(8,128)(2,1)S(1)}, u32[]{:S(2)}, u32[]{:S(2)}) %collective-permute-start.3) | collective-permute-done | bytes 135200 | tf_op jit(solution)/shard_map/ppermute | solution.py:403
  16.8 1.3 %collective-permute-start.5 = (bf16[3,176,128]{2,1,0:T(8,128)(2,1)S(1)}, bf16[3,176,128]{2,1,0:T(8,128)(2,1)S(1)}, u32[]{:S(2)}, u32[]{:S(2)}) collective-permute-start(bf16[3,176,128]{2,1,0:T(8,128)(2,1)S(1)} %collective-permute-done.2.hp1), channel_id=1, source_target_pairs={{0,4},{4,0},{8,12},{12,8},{16,20},{20,16},{24,28},{28,24},{32,36},... | collective-permute-start | bytes 405512 | tf_op jit(solution)/shard_map/ppermute | solution.py:408
  18.1 0.9 collective-permute-start.8
  19.0 2.1 %collective-permute-start.9 = (bf16[1024,128]{1,0:T(8,128)(2,1)S(1)}, bf16[1024,128]{1,0:T(8,128)(2,1)S(1)}, u32[]{:S(2)}, u32[]{:S(2)}) collective-permute-start(bf16[1024,128]{1,0:T(8,128)(2,1)S(1)} %get-tuple-element.51), channel_id=1, source_target_pairs={{0,2},{1,3},{2,0},{3,1},{4,6},{5,7},{6,4},{7,5},{8,10},{9,11},{10,... | collective-permute-start | bytes 786440 | tf_op jit(solution)/shard_map/ppermute | solution.py:403
  21.1 1.1 %collective-permute-start.10 = (bf16[1024,128]{1,0:T(8,128)(2,1)S(1)}, bf16[1024,128]{1,0:T(8,128)(2,1)S(1)}, u32[]{:S(2)}, u32[]{:S(2)}) collective-permute-start(bf16[1024,128]{1,0:T(8,128)(2,1)S(1)} %get-tuple-element.51), channel_id=1, source_target_pairs={{0,3},{1,0},{2,1},{3,2},{4,7},{5,4},{6,5},{7,6},{8,11},{9,8},{10,9... | collective-permute-start | bytes 786440 | tf_op jit(solution)/shard_map/ppermute | solution.py:403
  22.1 0.8 collective-permute-start.6
  23.0 1.0 %collective-permute-done.6.sp2 = bf16[3,176,128]{2,1,0:T(8,128)(2,1)S(1)} collective-permute-done((bf16[3,176,128]{2,1,0:T(8,128)(2,1)S(1)}, bf16[3,176,128]{2,1,0:T(8,128)(2,1)S(1)}, u32[]{:S(2)}, u32[]{:S(2)}) %collective-permute-start.6) | collective-permute-done | bytes 135200 | tf_op jit(solution)/shard_map/ppermute | solution.py:408
  24.3 4.0 %shard_map.134 = (bf16[1024,176]{1,0:T(8,128)(2,1)S(1)}, bf16[1024,176]{1,0:T(8,128)(2,1)S(1)}, bf16[176,1024]{1,0:T(8,128)(2,1)S(1)}, bf16[4,1200,256]{2,1,0:T(8,128)(2,1)S(1)}) custom-call(s32[80]{0:T(128)S(1)} %get-tuple-element.71.table, f32[4,8,512]{2,1,0:T(8,128)S(1)} %get-tuple-element.43.valid, bf16[4,176,256]{2,1,0:T(8,128)(2,1)S(1)} %get-tuple-element.45.scaled, ...), custom_call_target="tpu_custom_call" | custom-call | tf_op jit(solution)/shard_map/pallas_call | solution.py:388
  28.4 4.8 %collective-permute-done.9.ho2 = bf16[1024,128]{1,0:T(8,128)(2,1)S(1)} collective-permute-done((bf16[1024,128]{1,0:T(8,128)(2,1)S(1)}, bf16[1024,128]{1,0:T(8,128)(2,1)S(1)}, u32[]{:S(2)}, u32[]{:S(2)}) %collective-permute-start.9) | collective-permute-done | bytes 262176 | tf_op jit(solution)/shard_map/ppermute | solution.py:403
  33.2 1.1 %collective-permute-start.11 = (bf16[1024,128]{1,0:T(8,128)(2,1)S(1)}, bf16[1024,128]{1,0:T(8,128)(2,1)S(1)}, u32[]{:S(2)}, u32[]{:S(2)}) collective-permute-start(bf16[1024,128]{1,0:T(8,128)(2,1)S(1)} %collective-permute-done.8.ho1), channel_id=1, source_target_pairs={{0,4},{4,0},{8,12},{12,8},{16,20},{20,16},{24,28},{28,24},{32,36},... | collective-permute-start | bytes 786440 | tf_op jit(solution)/shard_map/ppermute | solution.py:408
  36.2 6.8 %shard_map.135 = (bf16[4,208,128]{2,1,0:T(8,128)(2,1)S(1)}, bf16[4,208,128]{2,1,0:T(8,128)(2,1)S(1)}, bf16[4,208,128]{2,1,0:T(8,128)(2,1)S(1)}, bf16[4,208,128]{2,1,0:T(8,128)(2,1)S(1)}) custom-call(s32[80]{0:T(128)S(1)} %get-tuple-element.71.table, bf16[4,80,512]{2,1,0:T(8,128)(2,1)S(1)} %get-tuple-element.41.context, ...), custom_call_target="tpu_custom_call" | custom-call | tf_op jit(solution)/shard_map/pallas_call | solution.py:388
  43.0 1.4 %collective-permute-start.14 = (bf16[4,208,128]{2,1,0:T(8,128)(2,1)S(1)}, bf16[4,208,128]{2,1,0:T(8,128)(2,1)S(1)}, u32[]{:S(2)}, u32[]{:S(2)}) collective-permute-start(bf16[4,208,128]{2,1,0:T(8,128)(2,1)S(1)} %get-tuple-element.67), channel_id=1, source_target_pairs={{0,1},{1,2},{2,3},{3,0},{4,5},{5,6},{6,7},{7,4},{8,9},{9,10},{10,1... | collective-permute-start | bytes 638984 | tf_op jit(solution)/shard_map/ppermute | solution.py:403
  44.3 2.2 %collective-permute-start.15 = (bf16[4,208,128]{2,1,0:T(8,128)(2,1)S(1)}, bf16[4,208,128]{2,1,0:T(8,128)(2,1)S(1)}, u32[]{:S(2)}, u32[]{:S(2)}) collective-permute-start(bf16[4,208,128]{2,1,0:T(8,128)(2,1)S(1)} %get-tuple-element.68), channel_id=1, source_target_pairs={{0,2},{1,3},{2,0},{3,1},{4,6},{5,7},{6,4},{7,5},{8,10},{9,11},{10,... | collective-permute-start | bytes 638984 | tf_op jit(solution)/shard_map/ppermute | solution.py:403
  47.1 6.5 %collective-permute-start.17 = (bf16[4,208,128]{2,1,0:T(8,128)(2,1)S(1)}, bf16[4,208,128]{2,1,0:T(8,128)(2,1)S(1)}, u32[]{:S(2)}, u32[]{:S(2)}) collective-permute-start(bf16[4,208,128]{2,1,0:T(8,128)(2,1)S(1)} %get-tuple-element.66.a0), channel_id=1, source_target_pairs={{0,4},{4,0},{8,12},{12,8},{16,20},{20,16},{24,28},{28,24},{32,36},... | collective-permute-start | bytes 638984 | tf_op jit(solution)/shard_map/ppermute | solution.py:408
  53.6 4.5 %collective-permute-start.18 = (bf16[4,208,128]{2,1,0:T(8,128)(2,1)S(1)}, bf16[4,208,128]{2,1,0:T(8,128)(2,1)S(1)}, u32[]{:S(2)}, u32[]{:S(2)}) collective-permute-start(bf16[4,208,128]{2,1,0:T(8,128)(2,1)S(1)} %collective-permute-done.14.a1), channel_id=1, source_target_pairs={{0,4},{4,0},{8,12},{12,8},{16,20},{20,16},{24,28},{28,24},{32,36},... | collective-permute-start | bytes 638984 | tf_op jit(solution)/shard_map/ppermute | solution.py:408
  58.1 0.8 collective-permute-start.20
  60.0 1.5 %shard_map.137 = bf16[32,48,128]{2,1,0:T(8,128)(2,1)} custom-call(s32[80]{0:T(128)S(1)} %get-tuple-element.71.table, bf16[4,208,128]{2,1,0:T(8,128)(2,1)S(1)} %get-tuple-element.66.a0, bf16[4,208,128]{2,1,0:T(8,128)(2,1)S(1)} %collective-permute-done.14.a1, bf16[4,208,128]{2,1,0:T(8,128)(2,1)S(1)} %collective-permute-done.15.a2, ...), custom_call_target="tpu_custom_call" | custom-call | tf_op jit(solution)/shard_map/pallas_call | solution.py:388
  61.5 12.9 %all-to-all-start = ((bf16[32,48,128]{2,1,0:T(8,128)(2,1)}), bf16[32,48,128]{2,1,0:T(8,128)(2,1)S(1)}, u32[]{:S(2)}, u32[]{:S(2)}) async-start(bf16[32,48,128]{2,1,0:T(8,128)(2,1)} %shard_map.137), calls=%async_computation | async-start | bytes 786432 | tf_op jit(solution)/shard_map/all_to_all | solution.py:539
  74.5 2.0 %shard_map.136 = f32[4,80,1024]{2,1,0:T(8,128)} custom-call(s32[80]{0:T(128)S(1)} %get-tuple-element.71.table, bf16[4,208,128]{2,1,0:T(8,128)(2,1)S(1)} %get-tuple-element.66.a0, bf16[4,208,128]{2,1,0:T(8,128)(2,1)S(1)} %collective-permute-done.14.a1, bf16[4,208,128]{2,1,0:T(8,128)(2,1)S(1)} %collective-permute-done.15.a2, ...), custom_call_target="tpu_custom_call" | custom-call | tf_op jit(solution)/shard_map/pallas_call | solution.py:388
  76.4 8.2 %all-to-all-done.got = bf16[32,48,128]{2,1,0:T(8,128)(2,1)S(1)} async-done(((bf16[32,48,128]{2,1,0:T(8,128)(2,1)}), bf16[32,48,128]{2,1,0:T(8,128)(2,1)S(1)}, u32[]{:S(2)}, u32[]{:S(2)}) %all-to-all-start) | async-done | bytes 393248 | tf_op jit(solution)/shard_map/all_to_all | solution.py:539
  84.6 0.7 shard_map.138.b0
  85.6 3.3 %collective-permute-start.22 = (bf16[6,48,128]{2,1,0:T(8,128)(2,1)S(1)}, bf16[6,48,128]{2,1,0:T(8,128)(2,1)S(1)}, u32[]{:S(2)}, u32[]{:S(2)}) collective-permute-start(bf16[6,48,128]{2,1,0:T(8,128)(2,1)S(1)} %shard_map.138.b0), channel_id=1, source_target_pairs={{0,2},{1,3},{2,0},{3,1},{4,6},{5,7},{6,4},{7,5},{8,10},{9,11},{10,... | collective-permute-start | bytes 221192 | tf_op jit(solution)/shard_map/ppermute | solution.py:403
  88.9 0.9 collective-permute-done.21.b1
  89.8 2.4 %collective-permute-done.22.b2 = bf16[6,48,128]{2,1,0:T(8,128)(2,1)S(1)} collective-permute-done((bf16[6,48,128]{2,1,0:T(8,128)(2,1)S(1)}, bf16[6,48,128]{2,1,0:T(8,128)(2,1)S(1)}, u32[]{:S(2)}, u32[]{:S(2)}) %collective-permute-start.22) | collective-permute-done | bytes 73760 | tf_op jit(solution)/shard_map/ppermute | solution.py:403
  92.6 0.8 shard_map.139
  (49 shorter events, 5.3 us)
Async XLA Ops:
  0.6 10.6 %copy-start.3 = (f32[16,1024]{1,0:T(8,128)S(1)}, f32[16,1024]{1,0:T(8,128)}, u32[]{:S(2)}) copy-start(f32[16,1024]{1,0:T(8,128)} %constant.2.clone.e_rows_h.e_rows) | copy-start | bytes 196612
  0.6 10.6 %copy-start = (bf16[160,1024]{1,0:T(8,128)(2,1)S(1)}, bf16[160,1024]{1,0:T(8,128)(2,1)}, u32[]{:S(2)}) copy-start(bf16[160,1024]{1,0:T(8,128)(2,1)} %w_in.3) | copy-start | bytes 983044
  0.7 3.2 %copy-start.1 = (bf16[4,80,2048]{2,1,0:T(8,128)(2,1)S(1)}, bf16[4,80,2048]{2,1,0:T(8,128)(2,1)}, u32[]{:S(2)}) copy-start(bf16[4,80,2048]{2,1,0:T(8,128)(2,1)} %mel_a.1) | copy-start | bytes 3932164
  0.7 10.5 %copy-start.9 = (s32[128]{0:T(128)S(1)}, s32[128]{0:T(128)}, u32[]{:S(2)}) copy-start(s32[128]{0:T(128)} %starts.1) | copy-start | bytes 1540
  0.7 10.5 %copy-start.10 = (s32[128]{0:T(128)S(1)}, s32[128]{0:T(128)}, u32[]{:S(2)}) copy-start(s32[128]{0:T(128)} %lengths.1) | copy-start | bytes 1540
  0.7 10.5 %copy-start.7 = (s32[512]{0:T(512)S(1)}, s32[512]{0:T(512)}, u32[]{:S(2)}) copy-start(s32[512]{0:T(512)} %route.1) | copy-start | bytes 6148
  3.8 7.4 %collective-permute-start = (bf16[4,80,2048]{2,1,0:T(8,128)(2,1)S(1)}, bf16[4,80,2048]{2,1,0:T(8,128)(2,1)S(1)}, u32[]{:S(2)}, u32[]{:S(2)}) collective-permute-start(bf16[4,80,2048]{2,1,0:T(8,128)(2,1)S(1)} %copy-done.1), channel_id=1, source_target_pairs={{0,4},{4,0},{8,12},{12,8},{16,20},{20,16},{24,28},{28,24},{32,36},... | collective-permute-start | bytes 3932168 | tf_op jit(solution)/shard_map/ppermute | solution.py:408
  5.3 5.8 %collective-permute-start.1 = (bf16[4,80,1024]{2,1,0:T(8,128)(2,1)}, bf16[4,80,1024]{2,1,0:T(8,128)(2,1)S(1)}, u32[]{:S(2)}, u32[]{:S(2)}) collective-permute-start(bf16[4,80,1024]{2,1,0:T(8,128)(2,1)} %noise_a.1), channel_id=1, source_target_pairs={{0,4},{4,0},{8,12},{12,8},{16,20},{20,16},{24,28},{28,24},{32,36},... | collective-permute-start | bytes 1966088 | tf_op jit(solution)/shard_map/ppermute | solution.py:408
  5.4 10.4 %collective-permute-start.2 = (bf16[3,176,128]{2,1,0:T(8,128)(2,1)}, bf16[3,176,128]{2,1,0:T(8,128)(2,1)S(1)}, u32[]{:S(2)}, u32[]{:S(2)}) collective-permute-start(bf16[3,176,128]{2,1,0:T(8,128)(2,1)} %get-tuple-element.37), channel_id=1, source_target_pairs={{0,1},{1,2},{2,3},{3,0},{4,5},{5,6},{6,7},{7,4},{8,9},{9,10},{10,1... | collective-permute-start | bytes 405512 | tf_op jit(solution)/shard_map/ppermute | solution.py:403
  7.1 9.7 %collective-permute-start.3 = (bf16[3,176,128]{2,1,0:T(8,128)(2,1)}, bf16[3,176,128]{2,1,0:T(8,128)(2,1)S(1)}, u32[]{:S(2)}, u32[]{:S(2)}) collective-permute-start(bf16[3,176,128]{2,1,0:T(8,128)(2,1)} %get-tuple-element.37), channel_id=1, source_target_pairs={{0,2},{1,3},{2,0},{3,1},{4,6},{5,7},{6,4},{7,5},{8,10},{9,11},{10,... | collective-permute-start | bytes 405512 | tf_op jit(solution)/shard_map/ppermute | solution.py:403
  10.5 6.4 %collective-permute-start.4 = (bf16[3,176,128]{2,1,0:T(8,128)(2,1)}, bf16[3,176,128]{2,1,0:T(8,128)(2,1)S(1)}, u32[]{:S(2)}, u32[]{:S(2)}) collective-permute-start(bf16[3,176,128]{2,1,0:T(8,128)(2,1)} %get-tuple-element.37), channel_id=1, source_target_pairs={{0,3},{1,0},{2,1},{3,2},{4,7},{5,4},{6,5},{7,6},{8,11},{9,8},{10,9... | collective-permute-start | bytes 405512 | tf_op jit(solution)/shard_map/ppermute | solution.py:403
  12.3 12.0 %copy-start.5 = (bf16[3,176,256]{2,1,0:T(8,128)(2,1)S(1)}, bf16[3,176,256]{2,1,0:T(8,128)(2,1)}, u32[]{:S(2)}) copy-start(bf16[3,176,256]{2,1,0:T(8,128)(2,1)} %get-tuple-element.49.wp0) | copy-start | bytes 811012
  16.8 6.1 %collective-permute-start.5 = (bf16[3,176,128]{2,1,0:T(8,128)(2,1)S(1)}, bf16[3,176,128]{2,1,0:T(8,128)(2,1)S(1)}, u32[]{:S(2)}, u32[]{:S(2)}) collective-permute-start(bf16[3,176,128]{2,1,0:T(8,128)(2,1)S(1)} %collective-permute-done.2.hp1), channel_id=1, source_target_pairs={{0,4},{4,0},{8,12},{12,8},{16,20},{20,16},{24,28},{28,24},{32,36},... | collective-permute-start | bytes 405512 | tf_op jit(solution)/shard_map/ppermute | solution.py:408
  18.1 10.3 %collective-permute-start.8 = (bf16[1024,128]{1,0:T(8,128)(2,1)S(1)}, bf16[1024,128]{1,0:T(8,128)(2,1)S(1)}, u32[]{:S(2)}, u32[]{:S(2)}) collective-permute-start(bf16[1024,128]{1,0:T(8,128)(2,1)S(1)} %get-tuple-element.51), channel_id=1, source_target_pairs={{0,1},{1,2},{2,3},{3,0},{4,5},{5,6},{6,7},{7,4},{8,9},{9,10},{10,1... | collective-permute-start | bytes 786440 | tf_op jit(solution)/shard_map/ppermute | solution.py:403
  19.0 14.2 %collective-permute-start.9 = (bf16[1024,128]{1,0:T(8,128)(2,1)S(1)}, bf16[1024,128]{1,0:T(8,128)(2,1)S(1)}, u32[]{:S(2)}, u32[]{:S(2)}) collective-permute-start(bf16[1024,128]{1,0:T(8,128)(2,1)S(1)} %get-tuple-element.51), channel_id=1, source_target_pairs={{0,2},{1,3},{2,0},{3,1},{4,6},{5,7},{6,4},{7,5},{8,10},{9,11},{10,... | collective-permute-start | bytes 786440 | tf_op jit(solution)/shard_map/ppermute | solution.py:403
  21.1 12.1 %collective-permute-start.10 = (bf16[1024,128]{1,0:T(8,128)(2,1)S(1)}, bf16[1024,128]{1,0:T(8,128)(2,1)S(1)}, u32[]{:S(2)}, u32[]{:S(2)}) collective-permute-start(bf16[1024,128]{1,0:T(8,128)(2,1)S(1)} %get-tuple-element.51), channel_id=1, source_target_pairs={{0,3},{1,0},{2,1},{3,2},{4,7},{5,4},{6,5},{7,6},{8,11},{9,8},{10,9... | collective-permute-start | bytes 786440 | tf_op jit(solution)/shard_map/ppermute | solution.py:403
  22.1 1.8 %collective-permute-start.6 = (bf16[3,176,128]{2,1,0:T(8,128)(2,1)S(1)}, bf16[3,176,128]{2,1,0:T(8,128)(2,1)S(1)}, u32[]{:S(2)}, u32[]{:S(2)}) collective-permute-start(bf16[3,176,128]{2,1,0:T(8,128)(2,1)S(1)} %collective-permute-done.3.hp2), channel_id=1, source_target_pairs={{0,4},{4,0},{8,12},{12,8},{16,20},{20,16},{24,28},{28,24},{32,36},... | collective-permute-start | bytes 405512 | tf_op jit(solution)/shard_map/ppermute | solution.py:408
  23.0 1.4 %collective-permute-start.7 = (bf16[3,176,128]{2,1,0:T(8,128)(2,1)S(1)}, bf16[3,176,128]{2,1,0:T(8,128)(2,1)S(1)}, u32[]{:S(2)}, u32[]{:S(2)}) collective-permute-start(bf16[3,176,128]{2,1,0:T(8,128)(2,1)S(1)} %collective-permute-done.4.hp3), channel_id=1, source_target_pairs={{0,4},{4,0},{8,12},{12,8},{16,20},{20,16},{24,28},{28,24},{32,36},... | collective-permute-start | bytes 405512 | tf_op jit(solution)/shard_map/ppermute | solution.py:408
  33.2 2.3 %collective-permute-start.11 = (bf16[1024,128]{1,0:T(8,128)(2,1)S(1)}, bf16[1024,128]{1,0:T(8,128)(2,1)S(1)}, u32[]{:S(2)}, u32[]{:S(2)}) collective-permute-start(bf16[1024,128]{1,0:T(8,128)(2,1)S(1)} %collective-permute-done.8.ho1), channel_id=1, source_target_pairs={{0,4},{4,0},{8,12},{12,8},{16,20},{20,16},{24,28},{28,24},{32,36},... | collective-permute-start | bytes 786440 | tf_op jit(solution)/shard_map/ppermute | solution.py:408
  34.3 1.5 %collective-permute-start.12 = (bf16[1024,128]{1,0:T(8,128)(2,1)S(1)}, bf16[1024,128]{1,0:T(8,128)(2,1)S(1)}, u32[]{:S(2)}, u32[]{:S(2)}) collective-permute-start(bf16[1024,128]{1,0:T(8,128)(2,1)S(1)} %collective-permute-done.9.ho2), channel_id=1, source_target_pairs={{0,4},{4,0},{8,12},{12,8},{16,20},{20,16},{24,28},{28,24},{32,36},... | collective-permute-start | bytes 786440 | tf_op jit(solution)/shard_map/ppermute | solution.py:408
  34.3 1.9 %collective-permute-start.13 = (bf16[1024,128]{1,0:T(8,128)(2,1)S(1)}, bf16[1024,128]{1,0:T(8,128)(2,1)S(1)}, u32[]{:S(2)}, u32[]{:S(2)}) collective-permute-start(bf16[1024,128]{1,0:T(8,128)(2,1)S(1)} %collective-permute-done.10.ho3), channel_id=1, source_target_pairs={{0,4},{4,0},{8,12},{12,8},{16,20},{20,16},{24,28},{28,24},{32,36},... | collective-permute-start | bytes 786440 | tf_op jit(solution)/shard_map/ppermute | solution.py:408
  43.0 10.6 %collective-permute-start.14 = (bf16[4,208,128]{2,1,0:T(8,128)(2,1)S(1)}, bf16[4,208,128]{2,1,0:T(8,128)(2,1)S(1)}, u32[]{:S(2)}, u32[]{:S(2)}) collective-permute-start(bf16[4,208,128]{2,1,0:T(8,128)(2,1)S(1)} %get-tuple-element.67), channel_id=1, source_target_pairs={{0,1},{1,2},{2,3},{3,0},{4,5},{5,6},{6,7},{7,4},{8,9},{9,10},{10,1... | collective-permute-start | bytes 638984 | tf_op jit(solution)/shard_map/ppermute | solution.py:403
  44.3 13.7 %collective-permute-start.15 = (bf16[4,208,128]{2,1,0:T(8,128)(2,1)S(1)}, bf16[4,208,128]{2,1,0:T(8,128)(2,1)S(1)}, u32[]{:S(2)}, u32[]{:S(2)}) collective-permute-start(bf16[4,208,128]{2,1,0:T(8,128)(2,1)S(1)} %get-tuple-element.68), channel_id=1, source_target_pairs={{0,2},{1,3},{2,0},{3,1},{4,6},{5,7},{6,4},{7,5},{8,10},{9,11},{10,... | collective-permute-start | bytes 638984 | tf_op jit(solution)/shard_map/ppermute | solution.py:403
  46.6 11.5 %collective-permute-start.16 = (bf16[4,208,128]{2,1,0:T(8,128)(2,1)S(1)}, bf16[4,208,128]{2,1,0:T(8,128)(2,1)S(1)}, u32[]{:S(2)}, u32[]{:S(2)}) collective-permute-start(bf16[4,208,128]{2,1,0:T(8,128)(2,1)S(1)} %get-tuple-element.69), channel_id=1, source_target_pairs={{0,3},{1,0},{2,1},{3,2},{4,7},{5,4},{6,5},{7,6},{8,11},{9,8},{10,9... | collective-permute-start | bytes 638984 | tf_op jit(solution)/shard_map/ppermute | solution.py:403
  47.1 11.9 %collective-permute-start.17 = (bf16[4,208,128]{2,1,0:T(8,128)(2,1)S(1)}, bf16[4,208,128]{2,1,0:T(8,128)(2,1)S(1)}, u32[]{:S(2)}, u32[]{:S(2)}) collective-permute-start(bf16[4,208,128]{2,1,0:T(8,128)(2,1)S(1)} %get-tuple-element.66.a0), channel_id=1, source_target_pairs={{0,4},{4,0},{8,12},{12,8},{16,20},{20,16},{24,28},{28,24},{32,36},... | collective-permute-start | bytes 638984 | tf_op jit(solution)/shard_map/ppermute | solution.py:408
  53.6 5.6 %collective-permute-start.18 = (bf16[4,208,128]{2,1,0:T(8,128)(2,1)S(1)}, bf16[4,208,128]{2,1,0:T(8,128)(2,1)S(1)}, u32[]{:S(2)}, u32[]{:S(2)}) collective-permute-start(bf16[4,208,128]{2,1,0:T(8,128)(2,1)S(1)} %collective-permute-done.14.a1), channel_id=1, source_target_pairs={{0,4},{4,0},{8,12},{12,8},{16,20},{20,16},{24,28},{28,24},{32,36},... | collective-permute-start | bytes 638984 | tf_op jit(solution)/shard_map/ppermute | solution.py:408
  58.1 1.5 %collective-permute-start.19 = (bf16[4,208,128]{2,1,0:T(8,128)(2,1)S(1)}, bf16[4,208,128]{2,1,0:T(8,128)(2,1)S(1)}, u32[]{:S(2)}, u32[]{:S(2)}) collective-permute-start(bf16[4,208,128]{2,1,0:T(8,128)(2,1)S(1)} %collective-permute-done.15.a2), channel_id=1, source_target_pairs={{0,4},{4,0},{8,12},{12,8},{16,20},{20,16},{24,28},{28,24},{32,36},... | collective-permute-start | bytes 638984 | tf_op jit(solution)/shard_map/ppermute | solution.py:408
  58.1 1.9 %collective-permute-start.20 = (bf16[4,208,128]{2,1,0:T(8,128)(2,1)S(1)}, bf16[4,208,128]{2,1,0:T(8,128)(2,1)S(1)}, u32[]{:S(2)}, u32[]{:S(2)}) collective-permute-start(bf16[4,208,128]{2,1,0:T(8,128)(2,1)S(1)} %collective-permute-done.16.a3), channel_id=1, source_target_pairs={{0,4},{4,0},{8,12},{12,8},{16,20},{20,16},{24,28},{28,24},{32,36},... | collective-permute-start | bytes 638984 | tf_op jit(solution)/shard_map/ppermute | solution.py:408
  61.5 23.1 %all-to-all-start = ((bf16[32,48,128]{2,1,0:T(8,128)(2,1)}), bf16[32,48,128]{2,1,0:T(8,128)(2,1)S(1)}, u32[]{:S(2)}, u32[]{:S(2)}) async-start(bf16[32,48,128]{2,1,0:T(8,128)(2,1)} %shard_map.137), calls=%async_computation | async-start | bytes 786432 | tf_op jit(solution)/shard_map/all_to_all | solution.py:539
  85.3 4.5 %collective-permute-start.21 = (bf16[6,48,128]{2,1,0:T(8,128)(2,1)S(1)}, bf16[6,48,128]{2,1,0:T(8,128)(2,1)S(1)}, u32[]{:S(2)}, u32[]{:S(2)}) collective-permute-start(bf16[6,48,128]{2,1,0:T(8,128)(2,1)S(1)} %shard_map.138.b0), channel_id=1, source_target_pairs={{0,1},{1,2},{2,3},{3,0},{4,5},{5,6},{6,7},{7,4},{8,9},{9,10},{10,1... | collective-permute-start | bytes 221192 | tf_op jit(solution)/shard_map/ppermute | solution.py:403
  85.6 6.6 %collective-permute-start.22 = (bf16[6,48,128]{2,1,0:T(8,128)(2,1)S(1)}, bf16[6,48,128]{2,1,0:T(8,128)(2,1)S(1)}, u32[]{:S(2)}, u32[]{:S(2)}) collective-permute-start(bf16[6,48,128]{2,1,0:T(8,128)(2,1)S(1)} %shard_map.138.b0), channel_id=1, source_target_pairs={{0,2},{1,3},{2,0},{3,1},{4,6},{5,7},{6,4},{7,5},{8,10},{9,11},{10,... | collective-permute-start | bytes 221192 | tf_op jit(solution)/shard_map/ppermute | solution.py:403
  88.9 3.7 %collective-permute-start.23 = (bf16[6,48,128]{2,1,0:T(8,128)(2,1)S(1)}, bf16[6,48,128]{2,1,0:T(8,128)(2,1)S(1)}, u32[]{:S(2)}, u32[]{:S(2)}) collective-permute-start(bf16[6,48,128]{2,1,0:T(8,128)(2,1)S(1)} %shard_map.138.b0), channel_id=1, source_target_pairs={{0,3},{1,0},{2,1},{3,2},{4,7},{5,4},{6,5},{7,6},{8,11},{9,8},{10,9... | collective-permute-start | bytes 221192 | tf_op jit(solution)/shard_map/ppermute | solution.py:403
  (4 other events, 9.5 us)

commit v4 on v3

--- a/solution.py
+++ b/solution.py
@@ -26,7 +26,6 @@
 JOBS = 4
 ROWS = 176
 PIECE = 48
-SENT = PIECE + 2 * MEL
 flow_steps = 32.0
 norm_eps = 1e-05
 f32 = jnp.float32
@@ -286,7 +285,7 @@
 def second_kernel(
     table, context, noise, valid, gram, wq_s, wv_s, wk_s, o_in, wa_t, wm,
     wo0, ho1, so1, ho2, so2, ho3, so3,
-    v0, v1, v2, v3,
+    tot_out, v0, v1, v2, v3,
     k_s, q_s, v_s, o_s, wr_s, stage, scaled_s, values_s, keys_s,
 ):
     m = lax.axis_index("mp")
@@ -314,14 +313,14 @@
         )
         last = velocity_of(wr_s, o_s, own)
         total = (first + last).astype(bf16)
+        tot_out[q, 0:MEL, :] = total[:, 0:128]
+        tot_out[q, MEL : 2 * MEL, :] = total[:, 128:256]
         vel = last.astype(bf16)
         stage[0:MEL, :] = vel[:, 0:128]
         stage[MEL : 2 * MEL, :] = vel[:, 128:256]
         for k, out in enumerate((v0, v1, v2, v3)):
             quarter = (m + k) & 3
-            out[q, 0:PIECE, :] = stage[pl.ds(pl.multiple_of(quarter * PIECE, 16), PIECE), :]
-            out[q, PIECE : PIECE + MEL, :] = total[:, 0:128]
-            out[q, PIECE + MEL : SENT, :] = total[:, 128:256]
+            out[q] = stage[pl.ds(pl.multiple_of(quarter * PIECE, 16), PIECE), :]
         return carry
 
     lax.fori_loop(0, table[COUNT_AT], job, 0)
@@ -336,7 +335,7 @@
 
                 @pl.when(worker >= 0)
                 def _():
-                    act(pltpu.make_async_copy(a.at[q, 0:PIECE], out.at[worker], sems.at[entry]))
+                    act(pltpu.make_async_copy(a.at[q], out.at[worker], sems.at[entry]))
 
     each(lambda copy: copy.start())
     each(lambda copy: copy.wait())
@@ -353,15 +352,17 @@
         copy.wait()
 
 
-def span_kernel(table, a0, a1, a2, a3, b0, b1, b2, b3, out):
+def span_kernel(table, a0, a1, a2, a3, b, out):
     out[...] = jnp.zeros(out.shape, f32)
-    for i, a in enumerate((a0, a1, a2, a3, b0, b1, b2, b3)):
+    sources = [lambda q, a=a: a[q] for a in (a0, a1, a2, a3)]
+    sources += [lambda q, k=k: b[k * JOBS + q] for k in range(N_MP)]
+    for i, source in enumerate(sources):
         for q in range(JOBS):
             s = table[SLOT_AT + i * JOBS + q]
 
             @pl.when(s >= 0)
             def _():
-                block = a[q, PIECE:SENT, :].astype(f32)
+                block = source(q).astype(f32)
                 off = (s & 3) * BLOCK
                 out[s >> 2, :, pl.ds(pl.multiple_of(off, 128), 128)] = block[0:MEL]
                 out[s >> 2, :, pl.ds(pl.multiple_of(off + 128, 128), 128)] = block[MEL : 2 * MEL]
@@ -460,7 +461,7 @@
 def run_second(table, context, noise, valid, gram, first, wa_t, wm, wo):
     return call(
         second_kernel,
-        (shape((JOBS, SENT, 128), bf16),) * 4,
+        (shape((JOBS, 2 * MEL, 128), bf16),) + (shape((JOBS, PIECE, 128), bf16),) * 4,
         "s" + "v" * 17,
         (table, context, noise, valid, gram, *first, wa_t, wm, *wo),
         scratch=work_shapes()
@@ -525,8 +526,9 @@
     wo = [wo_t]
     for h in out_halves[:-1]:
         wo += [h, to_other(h)]
-    v0, v1, v2, v3 = run_second(table, context, noise, valid, gram, first, wa_t, wm, wo)
+    tot, v0, v1, v2, v3 = run_second(table, context, noise, valid, gram, first, wa_t, wm, wo)
     pieces = [v0] + [to_next(v, k) for k, v in ((1, v1), (2, v2), (3, v3))]
+    totals = gathered(after(tot, *pieces[1:]))
     pieces += [to_other(v) for v in pieces]
     packed = call(
         pack_kernel,
@@ -537,10 +539,6 @@
         out_kinds="h",
     )
     got = lax.all_to_all(packed, "dp", 0, 0, tiled=True)
-    infilled = call(
-        span_kernel, shape((UTT_DEV, MEL, SPAN_MAX), f32), "s" + "v" * 8, (table, *pieces)
-    )
-    table, infilled = lax.optimization_barrier((table, infilled))
     chosen = call(
         select_kernel,
         shape((WORK_DEV, PIECE, 128), bf16),
@@ -550,6 +548,14 @@
         out_kinds="h",
     )
     parts = gathered(chosen)
+    *totals, _ = lax.optimization_barrier((*totals, chosen))
+    infilled = call(
+        span_kernel,
+        shape((UTT_DEV, MEL, SPAN_MAX), f32),
+        "s" + "v" * 5,
+        (table, *totals, to_other(jnp.concatenate(totals, axis=0))),
+    )
+    *parts, infilled = lax.optimization_barrier((*parts, infilled))
     velocity = call(
         final_kernel,
         shape((WORK_DEV, MEL, BLOCK), f32),

time: 94.5 us -> 90.6 us (0.959)
  waiting for transfers between devices: 21.6 us -> 18.1 us
    ppermute x12 -> x15, starting transfers between devices: 17.5 us -> 20.9 us  [to_next(): return lax.ppermute(value, 'mp', [(i, (i + k) % N_MP) for i in range(N_MP)])]
    ppermute x12 -> x13, starting transfers between devices: 17.2 us -> 14.8 us  [to_other(): return lax.ppermute(value, 'dp', [(i, i ^ 1) for i in range(size)])]
    ppermute x12 -> x15, waiting for transfers between devices: 9.52 us -> 7.83 us  [to_next(): return lax.ppermute(value, 'mp', [(i, (i + k) % N_MP) for i in range(N_MP)])]
    all_to_all x1, waiting for transfers between devices: 8.21 us -> 6.64 us  [shards(): got = lax.all_to_all(packed, 'dp', 0, 0, tiled=True)]
    all_to_all x1, starting transfers between devices: 12.9 us -> 11.4 us  [shards(): got = lax.all_to_all(packed, 'dp', 0, 0, tiled=True)]
    ppermute x12 -> x13, waiting for transfers between devices: 3.85 us -> 3.64 us  [to_other(): return lax.ppermute(value, 'dp', [(i, i ^ 1) for i in range(size)])]
  transfers between devices with their start and end apart: 25 -> 29, of which waited for: 14 -> 11; matrix products, arithmetic and copies ran while one was open for 0% -> 0% of each run, Pallas kernels for 10% -> 11%
where the time goes in v4:
time: 90.6 us; the launch traced here: 89.7 us
  starting transfers between devices  47.2 us (52%)
  Pallas kernels  22.3 us (25%)
  waiting for transfers between devices  18.1 us (20%)
  local copies, waits for them, and re-layouts  1.13 us (1%)
    pallas_call x9, Pallas kernels, call(): pl.pallas_call(kernel, out_shape=outs, in_specs=[spec(k) for k in kinds],...  22.3 us
    ppermute x15, starting transfers between devices, to_next(): return lax.ppermute(value, 'mp', [(i, (i + k) % N_MP) for i in range(N_MP)])  20.9 us
    ppermute x13, starting transfers between devices, to_other(): return lax.ppermute(value, 'dp', [(i, i ^ 1) for i in range(size)])  14.8 us
    all_to_all x1, starting transfers between devices, shards(): got = lax.all_to_all(packed, 'dp', 0, 0, tiled=True)  11.4 us
    ppermute x15, waiting for transfers between devices, to_next(): return lax.ppermute(value, 'mp', [(i, (i + k) % N_MP) for i in range(N_MP)])  7.83 us
    all_to_all x1, waiting for transfers between devices, shards(): got = lax.all_to_all(packed, 'dp', 0, 0, tiled=True)  6.64 us
    ppermute x13, waiting for transfers between devices, to_other(): return lax.ppermute(value, 'dp', [(i, i ^ 1) for i in range(size)])  3.64 us
  transfers between devices with their start and end apart: 29, of which 11 were waited for; matrix products, arithmetic and copies ran while one was open for 0% of the time, Pallas kernels for 11%

profile of v4, /device:TPU:1, one launch (start us, length us, event | category | flops | bytes accessed | tf_op | source)
XLA Modules:
  0.0 89.7 jit_solution(7803434346225801030)
XLA Ops:
  0.7 3.1 %shard_map.131 = (bf16[3,176,256]{2,1,0:T(8,128)(2,1)}, bf16[3,176,128]{2,1,0:T(8,128)(2,1)}) custom-call(bf16[160,1024]{1,0:T(8,128)(2,1)} %w_in.3, f32[16,1024]{1,0:T(8,128)} %constant.2.clone.e_rows_h.e_rows, f32[1,1024]{1,0:T(1,128)} %bitcast.7, bf16[3,1024,256]{2,1,0:T(8,128)(2,1)} %bitcast.6), custom_call_target="tpu_custom_call" | custom-call | tf_op jit(solution)/shard_map/pallas_call | solution.py:389
  3.8 1.5 %collective-permute-start = (bf16[4,80,2048]{2,1,0:T(8,128)(2,1)S(1)}, bf16[4,80,2048]{2,1,0:T(8,128)(2,1)S(1)}, u32[]{:S(2)}, u32[]{:S(2)}) collective-permute-start(bf16[4,80,2048]{2,1,0:T(8,128)(2,1)S(1)} %copy-done.1), channel_id=1, source_target_pairs={{0,4},{4,0},{8,12},{12,8},{16,20},{20,16},{24,28},{28,24},{32,36},... | collective-permute-start | bytes 3932168 | tf_op jit(solution)/shard_map/ppermute | solution.py:409
  5.4 1.7 %collective-permute-start.2 = (bf16[3,176,128]{2,1,0:T(8,128)(2,1)}, bf16[3,176,128]{2,1,0:T(8,128)(2,1)S(1)}, u32[]{:S(2)}, u32[]{:S(2)}) collective-permute-start(bf16[3,176,128]{2,1,0:T(8,128)(2,1)} %get-tuple-element.46), channel_id=1, source_target_pairs={{0,1},{1,2},{2,3},{3,0},{4,5},{5,6},{6,7},{7,4},{8,9},{9,10},{10,1... | collective-permute-start | bytes 405512 | tf_op jit(solution)/shard_map/ppermute | solution.py:404
  7.1 3.3 %collective-permute-start.3 = (bf16[3,176,128]{2,1,0:T(8,128)(2,1)}, bf16[3,176,128]{2,1,0:T(8,128)(2,1)S(1)}, u32[]{:S(2)}, u32[]{:S(2)}) collective-permute-start(bf16[3,176,128]{2,1,0:T(8,128)(2,1)} %get-tuple-element.46), channel_id=1, source_target_pairs={{0,2},{1,3},{2,0},{3,1},{4,6},{5,7},{6,4},{7,5},{8,10},{9,11},{10,... | collective-permute-start | bytes 405512 | tf_op jit(solution)/shard_map/ppermute | solution.py:404
  11.2 1.1 %copy-done.2 = bf16[4,80,1024]{2,1,0:T(8,128)(2,1)S(1)} copy-done((bf16[4,80,1024]{2,1,0:T(8,128)(2,1)S(1)}, bf16[4,80,1024]{2,1,0:T(8,128)(2,1)}, u32[]{:S(2)}) %copy-start.2) | copy-done | bytes 655384
  12.3 2.8 %shard_map.132 = (s32[80]{0:T(128)S(1)}, bf16[352,176]{1,0:T(8,128)(2,1)S(1)}, bf16[4,80,512]{2,1,0:T(8,128)(2,1)S(1)}, bf16[4,80,256]{2,1,0:T(8,128)(2,1)S(1)},...) custom-call(s32[512]{0:T(512)S(1)} %copy-done.7, ...), custom_call_target="tpu_custom_call" | custom-call | tf_op jit(solution)/shard_map/pallas_call | solution.py:389
  15.8 1.0 %collective-permute-done.3.hp2 = bf16[3,176,128]{2,1,0:T(8,128)(2,1)S(1)} collective-permute-done((bf16[3,176,128]{2,1,0:T(8,128)(2,1)}, bf16[3,176,128]{2,1,0:T(8,128)(2,1)S(1)}, u32[]{:S(2)}, u32[]{:S(2)}) %collective-permute-start.3) | collective-permute-done | bytes 135200 | tf_op jit(solution)/shard_map/ppermute | solution.py:404
  16.8 1.3 %collective-permute-start.5 = (bf16[3,176,128]{2,1,0:T(8,128)(2,1)S(1)}, bf16[3,176,128]{2,1,0:T(8,128)(2,1)S(1)}, u32[]{:S(2)}, u32[]{:S(2)}) collective-permute-start(bf16[3,176,128]{2,1,0:T(8,128)(2,1)S(1)} %collective-permute-done.2.hp1), channel_id=1, source_target_pairs={{0,4},{4,0},{8,12},{12,8},{16,20},{20,16},{24,28},{28,24},{32,36},... | collective-permute-start | bytes 405512 | tf_op jit(solution)/shard_map/ppermute | solution.py:409
  18.1 0.9 collective-permute-start.8
  19.0 2.1 %collective-permute-start.9 = (bf16[1024,128]{1,0:T(8,128)(2,1)S(1)}, bf16[1024,128]{1,0:T(8,128)(2,1)S(1)}, u32[]{:S(2)}, u32[]{:S(2)}) collective-permute-start(bf16[1024,128]{1,0:T(8,128)(2,1)S(1)} %get-tuple-element.60), channel_id=1, source_target_pairs={{0,2},{1,3},{2,0},{3,1},{4,6},{5,7},{6,4},{7,5},{8,10},{9,11},{10,... | collective-permute-start | bytes 786440 | tf_op jit(solution)/shard_map/ppermute | solution.py:404
  21.1 1.1 %collective-permute-start.10 = (bf16[1024,128]{1,0:T(8,128)(2,1)S(1)}, bf16[1024,128]{1,0:T(8,128)(2,1)S(1)}, u32[]{:S(2)}, u32[]{:S(2)}) collective-permute-start(bf16[1024,128]{1,0:T(8,128)(2,1)S(1)} %get-tuple-element.60), channel_id=1, source_target_pairs={{0,3},{1,0},{2,1},{3,2},{4,7},{5,4},{6,5},{7,6},{8,11},{9,8},{10,9... | collective-permute-start | bytes 786440 | tf_op jit(solution)/shard_map/ppermute | solution.py:404
  22.1 0.8 collective-permute-start.6
  23.0 1.0 %collective-permute-done.6.sp2 = bf16[3,176,128]{2,1,0:T(8,128)(2,1)S(1)} collective-permute-done((bf16[3,176,128]{2,1,0:T(8,128)(2,1)S(1)}, bf16[3,176,128]{2,1,0:T(8,128)(2,1)S(1)}, u32[]{:S(2)}, u32[]{:S(2)}) %collective-permute-start.6) | collective-permute-done | bytes 135200 | tf_op jit(solution)/shard_map/ppermute | solution.py:409
  24.3 4.0 %shard_map.134 = (bf16[1024,176]{1,0:T(8,128)(2,1)S(1)}, bf16[1024,176]{1,0:T(8,128)(2,1)S(1)}, bf16[176,1024]{1,0:T(8,128)(2,1)S(1)}, bf16[4,1200,256]{2,1,0:T(8,128)(2,1)S(1)}) custom-call(s32[80]{0:T(128)S(1)} %get-tuple-element.49.table, f32[4,8,512]{2,1,0:T(8,128)S(1)} %get-tuple-element.52.valid, bf16[4,176,256]{2,1,0:T(8,128)(2,1)S(1)} %get-tuple-element.54.scaled, ...), custom_call_target="tpu_custom_call" | custom-call | tf_op jit(solution)/shard_map/pallas_call | solution.py:389
  28.4 4.8 %collective-permute-done.9.ho2 = bf16[1024,128]{1,0:T(8,128)(2,1)S(1)} collective-permute-done((bf16[1024,128]{1,0:T(8,128)(2,1)S(1)}, bf16[1024,128]{1,0:T(8,128)(2,1)S(1)}, u32[]{:S(2)}, u32[]{:S(2)}) %collective-permute-start.9) | collective-permute-done | bytes 262176 | tf_op jit(solution)/shard_map/ppermute | solution.py:404
  33.2 1.1 %collective-permute-start.11 = (bf16[1024,128]{1,0:T(8,128)(2,1)S(1)}, bf16[1024,128]{1,0:T(8,128)(2,1)S(1)}, u32[]{:S(2)}, u32[]{:S(2)}) collective-permute-start(bf16[1024,128]{1,0:T(8,128)(2,1)S(1)} %collective-permute-done.8.ho1), channel_id=1, source_target_pairs={{0,4},{4,0},{8,12},{12,8},{16,20},{20,16},{24,28},{28,24},{32,36},... | collective-permute-start | bytes 786440 | tf_op jit(solution)/shard_map/ppermute | solution.py:409
  36.2 6.8 %shard_map.135 = (bf16[4,160,128]{2,1,0:T(8,128)(2,1)S(1)}, bf16[4,48,128]{2,1,0:T(8,128)(2,1)S(1)}, bf16[4,48,128]{2,1,0:T(8,128)(2,1)S(1)}, bf16[4,48,128]{2,1,0:T(8,128)(2,1)S(1)}, bf16[4,48,128]{2,1,0:T(8,128)(2,1)S(1)}) custom-call(s32[80]{0:T(128)S(1)} %get-tuple-element.49.table, bf16[4,80,512]{2,1,0:T(8,128)(2,1)S(1)} %get-tuple-element.50.context, ...), custom_call_target="tpu_custom_call" | custom-call | tf_op jit(solution)/shard_map/pallas_call | solution.py:389
  43.0 1.4 %collective-permute-start.14 = (bf16[4,48,128]{2,1,0:T(8,128)(2,1)S(1)}, bf16[4,48,128]{2,1,0:T(8,128)(2,1)S(1)}, u32[]{:S(2)}, u32[]{:S(2)}) collective-permute-start(bf16[4,48,128]{2,1,0:T(8,128)(2,1)S(1)} %get-tuple-element.76), channel_id=1, source_target_pairs={{0,1},{1,2},{2,3},{3,0},{4,5},{5,6},{6,7},{7,4},{8,9},{9,10},{10,1... | collective-permute-start | bytes 147464 | tf_op jit(solution)/shard_map/ppermute | solution.py:404
  44.3 2.2 %collective-permute-start.15 = (bf16[4,48,128]{2,1,0:T(8,128)(2,1)S(1)}, bf16[4,48,128]{2,1,0:T(8,128)(2,1)S(1)}, u32[]{:S(2)}, u32[]{:S(2)}) collective-permute-start(bf16[4,48,128]{2,1,0:T(8,128)(2,1)S(1)} %get-tuple-element.77), channel_id=1, source_target_pairs={{0,2},{1,3},{2,0},{3,1},{4,6},{5,7},{6,4},{7,5},{8,10},{9,11},{10,... | collective-permute-start | bytes 147464 | tf_op jit(solution)/shard_map/ppermute | solution.py:404
  47.0 4.9 %collective-permute-start.17 = (bf16[4,48,128]{2,1,0:T(8,128)(2,1)S(1)}, bf16[4,48,128]{2,1,0:T(8,128)(2,1)S(1)}, u32[]{:S(2)}, u32[]{:S(2)}) collective-permute-start(bf16[4,48,128]{2,1,0:T(8,128)(2,1)S(1)} %get-tuple-element.75.a0), channel_id=1, source_target_pairs={{0,4},{4,0},{8,12},{12,8},{16,20},{20,16},{24,28},{28,24},{32,36},... | collective-permute-start | bytes 147464 | tf_op jit(solution)/shard_map/ppermute | solution.py:409
  51.9 2.6 %collective-permute-start.18 = (bf16[4,48,128]{2,1,0:T(8,128)(2,1)S(1)}, bf16[4,48,128]{2,1,0:T(8,128)(2,1)S(1)}, u32[]{:S(2)}, u32[]{:S(2)}) collective-permute-start(bf16[4,48,128]{2,1,0:T(8,128)(2,1)S(1)} %collective-permute-done.14.a1), channel_id=1, source_target_pairs={{0,4},{4,0},{8,12},{12,8},{16,20},{20,16},{24,28},{28,24},{32,36},... | collective-permute-start | bytes 147464 | tf_op jit(solution)/shard_map/ppermute | solution.py:409
  54.5 0.8 collective-permute-start.20
  56.3 1.5 %shard_map.136 = bf16[32,48,128]{2,1,0:T(8,128)(2,1)} custom-call(s32[80]{0:T(128)S(1)} %get-tuple-element.49.table, bf16[4,48,128]{2,1,0:T(8,128)(2,1)S(1)} %get-tuple-element.75.a0, bf16[4,48,128]{2,1,0:T(8,128)(2,1)S(1)} %collective-permute-done.14.a1, bf16[4,48,128]{2,1,0:T(8,128)(2,1)S(1)} %collective-permute-done.15.a2, ...), custom_call_target="tpu_custom_call" | custom-call | tf_op jit(solution)/shard_map/pallas_call | solution.py:389
  57.7 11.4 %all-to-all-start = ((bf16[32,48,128]{2,1,0:T(8,128)(2,1)}), bf16[32,48,128]{2,1,0:T(8,128)(2,1)S(1)}, u32[]{:S(2)}, u32[]{:S(2)}) async-start(bf16[32,48,128]{2,1,0:T(8,128)(2,1)} %shard_map.136), calls=%async_computation | async-start | bytes 786432 | tf_op jit(solution)/shard_map/all_to_all | solution.py:541
  69.3 2.6 %collective-permute-start.25 = (bf16[4,160,128]{2,1,0:T(8,128)(2,1)S(1)}, bf16[4,160,128]{2,1,0:T(8,128)(2,1)S(1)}, u32[]{:S(2)}, u32[]{:S(2)}) collective-permute-start(bf16[4,160,128]{2,1,0:T(8,128)(2,1)S(1)} %get-tuple-element.81.a0), channel_id=1, source_target_pairs={{0,2},{1,3},{2,0},{3,1},{4,6},{5,7},{6,4},{7,5},{8,10},{9,11},{10,... | collective-permute-start | bytes 491528 | tf_op jit(solution)/shard_map/ppermute | solution.py:404
  71.9 0.8 collective-permute-start.26
  72.7 6.6 %all-to-all-done.got = bf16[32,48,128]{2,1,0:T(8,128)(2,1)S(1)} async-done(((bf16[32,48,128]{2,1,0:T(8,128)(2,1)}), bf16[32,48,128]{2,1,0:T(8,128)(2,1)S(1)}, u32[]{:S(2)}, u32[]{:S(2)}) %all-to-all-start) | async-done | bytes 393248 | tf_op jit(solution)/shard_map/all_to_all | solution.py:541
  80.2 1.2 %collective-permute-start.27 = (bf16[16,160,128]{2,1,0:T(8,128)(2,1)S(1)}, bf16[16,160,128]{2,1,0:T(8,128)(2,1)S(1)}, u32[]{:S(2)}, u32[]{:S(2)}) collective-permute-start(bf16[16,160,128]{2,1,0:T(8,128)(2,1)S(1)} %pad_maximum_fusion), channel_id=1, source_target_pairs={{0,4},{4,0},{8,12},{12,8},{16,20},{20,16},{24,28},{28,24},{32,36},... | collective-permute-start | bytes 1966088 | tf_op jit(solution)/shard_map/ppermute | solution.py:409
  82.1 2.8 %collective-permute-start.22 = (bf16[6,48,128]{2,1,0:T(8,128)(2,1)S(1)}, bf16[6,48,128]{2,1,0:T(8,128)(2,1)S(1)}, u32[]{:S(2)}, u32[]{:S(2)}) collective-permute-start(bf16[6,48,128]{2,1,0:T(8,128)(2,1)S(1)} %shard_map.137.b0), channel_id=1, source_target_pairs={{0,2},{1,3},{2,0},{3,1},{4,6},{5,7},{6,4},{7,5},{8,10},{9,11},{10,... | collective-permute-start | bytes 221192 | tf_op jit(solution)/shard_map/ppermute | solution.py:404
  84.9 2.0 %shard_map.138 = f32[4,80,1024]{2,1,0:T(8,128)} custom-call(s32[80]{0:T(128)S(1)} %get-tuple-element.49.table, bf16[4,160,128]{2,1,0:T(8,128)(2,1)S(1)} %get-tuple-element.81.a0, bf16[4,160,128]{2,1,0:T(8,128)(2,1)S(1)} %collective-permute-done.24.a1, bf16[4,160,128]{2,1,0:T(8,128)(2,1)S(1)} %collective-permute-done.25.a2, ...), custom_call_target="tpu_custom_call" | custom-call | tf_op jit(solution)/shard_map/pallas_call | solution.py:389
  86.9 2.0 %collective-permute-done.22.b2 = bf16[6,48,128]{2,1,0:T(8,128)(2,1)S(1)} collective-permute-done((bf16[6,48,128]{2,1,0:T(8,128)(2,1)S(1)}, bf16[6,48,128]{2,1,0:T(8,128)(2,1)S(1)}, u32[]{:S(2)}, u32[]{:S(2)}) %collective-permute-start.22) | collective-permute-done | bytes 73760 | tf_op jit(solution)/shard_map/ppermute | solution.py:404
  88.9 0.8 shard_map.139
  (58 shorter events, 6.9 us)
Async XLA Ops:
  0.6 10.6 %copy-start.3 = (f32[16,1024]{1,0:T(8,128)S(1)}, f32[16,1024]{1,0:T(8,128)}, u32[]{:S(2)}) copy-start(f32[16,1024]{1,0:T(8,128)} %constant.2.clone.e_rows_h.e_rows) | copy-start | bytes 196612
  0.6 10.6 %copy-start = (bf16[160,1024]{1,0:T(8,128)(2,1)S(1)}, bf16[160,1024]{1,0:T(8,128)(2,1)}, u32[]{:S(2)}) copy-start(bf16[160,1024]{1,0:T(8,128)(2,1)} %w_in.3) | copy-start | bytes 983044
  3.8 7.4 %collective-permute-start = (bf16[4,80,2048]{2,1,0:T(8,128)(2,1)S(1)}, bf16[4,80,2048]{2,1,0:T(8,128)(2,1)S(1)}, u32[]{:S(2)}, u32[]{:S(2)}) collective-permute-start(bf16[4,80,2048]{2,1,0:T(8,128)(2,1)S(1)} %copy-done.1), channel_id=1, source_target_pairs={{0,4},{4,0},{8,12},{12,8},{16,20},{20,16},{24,28},{28,24},{32,36},... | collective-permute-start | bytes 3932168 | tf_op jit(solution)/shard_map/ppermute | solution.py:409
  5.3 5.8 %collective-permute-start.1 = (bf16[4,80,1024]{2,1,0:T(8,128)(2,1)}, bf16[4,80,1024]{2,1,0:T(8,128)(2,1)S(1)}, u32[]{:S(2)}, u32[]{:S(2)}) collective-permute-start(bf16[4,80,1024]{2,1,0:T(8,128)(2,1)} %noise_a.1), channel_id=1, source_target_pairs={{0,4},{4,0},{8,12},{12,8},{16,20},{20,16},{24,28},{28,24},{32,36},... | collective-permute-start | bytes 1966088 | tf_op jit(solution)/shard_map/ppermute | solution.py:409
  5.4 10.4 %collective-permute-start.2 = (bf16[3,176,128]{2,1,0:T(8,128)(2,1)}, bf16[3,176,128]{2,1,0:T(8,128)(2,1)S(1)}, u32[]{:S(2)}, u32[]{:S(2)}) collective-permute-start(bf16[3,176,128]{2,1,0:T(8,128)(2,1)} %get-tuple-element.46), channel_id=1, source_target_pairs={{0,1},{1,2},{2,3},{3,0},{4,5},{5,6},{6,7},{7,4},{8,9},{9,10},{10,1... | collective-permute-start | bytes 405512 | tf_op jit(solution)/shard_map/ppermute | solution.py:404
  7.1 9.7 %collective-permute-start.3 = (bf16[3,176,128]{2,1,0:T(8,128)(2,1)}, bf16[3,176,128]{2,1,0:T(8,128)(2,1)S(1)}, u32[]{:S(2)}, u32[]{:S(2)}) collective-permute-start(bf16[3,176,128]{2,1,0:T(8,128)(2,1)} %get-tuple-element.46), channel_id=1, source_target_pairs={{0,2},{1,3},{2,0},{3,1},{4,6},{5,7},{6,4},{7,5},{8,10},{9,11},{10,... | collective-permute-start | bytes 405512 | tf_op jit(solution)/shard_map/ppermute | solution.py:404
  10.5 6.4 %collective-permute-start.4 = (bf16[3,176,128]{2,1,0:T(8,128)(2,1)}, bf16[3,176,128]{2,1,0:T(8,128)(2,1)S(1)}, u32[]{:S(2)}, u32[]{:S(2)}) collective-permute-start(bf16[3,176,128]{2,1,0:T(8,128)(2,1)} %get-tuple-element.46), channel_id=1, source_target_pairs={{0,3},{1,0},{2,1},{3,2},{4,7},{5,4},{6,5},{7,6},{8,11},{9,8},{10,9... | collective-permute-start | bytes 405512 | tf_op jit(solution)/shard_map/ppermute | solution.py:404
  12.3 12.0 %copy-start.5 = (bf16[3,176,256]{2,1,0:T(8,128)(2,1)S(1)}, bf16[3,176,256]{2,1,0:T(8,128)(2,1)}, u32[]{:S(2)}) copy-start(bf16[3,176,256]{2,1,0:T(8,128)(2,1)} %get-tuple-element.58.wp0) | copy-start | bytes 811012
  16.8 6.1 %collective-permute-start.5 = (bf16[3,176,128]{2,1,0:T(8,128)(2,1)S(1)}, bf16[3,176,128]{2,1,0:T(8,128)(2,1)S(1)}, u32[]{:S(2)}, u32[]{:S(2)}) collective-permute-start(bf16[3,176,128]{2,1,0:T(8,128)(2,1)S(1)} %collective-permute-done.2.hp1), channel_id=1, source_target_pairs={{0,4},{4,0},{8,12},{12,8},{16,20},{20,16},{24,28},{28,24},{32,36},... | collective-permute-start | bytes 405512 | tf_op jit(solution)/shard_map/ppermute | solution.py:409
  18.1 10.3 %collective-permute-start.8 = (bf16[1024,128]{1,0:T(8,128)(2,1)S(1)}, bf16[1024,128]{1,0:T(8,128)(2,1)S(1)}, u32[]{:S(2)}, u32[]{:S(2)}) collective-permute-start(bf16[1024,128]{1,0:T(8,128)(2,1)S(1)} %get-tuple-element.60), channel_id=1, source_target_pairs={{0,1},{1,2},{2,3},{3,0},{4,5},{5,6},{6,7},{7,4},{8,9},{9,10},{10,1... | collective-permute-start | bytes 786440 | tf_op jit(solution)/shard_map/ppermute | solution.py:404
  19.0 14.2 %collective-permute-start.9 = (bf16[1024,128]{1,0:T(8,128)(2,1)S(1)}, bf16[1024,128]{1,0:T(8,128)(2,1)S(1)}, u32[]{:S(2)}, u32[]{:S(2)}) collective-permute-start(bf16[1024,128]{1,0:T(8,128)(2,1)S(1)} %get-tuple-element.60), channel_id=1, source_target_pairs={{0,2},{1,3},{2,0},{3,1},{4,6},{5,7},{6,4},{7,5},{8,10},{9,11},{10,... | collective-permute-start | bytes 786440 | tf_op jit(solution)/shard_map/ppermute | solution.py:404
  21.1 12.1 %collective-permute-start.10 = (bf16[1024,128]{1,0:T(8,128)(2,1)S(1)}, bf16[1024,128]{1,0:T(8,128)(2,1)S(1)}, u32[]{:S(2)}, u32[]{:S(2)}) collective-permute-start(bf16[1024,128]{1,0:T(8,128)(2,1)S(1)} %get-tuple-element.60), channel_id=1, source_target_pairs={{0,3},{1,0},{2,1},{3,2},{4,7},{5,4},{6,5},{7,6},{8,11},{9,8},{10,9... | collective-permute-start | bytes 786440 | tf_op jit(solution)/shard_map/ppermute | solution.py:404
  22.1 1.8 %collective-permute-start.6 = (bf16[3,176,128]{2,1,0:T(8,128)(2,1)S(1)}, bf16[3,176,128]{2,1,0:T(8,128)(2,1)S(1)}, u32[]{:S(2)}, u32[]{:S(2)}) collective-permute-start(bf16[3,176,128]{2,1,0:T(8,128)(2,1)S(1)} %collective-permute-done.3.hp2), channel_id=1, source_target_pairs={{0,4},{4,0},{8,12},{12,8},{16,20},{20,16},{24,28},{28,24},{32,36},... | collective-permute-start | bytes 405512 | tf_op jit(solution)/shard_map/ppermute | solution.py:409
  23.0 1.4 %collective-permute-start.7 = (bf16[3,176,128]{2,1,0:T(8,128)(2,1)S(1)}, bf16[3,176,128]{2,1,0:T(8,128)(2,1)S(1)}, u32[]{:S(2)}, u32[]{:S(2)}) collective-permute-start(bf16[3,176,128]{2,1,0:T(8,128)(2,1)S(1)} %collective-permute-done.4.hp3), channel_id=1, source_target_pairs={{0,4},{4,0},{8,12},{12,8},{16,20},{20,16},{24,28},{28,24},{32,36},... | collective-permute-start | bytes 405512 | tf_op jit(solution)/shard_map/ppermute | solution.py:409
  33.2 2.3 %collective-permute-start.11 = (bf16[1024,128]{1,0:T(8,128)(2,1)S(1)}, bf16[1024,128]{1,0:T(8,128)(2,1)S(1)}, u32[]{:S(2)}, u32[]{:S(2)}) collective-permute-start(bf16[1024,128]{1,0:T(8,128)(2,1)S(1)} %collective-permute-done.8.ho1), channel_id=1, source_target_pairs={{0,4},{4,0},{8,12},{12,8},{16,20},{20,16},{24,28},{28,24},{32,36},... | collective-permute-start | bytes 786440 | tf_op jit(solution)/shard_map/ppermute | solution.py:409
  34.3 1.5 %collective-permute-start.12 = (bf16[1024,128]{1,0:T(8,128)(2,1)S(1)}, bf16[1024,128]{1,0:T(8,128)(2,1)S(1)}, u32[]{:S(2)}, u32[]{:S(2)}) collective-permute-start(bf16[1024,128]{1,0:T(8,128)(2,1)S(1)} %collective-permute-done.9.ho2), channel_id=1, source_target_pairs={{0,4},{4,0},{8,12},{12,8},{16,20},{20,16},{24,28},{28,24},{32,36},... | collective-permute-start | bytes 786440 | tf_op jit(solution)/shard_map/ppermute | solution.py:409
  34.3 1.9 %collective-permute-start.13 = (bf16[1024,128]{1,0:T(8,128)(2,1)S(1)}, bf16[1024,128]{1,0:T(8,128)(2,1)S(1)}, u32[]{:S(2)}, u32[]{:S(2)}) collective-permute-start(bf16[1024,128]{1,0:T(8,128)(2,1)S(1)} %collective-permute-done.10.ho3), channel_id=1, source_target_pairs={{0,4},{4,0},{8,12},{12,8},{16,20},{20,16},{24,28},{28,24},{32,36},... | collective-permute-start | bytes 786440 | tf_op jit(solution)/shard_map/ppermute | solution.py:409
  43.0 9.0 %collective-permute-start.14 = (bf16[4,48,128]{2,1,0:T(8,128)(2,1)S(1)}, bf16[4,48,128]{2,1,0:T(8,128)(2,1)S(1)}, u32[]{:S(2)}, u32[]{:S(2)}) collective-permute-start(bf16[4,48,128]{2,1,0:T(8,128)(2,1)S(1)} %get-tuple-element.76), channel_id=1, source_target_pairs={{0,1},{1,2},{2,3},{3,0},{4,5},{5,6},{6,7},{7,4},{8,9},{9,10},{10,1... | collective-permute-start | bytes 147464 | tf_op jit(solution)/shard_map/ppermute | solution.py:404
  44.3 10.2 %collective-permute-start.15 = (bf16[4,48,128]{2,1,0:T(8,128)(2,1)S(1)}, bf16[4,48,128]{2,1,0:T(8,128)(2,1)S(1)}, u32[]{:S(2)}, u32[]{:S(2)}) collective-permute-start(bf16[4,48,128]{2,1,0:T(8,128)(2,1)S(1)} %get-tuple-element.77), channel_id=1, source_target_pairs={{0,2},{1,3},{2,0},{3,1},{4,6},{5,7},{6,4},{7,5},{8,10},{9,11},{10,... | collective-permute-start | bytes 147464 | tf_op jit(solution)/shard_map/ppermute | solution.py:404
  46.6 8.0 %collective-permute-start.16 = (bf16[4,48,128]{2,1,0:T(8,128)(2,1)S(1)}, bf16[4,48,128]{2,1,0:T(8,128)(2,1)S(1)}, u32[]{:S(2)}, u32[]{:S(2)}) collective-permute-start(bf16[4,48,128]{2,1,0:T(8,128)(2,1)S(1)} %get-tuple-element.78), channel_id=1, source_target_pairs={{0,3},{1,0},{2,1},{3,2},{4,7},{5,4},{6,5},{7,6},{8,11},{9,8},{10,9... | collective-permute-start | bytes 147464 | tf_op jit(solution)/shard_map/ppermute | solution.py:404
  47.0 8.3 %collective-permute-start.17 = (bf16[4,48,128]{2,1,0:T(8,128)(2,1)S(1)}, bf16[4,48,128]{2,1,0:T(8,128)(2,1)S(1)}, u32[]{:S(2)}, u32[]{:S(2)}) collective-permute-start(bf16[4,48,128]{2,1,0:T(8,128)(2,1)S(1)} %get-tuple-element.75.a0), channel_id=1, source_target_pairs={{0,4},{4,0},{8,12},{12,8},{16,20},{20,16},{24,28},{28,24},{32,36},... | collective-permute-start | bytes 147464 | tf_op jit(solution)/shard_map/ppermute | solution.py:409
  51.9 3.5 %collective-permute-start.18 = (bf16[4,48,128]{2,1,0:T(8,128)(2,1)S(1)}, bf16[4,48,128]{2,1,0:T(8,128)(2,1)S(1)}, u32[]{:S(2)}, u32[]{:S(2)}) collective-permute-start(bf16[4,48,128]{2,1,0:T(8,128)(2,1)S(1)} %collective-permute-done.14.a1), channel_id=1, source_target_pairs={{0,4},{4,0},{8,12},{12,8},{16,20},{20,16},{24,28},{28,24},{32,36},... | collective-permute-start | bytes 147464 | tf_op jit(solution)/shard_map/ppermute | solution.py:409
  54.5 1.2 %collective-permute-start.19 = (bf16[4,48,128]{2,1,0:T(8,128)(2,1)S(1)}, bf16[4,48,128]{2,1,0:T(8,128)(2,1)S(1)}, u32[]{:S(2)}, u32[]{:S(2)}) collective-permute-start(bf16[4,48,128]{2,1,0:T(8,128)(2,1)S(1)} %collective-permute-done.15.a2), channel_id=1, source_target_pairs={{0,4},{4,0},{8,12},{12,8},{16,20},{20,16},{24,28},{28,24},{32,36},... | collective-permute-start | bytes 147464 | tf_op jit(solution)/shard_map/ppermute | solution.py:409
  54.5 1.7 %collective-permute-start.20 = (bf16[4,48,128]{2,1,0:T(8,128)(2,1)S(1)}, bf16[4,48,128]{2,1,0:T(8,128)(2,1)S(1)}, u32[]{:S(2)}, u32[]{:S(2)}) collective-permute-start(bf16[4,48,128]{2,1,0:T(8,128)(2,1)S(1)} %collective-permute-done.16.a3), channel_id=1, source_target_pairs={{0,4},{4,0},{8,12},{12,8},{16,20},{20,16},{24,28},{28,24},{32,36},... | collective-permute-start | bytes 147464 | tf_op jit(solution)/shard_map/ppermute | solution.py:409
  57.7 21.6 %all-to-all-start = ((bf16[32,48,128]{2,1,0:T(8,128)(2,1)}), bf16[32,48,128]{2,1,0:T(8,128)(2,1)S(1)}, u32[]{:S(2)}, u32[]{:S(2)}) async-start(bf16[32,48,128]{2,1,0:T(8,128)(2,1)} %shard_map.136), calls=%async_computation | async-start | bytes 786432 | tf_op jit(solution)/shard_map/all_to_all | solution.py:541
  69.2 10.9 %collective-permute-start.24 = (bf16[4,160,128]{2,1,0:T(8,128)(2,1)S(1)}, bf16[4,160,128]{2,1,0:T(8,128)(2,1)S(1)}, u32[]{:S(2)}, u32[]{:S(2)}) collective-permute-start(bf16[4,160,128]{2,1,0:T(8,128)(2,1)S(1)} %get-tuple-element.81.a0), channel_id=1, source_target_pairs={{0,1},{1,2},{2,3},{3,0},{4,5},{5,6},{6,7},{7,4},{8,9},{9,10},{10,1... | collective-permute-start | bytes 491528 | tf_op jit(solution)/shard_map/ppermute | solution.py:404
  69.3 10.8 %collective-permute-start.25 = (bf16[4,160,128]{2,1,0:T(8,128)(2,1)S(1)}, bf16[4,160,128]{2,1,0:T(8,128)(2,1)S(1)}, u32[]{:S(2)}, u32[]{:S(2)}) collective-permute-start(bf16[4,160,128]{2,1,0:T(8,128)(2,1)S(1)} %get-tuple-element.81.a0), channel_id=1, source_target_pairs={{0,2},{1,3},{2,0},{3,1},{4,6},{5,7},{6,4},{7,5},{8,10},{9,11},{10,... | collective-permute-start | bytes 491528 | tf_op jit(solution)/shard_map/ppermute | solution.py:404
  71.9 8.2 %collective-permute-start.26 = (bf16[4,160,128]{2,1,0:T(8,128)(2,1)S(1)}, bf16[4,160,128]{2,1,0:T(8,128)(2,1)S(1)}, u32[]{:S(2)}, u32[]{:S(2)}) collective-permute-start(bf16[4,160,128]{2,1,0:T(8,128)(2,1)S(1)} %get-tuple-element.81.a0), channel_id=1, source_target_pairs={{0,3},{1,0},{2,1},{3,2},{4,7},{5,4},{6,5},{7,6},{8,11},{9,8},{10,9... | collective-permute-start | bytes 491528 | tf_op jit(solution)/shard_map/ppermute | solution.py:404
  80.2 4.7 %collective-permute-start.27 = (bf16[16,160,128]{2,1,0:T(8,128)(2,1)S(1)}, bf16[16,160,128]{2,1,0:T(8,128)(2,1)S(1)}, u32[]{:S(2)}, u32[]{:S(2)}) collective-permute-start(bf16[16,160,128]{2,1,0:T(8,128)(2,1)S(1)} %pad_maximum_fusion), channel_id=1, source_target_pairs={{0,4},{4,0},{8,12},{12,8},{16,20},{20,16},{24,28},{28,24},{32,36},... | collective-permute-start | bytes 1966088 | tf_op jit(solution)/shard_map/ppermute | solution.py:409
  81.4 5.5 %collective-permute-start.21 = (bf16[6,48,128]{2,1,0:T(8,128)(2,1)S(1)}, bf16[6,48,128]{2,1,0:T(8,128)(2,1)S(1)}, u32[]{:S(2)}, u32[]{:S(2)}) collective-permute-start(bf16[6,48,128]{2,1,0:T(8,128)(2,1)S(1)} %shard_map.137.b0), channel_id=1, source_target_pairs={{0,1},{1,2},{2,3},{3,0},{4,5},{5,6},{6,7},{7,4},{8,9},{9,10},{10,1... | collective-permute-start | bytes 221192 | tf_op jit(solution)/shard_map/ppermute | solution.py:404
  82.1 6.7 %collective-permute-start.22 = (bf16[6,48,128]{2,1,0:T(8,128)(2,1)S(1)}, bf16[6,48,128]{2,1,0:T(8,128)(2,1)S(1)}, u32[]{:S(2)}, u32[]{:S(2)}) collective-permute-start(bf16[6,48,128]{2,1,0:T(8,128)(2,1)S(1)} %shard_map.137.b0), channel_id=1, source_target_pairs={{0,2},{1,3},{2,0},{3,1},{4,6},{5,7},{6,4},{7,5},{8,10},{9,11},{10,... | collective-permute-start | bytes 221192 | tf_op jit(solution)/shard_map/ppermute | solution.py:404
  84.9 3.9 %collective-permute-start.23 = (bf16[6,48,128]{2,1,0:T(8,128)(2,1)S(1)}, bf16[6,48,128]{2,1,0:T(8,128)(2,1)S(1)}, u32[]{:S(2)}, u32[]{:S(2)}) collective-permute-start(bf16[6,48,128]{2,1,0:T(8,128)(2,1)S(1)} %shard_map.137.b0), channel_id=1, source_target_pairs={{0,3},{1,0},{2,1},{3,2},{4,7},{5,4},{6,5},{7,6},{8,11},{9,8},{10,9... | collective-permute-start | bytes 221192 | tf_op jit(solution)/shard_map/ppermute | solution.py:404
  (8 other events, 44.3 us)

commit v5 on v4

--- a/solution.py
+++ b/solution.py
@@ -244,11 +244,16 @@
 
 
 def velocity_of(wr_s, o, own):
-    v = jnp.dot(wr_s[D : D + MEL, :], o[...], preferred_element_type=f32)
     squares = jnp.zeros((8, BLOCK), f32)
     part = D // 4
+    v = None
     for i in range(4):
-        r = jnp.dot(wr_s[part * i : part * i + part, :], o[...], preferred_element_type=f32)
+        last = i == 3
+        rows = slice(part * i, D + MEL if last else part * i + part)
+        r = jnp.dot(wr_s[rows, :], o[...], preferred_element_type=f32)
+        if last:
+            v = r[part:]
+            r = r[0:part]
         squares = squares + jnp.sum((r * r).reshape(part // 8, 8, BLOCK), axis=0)
     var = jnp.sum(squares, axis=0, keepdims=True) * (1.0 / D)
     return jnp.where(own, v * lax.rsqrt(var + norm_eps), 0.0)

time: 90.6 us -> 90 us (level)
  Pallas kernels: 22.3 us -> 31.1 us
  starting transfers between devices: 47.2 us -> 41.9 us
  waiting for transfers between devices: 18.1 us -> 14.9 us
    pallas_call x9, Pallas kernels: 22.3 us -> 31.1 us  [call(): pl.pallas_call(kernel, out_shape=outs, in_specs=[spec(k) for k in kinds],...]
    ppermute x13, starting transfers between devices: 14.8 us -> 10.7 us  [to_other(): return lax.ppermute(value, 'dp', [(i, i ^ 1) for i in range(size)])]
    ppermute x15, waiting for transfers between devices: 7.83 us -> 4.64 us  [to_next(): return lax.ppermute(value, 'mp', [(i, (i + k) % N_MP) for i in range(N_MP)])]
    all_to_all x1, starting transfers between devices: 11.4 us -> 10.5 us  [shards(): got = lax.all_to_all(packed, 'dp', 0, 0, tiled=True)]
  transfers between devices with their start and end apart: 29 -> 29, of which waited for: 11 -> 11; matrix products, arithmetic and copies ran while one was open for 0% -> 0% of each run, Pallas kernels for 11% -> 15%
where the time goes in v5:
time: 90 us
  starting transfers between devices  41.9 us (47%)
  Pallas kernels  31.1 us (35%)
  waiting for transfers between devices  14.9 us (17%)
  local copies, waits for them, and re-layouts  1.13 us (1%)
  between operations  0.9 us (1%)
    pallas_call x9, Pallas kernels, call(): pl.pallas_call(kernel, out_shape=outs, in_specs=[spec(k) for k in kinds],...  31.1 us
    ppermute x15, starting transfers between devices, to_next(): return lax.ppermute(value, 'mp', [(i, (i + k) % N_MP) for i in range(N_MP)])  20.7 us
    ppermute x13, starting transfers between devices, to_other(): return lax.ppermute(value, 'dp', [(i, i ^ 1) for i in range(size)])  10.7 us
    all_to_all x1, starting transfers between devices, shards(): got = lax.all_to_all(packed, 'dp', 0, 0, tiled=True)  10.5 us
    all_to_all x1, waiting for transfers between devices, shards(): got = lax.all_to_all(packed, 'dp', 0, 0, tiled=True)  6.64 us
    ppermute x15, waiting for transfers between devices, to_next(): return lax.ppermute(value, 'mp', [(i, (i + k) % N_MP) for i in range(N_MP)])  4.64 us
    ppermute x13, waiting for transfers between devices, to_other(): return lax.ppermute(value, 'dp', [(i, i ^ 1) for i in range(size)])  3.64 us
  transfers between devices with their start and end apart: 29, of which 11 were waited for; matrix products, arithmetic and copies ran while one was open for 0% of the time, Pallas kernels for 15%

profile of v5, /device:TPU:1, one launch (start us, length us, event | category | flops | bytes accessed | tf_op | source)
XLA Modules:
  0.0 90.0 jit_solution(6008212003925663584)
XLA Ops:
  0.7 3.1 %shard_map.131 = (bf16[3,176,256]{2,1,0:T(8,128)(2,1)}, bf16[3,176,128]{2,1,0:T(8,128)(2,1)}) custom-call(bf16[160,1024]{1,0:T(8,128)(2,1)} %w_in.3, f32[16,1024]{1,0:T(8,128)} %constant.2.clone.e_rows_h.e_rows, f32[1,1024]{1,0:T(1,128)} %bitcast.7, bf16[3,1024,256]{2,1,0:T(8,128)(2,1)} %bitcast.6), custom_call_target="tpu_custom_call" | custom-call | tf_op jit(solution)/shard_map/pallas_call | solution.py:394
  3.8 1.5 %collective-permute-start = (bf16[4,80,2048]{2,1,0:T(8,128)(2,1)S(1)}, bf16[4,80,2048]{2,1,0:T(8,128)(2,1)S(1)}, u32[]{:S(2)}, u32[]{:S(2)}) collective-permute-start(bf16[4,80,2048]{2,1,0:T(8,128)(2,1)S(1)} %copy-done.1), channel_id=1, source_target_pairs={{0,4},{4,0},{8,12},{12,8},{16,20},{20,16},{24,28},{28,24},{32,36},... | collective-permute-start | bytes 3932168 | tf_op jit(solution)/shard_map/ppermute | solution.py:414
  5.4 1.7 %collective-permute-start.2 = (bf16[3,176,128]{2,1,0:T(8,128)(2,1)}, bf16[3,176,128]{2,1,0:T(8,128)(2,1)S(1)}, u32[]{:S(2)}, u32[]{:S(2)}) collective-permute-start(bf16[3,176,128]{2,1,0:T(8,128)(2,1)} %get-tuple-element.46), channel_id=1, source_target_pairs={{0,1},{1,2},{2,3},{3,0},{4,5},{5,6},{6,7},{7,4},{8,9},{9,10},{10,1... | collective-permute-start | bytes 405512 | tf_op jit(solution)/shard_map/ppermute | solution.py:409
  7.1 3.3 %collective-permute-start.3 = (bf16[3,176,128]{2,1,0:T(8,128)(2,1)}, bf16[3,176,128]{2,1,0:T(8,128)(2,1)S(1)}, u32[]{:S(2)}, u32[]{:S(2)}) collective-permute-start(bf16[3,176,128]{2,1,0:T(8,128)(2,1)} %get-tuple-element.46), channel_id=1, source_target_pairs={{0,2},{1,3},{2,0},{3,1},{4,6},{5,7},{6,4},{7,5},{8,10},{9,11},{10,... | collective-permute-start | bytes 405512 | tf_op jit(solution)/shard_map/ppermute | solution.py:409
  11.2 1.1 %copy-done.2 = bf16[4,80,1024]{2,1,0:T(8,128)(2,1)S(1)} copy-done((bf16[4,80,1024]{2,1,0:T(8,128)(2,1)S(1)}, bf16[4,80,1024]{2,1,0:T(8,128)(2,1)}, u32[]{:S(2)}) %copy-start.2) | copy-done | bytes 655384
  12.3 3.4 %shard_map.132 = (s32[80]{0:T(128)S(1)}, bf16[352,176]{1,0:T(8,128)(2,1)S(1)}, bf16[4,80,512]{2,1,0:T(8,128)(2,1)S(1)}, bf16[4,80,256]{2,1,0:T(8,128)(2,1)S(1)},...) custom-call(s32[512]{0:T(512)S(1)} %copy-done.7, ...), custom_call_target="tpu_custom_call" | custom-call | tf_op jit(solution)/shard_map/pallas_call | solution.py:394
  16.8 1.3 %collective-permute-start.5 = (bf16[3,176,128]{2,1,0:T(8,128)(2,1)S(1)}, bf16[3,176,128]{2,1,0:T(8,128)(2,1)S(1)}, u32[]{:S(2)}, u32[]{:S(2)}) collective-permute-start(bf16[3,176,128]{2,1,0:T(8,128)(2,1)S(1)} %collective-permute-done.2.hp1), channel_id=1, source_target_pairs={{0,4},{4,0},{8,12},{12,8},{16,20},{20,16},{24,28},{28,24},{32,36},... | collective-permute-start | bytes 405512 | tf_op jit(solution)/shard_map/ppermute | solution.py:414
  18.1 0.9 collective-permute-start.8
  19.0 2.1 %collective-permute-start.9 = (bf16[1024,128]{1,0:T(8,128)(2,1)S(1)}, bf16[1024,128]{1,0:T(8,128)(2,1)S(1)}, u32[]{:S(2)}, u32[]{:S(2)}) collective-permute-start(bf16[1024,128]{1,0:T(8,128)(2,1)S(1)} %get-tuple-element.60), channel_id=1, source_target_pairs={{0,2},{1,3},{2,0},{3,1},{4,6},{5,7},{6,4},{7,5},{8,10},{9,11},{10,... | collective-permute-start | bytes 786440 | tf_op jit(solution)/shard_map/ppermute | solution.py:409
  21.1 1.1 %collective-permute-start.10 = (bf16[1024,128]{1,0:T(8,128)(2,1)S(1)}, bf16[1024,128]{1,0:T(8,128)(2,1)S(1)}, u32[]{:S(2)}, u32[]{:S(2)}) collective-permute-start(bf16[1024,128]{1,0:T(8,128)(2,1)S(1)} %get-tuple-element.60), channel_id=1, source_target_pairs={{0,3},{1,0},{2,1},{3,2},{4,7},{5,4},{6,5},{7,6},{8,11},{9,8},{10,9... | collective-permute-start | bytes 786440 | tf_op jit(solution)/shard_map/ppermute | solution.py:409
  22.1 0.8 collective-permute-start.6
  23.0 1.0 %collective-permute-done.6.sp2 = bf16[3,176,128]{2,1,0:T(8,128)(2,1)S(1)} collective-permute-done((bf16[3,176,128]{2,1,0:T(8,128)(2,1)S(1)}, bf16[3,176,128]{2,1,0:T(8,128)(2,1)S(1)}, u32[]{:S(2)}, u32[]{:S(2)}) %collective-permute-start.6) | collective-permute-done | bytes 135200 | tf_op jit(solution)/shard_map/ppermute | solution.py:414
  24.3 7.1 %shard_map.134 = (bf16[1024,176]{1,0:T(8,128)(2,1)S(1)}, bf16[1024,176]{1,0:T(8,128)(2,1)S(1)}, bf16[176,1024]{1,0:T(8,128)(2,1)S(1)}, bf16[4,1200,256]{2,1,0:T(8,128)(2,1)S(1)}) custom-call(s32[80]{0:T(128)S(1)} %get-tuple-element.49.table, f32[4,8,512]{2,1,0:T(8,128)S(1)} %get-tuple-element.52.valid, bf16[4,176,256]{2,1,0:T(8,128)(2,1)S(1)} %get-tuple-element.54.scaled, ...), custom_call_target="tpu_custom_call" | custom-call | tf_op jit(solution)/shard_map/pallas_call | solution.py:394
  31.5 1.7 %collective-permute-done.9.ho2 = bf16[1024,128]{1,0:T(8,128)(2,1)S(1)} collective-permute-done((bf16[1024,128]{1,0:T(8,128)(2,1)S(1)}, bf16[1024,128]{1,0:T(8,128)(2,1)S(1)}, u32[]{:S(2)}, u32[]{:S(2)}) %collective-permute-start.9) | collective-permute-done | bytes 262176 | tf_op jit(solution)/shard_map/ppermute | solution.py:409
  33.2 1.1 %collective-permute-start.11 = (bf16[1024,128]{1,0:T(8,128)(2,1)S(1)}, bf16[1024,128]{1,0:T(8,128)(2,1)S(1)}, u32[]{:S(2)}, u32[]{:S(2)}) collective-permute-start(bf16[1024,128]{1,0:T(8,128)(2,1)S(1)} %collective-permute-done.8.ho1), channel_id=1, source_target_pairs={{0,4},{4,0},{8,12},{12,8},{16,20},{20,16},{24,28},{28,24},{32,36},... | collective-permute-start | bytes 786440 | tf_op jit(solution)/shard_map/ppermute | solution.py:414
  36.2 11.8 %shard_map.135 = (bf16[4,160,128]{2,1,0:T(8,128)(2,1)S(1)}, bf16[4,48,128]{2,1,0:T(8,128)(2,1)S(1)}, bf16[4,48,128]{2,1,0:T(8,128)(2,1)S(1)}, bf16[4,48,128]{2,1,0:T(8,128)(2,1)S(1)}, bf16[4,48,128]{2,1,0:T(8,128)(2,1)S(1)}) custom-call(s32[80]{0:T(128)S(1)} %get-tuple-element.49.table, bf16[4,80,512]{2,1,0:T(8,128)(2,1)S(1)} %get-tuple-element.50.context, ...), custom_call_target="tpu_custom_call" | custom-call | tf_op jit(solution)/shard_map/pallas_call | solution.py:394
  48.0 1.4 %collective-permute-start.14 = (bf16[4,48,128]{2,1,0:T(8,128)(2,1)S(1)}, bf16[4,48,128]{2,1,0:T(8,128)(2,1)S(1)}, u32[]{:S(2)}, u32[]{:S(2)}) collective-permute-start(bf16[4,48,128]{2,1,0:T(8,128)(2,1)S(1)} %get-tuple-element.76), channel_id=1, source_target_pairs={{0,1},{1,2},{2,3},{3,0},{4,5},{5,6},{6,7},{7,4},{8,9},{9,10},{10,1... | collective-permute-start | bytes 147464 | tf_op jit(solution)/shard_map/ppermute | solution.py:409
  49.4 2.5 %collective-permute-start.16 = (bf16[4,48,128]{2,1,0:T(8,128)(2,1)S(1)}, bf16[4,48,128]{2,1,0:T(8,128)(2,1)S(1)}, u32[]{:S(2)}, u32[]{:S(2)}) collective-permute-start(bf16[4,48,128]{2,1,0:T(8,128)(2,1)S(1)} %get-tuple-element.78), channel_id=1, source_target_pairs={{0,3},{1,0},{2,1},{3,2},{4,7},{5,4},{6,5},{7,6},{8,11},{9,8},{10,9... | collective-permute-start | bytes 147464 | tf_op jit(solution)/shard_map/ppermute | solution.py:409
  51.9 1.4 %collective-permute-start.17 = (bf16[4,48,128]{2,1,0:T(8,128)(2,1)S(1)}, bf16[4,48,128]{2,1,0:T(8,128)(2,1)S(1)}, u32[]{:S(2)}, u32[]{:S(2)}) collective-permute-start(bf16[4,48,128]{2,1,0:T(8,128)(2,1)S(1)} %get-tuple-element.75.a0), channel_id=1, source_target_pairs={{0,4},{4,0},{8,12},{12,8},{16,20},{20,16},{24,28},{28,24},{32,36},... | collective-permute-start | bytes 147464 | tf_op jit(solution)/shard_map/ppermute | solution.py:414
  54.3 1.3 %collective-permute-start.19 = (bf16[4,48,128]{2,1,0:T(8,128)(2,1)S(1)}, bf16[4,48,128]{2,1,0:T(8,128)(2,1)S(1)}, u32[]{:S(2)}, u32[]{:S(2)}) collective-permute-start(bf16[4,48,128]{2,1,0:T(8,128)(2,1)S(1)} %collective-permute-done.15.a2), channel_id=1, source_target_pairs={{0,4},{4,0},{8,12},{12,8},{16,20},{20,16},{24,28},{28,24},{32,36},... | collective-permute-start | bytes 147464 | tf_op jit(solution)/shard_map/ppermute | solution.py:414
  55.6 1.0 %collective-permute-start.20 = (bf16[4,48,128]{2,1,0:T(8,128)(2,1)S(1)}, bf16[4,48,128]{2,1,0:T(8,128)(2,1)S(1)}, u32[]{:S(2)}, u32[]{:S(2)}) collective-permute-start(bf16[4,48,128]{2,1,0:T(8,128)(2,1)S(1)} %collective-permute-done.16.a3), channel_id=1, source_target_pairs={{0,4},{4,0},{8,12},{12,8},{16,20},{20,16},{24,28},{28,24},{32,36},... | collective-permute-start | bytes 147464 | tf_op jit(solution)/shard_map/ppermute | solution.py:414
  56.6 0.9 collective-permute-done.20.b3
  57.5 1.5 %shard_map.136 = bf16[32,48,128]{2,1,0:T(8,128)(2,1)} custom-call(s32[80]{0:T(128)S(1)} %get-tuple-element.49.table, bf16[4,48,128]{2,1,0:T(8,128)(2,1)S(1)} %get-tuple-element.75.a0, bf16[4,48,128]{2,1,0:T(8,128)(2,1)S(1)} %collective-permute-done.14.a1, bf16[4,48,128]{2,1,0:T(8,128)(2,1)S(1)} %collective-permute-done.15.a2, ...), custom_call_target="tpu_custom_call" | custom-call | tf_op jit(solution)/shard_map/pallas_call | solution.py:394
  59.0 10.5 %all-to-all-start = ((bf16[32,48,128]{2,1,0:T(8,128)(2,1)}), bf16[32,48,128]{2,1,0:T(8,128)(2,1)S(1)}, u32[]{:S(2)}, u32[]{:S(2)}) async-start(bf16[32,48,128]{2,1,0:T(8,128)(2,1)} %shard_map.136), calls=%async_computation | async-start | bytes 786432 | tf_op jit(solution)/shard_map/all_to_all | solution.py:546
  69.6 2.6 %collective-permute-start.25 = (bf16[4,160,128]{2,1,0:T(8,128)(2,1)S(1)}, bf16[4,160,128]{2,1,0:T(8,128)(2,1)S(1)}, u32[]{:S(2)}, u32[]{:S(2)}) collective-permute-start(bf16[4,160,128]{2,1,0:T(8,128)(2,1)S(1)} %get-tuple-element.81.a0), channel_id=1, source_target_pairs={{0,2},{1,3},{2,0},{3,1},{4,6},{5,7},{6,4},{7,5},{8,10},{9,11},{10,... | collective-permute-start | bytes 491528 | tf_op jit(solution)/shard_map/ppermute | solution.py:409
  72.2 0.8 collective-permute-start.26
  73.0 6.6 %all-to-all-done.got = bf16[32,48,128]{2,1,0:T(8,128)(2,1)S(1)} async-done(((bf16[32,48,128]{2,1,0:T(8,128)(2,1)}), bf16[32,48,128]{2,1,0:T(8,128)(2,1)S(1)}, u32[]{:S(2)}, u32[]{:S(2)}) %all-to-all-start) | async-done | bytes 393248 | tf_op jit(solution)/shard_map/all_to_all | solution.py:546
  80.5 1.2 %collective-permute-start.27 = (bf16[16,160,128]{2,1,0:T(8,128)(2,1)S(1)}, bf16[16,160,128]{2,1,0:T(8,128)(2,1)S(1)}, u32[]{:S(2)}, u32[]{:S(2)}) collective-permute-start(bf16[16,160,128]{2,1,0:T(8,128)(2,1)S(1)} %pad_maximum_fusion), channel_id=1, source_target_pairs={{0,4},{4,0},{8,12},{12,8},{16,20},{20,16},{24,28},{28,24},{32,36},... | collective-permute-start | bytes 1966088 | tf_op jit(solution)/shard_map/ppermute | solution.py:414
  82.4 2.8 %collective-permute-start.22 = (bf16[6,48,128]{2,1,0:T(8,128)(2,1)S(1)}, bf16[6,48,128]{2,1,0:T(8,128)(2,1)S(1)}, u32[]{:S(2)}, u32[]{:S(2)}) collective-permute-start(bf16[6,48,128]{2,1,0:T(8,128)(2,1)S(1)} %shard_map.137.b0), channel_id=1, source_target_pairs={{0,2},{1,3},{2,0},{3,1},{4,6},{5,7},{6,4},{7,5},{8,10},{9,11},{10,... | collective-permute-start | bytes 221192 | tf_op jit(solution)/shard_map/ppermute | solution.py:409
  85.2 2.0 %shard_map.138 = f32[4,80,1024]{2,1,0:T(8,128)} custom-call(s32[80]{0:T(128)S(1)} %get-tuple-element.49.table, bf16[4,160,128]{2,1,0:T(8,128)(2,1)S(1)} %get-tuple-element.81.a0, bf16[4,160,128]{2,1,0:T(8,128)(2,1)S(1)} %collective-permute-done.24.a1, bf16[4,160,128]{2,1,0:T(8,128)(2,1)S(1)} %collective-permute-done.25.a2, ...), custom_call_target="tpu_custom_call" | custom-call | tf_op jit(solution)/shard_map/pallas_call | solution.py:394
  87.2 1.9 %collective-permute-done.22.b2 = bf16[6,48,128]{2,1,0:T(8,128)(2,1)S(1)} collective-permute-done((bf16[6,48,128]{2,1,0:T(8,128)(2,1)S(1)}, bf16[6,48,128]{2,1,0:T(8,128)(2,1)S(1)}, u32[]{:S(2)}, u32[]{:S(2)}) %collective-permute-start.22) | collective-permute-done | bytes 73760 | tf_op jit(solution)/shard_map/ppermute | solution.py:409
  89.1 0.8 shard_map.139
  (58 shorter events, 6.9 us)
Async XLA Ops:
  0.6 10.6 %copy-start.3 = (f32[16,1024]{1,0:T(8,128)S(1)}, f32[16,1024]{1,0:T(8,128)}, u32[]{:S(2)}) copy-start(f32[16,1024]{1,0:T(8,128)} %constant.2.clone.e_rows_h.e_rows) | copy-start | bytes 196612
  0.6 10.6 %copy-start = (bf16[160,1024]{1,0:T(8,128)(2,1)S(1)}, bf16[160,1024]{1,0:T(8,128)(2,1)}, u32[]{:S(2)}) copy-start(bf16[160,1024]{1,0:T(8,128)(2,1)} %w_in.3) | copy-start | bytes 983044
  3.8 7.4 %collective-permute-start = (bf16[4,80,2048]{2,1,0:T(8,128)(2,1)S(1)}, bf16[4,80,2048]{2,1,0:T(8,128)(2,1)S(1)}, u32[]{:S(2)}, u32[]{:S(2)}) collective-permute-start(bf16[4,80,2048]{2,1,0:T(8,128)(2,1)S(1)} %copy-done.1), channel_id=1, source_target_pairs={{0,4},{4,0},{8,12},{12,8},{16,20},{20,16},{24,28},{28,24},{32,36},... | collective-permute-start | bytes 3932168 | tf_op jit(solution)/shard_map/ppermute | solution.py:414
  5.3 5.8 %collective-permute-start.1 = (bf16[4,80,1024]{2,1,0:T(8,128)(2,1)}, bf16[4,80,1024]{2,1,0:T(8,128)(2,1)S(1)}, u32[]{:S(2)}, u32[]{:S(2)}) collective-permute-start(bf16[4,80,1024]{2,1,0:T(8,128)(2,1)} %noise_a.1), channel_id=1, source_target_pairs={{0,4},{4,0},{8,12},{12,8},{16,20},{20,16},{24,28},{28,24},{32,36},... | collective-permute-start | bytes 1966088 | tf_op jit(solution)/shard_map/ppermute | solution.py:414
  5.4 11.0 %collective-permute-start.2 = (bf16[3,176,128]{2,1,0:T(8,128)(2,1)}, bf16[3,176,128]{2,1,0:T(8,128)(2,1)S(1)}, u32[]{:S(2)}, u32[]{:S(2)}) collective-permute-start(bf16[3,176,128]{2,1,0:T(8,128)(2,1)} %get-tuple-element.46), channel_id=1, source_target_pairs={{0,1},{1,2},{2,3},{3,0},{4,5},{5,6},{6,7},{7,4},{8,9},{9,10},{10,1... | collective-permute-start | bytes 405512 | tf_op jit(solution)/shard_map/ppermute | solution.py:409
  7.1 9.7 %collective-permute-start.3 = (bf16[3,176,128]{2,1,0:T(8,128)(2,1)}, bf16[3,176,128]{2,1,0:T(8,128)(2,1)S(1)}, u32[]{:S(2)}, u32[]{:S(2)}) collective-permute-start(bf16[3,176,128]{2,1,0:T(8,128)(2,1)} %get-tuple-element.46), channel_id=1, source_target_pairs={{0,2},{1,3},{2,0},{3,1},{4,6},{5,7},{6,4},{7,5},{8,10},{9,11},{10,... | collective-permute-start | bytes 405512 | tf_op jit(solution)/shard_map/ppermute | solution.py:409
  10.5 6.4 %collective-permute-start.4 = (bf16[3,176,128]{2,1,0:T(8,128)(2,1)}, bf16[3,176,128]{2,1,0:T(8,128)(2,1)S(1)}, u32[]{:S(2)}, u32[]{:S(2)}) collective-permute-start(bf16[3,176,128]{2,1,0:T(8,128)(2,1)} %get-tuple-element.46), channel_id=1, source_target_pairs={{0,3},{1,0},{2,1},{3,2},{4,7},{5,4},{6,5},{7,6},{8,11},{9,8},{10,9... | collective-permute-start | bytes 405512 | tf_op jit(solution)/shard_map/ppermute | solution.py:409
  12.3 12.0 %copy-start.5 = (bf16[3,176,256]{2,1,0:T(8,128)(2,1)S(1)}, bf16[3,176,256]{2,1,0:T(8,128)(2,1)}, u32[]{:S(2)}) copy-start(bf16[3,176,256]{2,1,0:T(8,128)(2,1)} %get-tuple-element.58.wp0) | copy-start | bytes 811012
  16.8 6.1 %collective-permute-start.5 = (bf16[3,176,128]{2,1,0:T(8,128)(2,1)S(1)}, bf16[3,176,128]{2,1,0:T(8,128)(2,1)S(1)}, u32[]{:S(2)}, u32[]{:S(2)}) collective-permute-start(bf16[3,176,128]{2,1,0:T(8,128)(2,1)S(1)} %collective-permute-done.2.hp1), channel_id=1, source_target_pairs={{0,4},{4,0},{8,12},{12,8},{16,20},{20,16},{24,28},{28,24},{32,36},... | collective-permute-start | bytes 405512 | tf_op jit(solution)/shard_map/ppermute | solution.py:414
  18.1 13.4 %collective-permute-start.8 = (bf16[1024,128]{1,0:T(8,128)(2,1)S(1)}, bf16[1024,128]{1,0:T(8,128)(2,1)S(1)}, u32[]{:S(2)}, u32[]{:S(2)}) collective-permute-start(bf16[1024,128]{1,0:T(8,128)(2,1)S(1)} %get-tuple-element.60), channel_id=1, source_target_pairs={{0,1},{1,2},{2,3},{3,0},{4,5},{5,6},{6,7},{7,4},{8,9},{9,10},{10,1... | collective-permute-start | bytes 786440 | tf_op jit(solution)/shard_map/ppermute | solution.py:409
  19.0 14.2 %collective-permute-start.9 = (bf16[1024,128]{1,0:T(8,128)(2,1)S(1)}, bf16[1024,128]{1,0:T(8,128)(2,1)S(1)}, u32[]{:S(2)}, u32[]{:S(2)}) collective-permute-start(bf16[1024,128]{1,0:T(8,128)(2,1)S(1)} %get-tuple-element.60), channel_id=1, source_target_pairs={{0,2},{1,3},{2,0},{3,1},{4,6},{5,7},{6,4},{7,5},{8,10},{9,11},{10,... | collective-permute-start | bytes 786440 | tf_op jit(solution)/shard_map/ppermute | solution.py:409
  21.1 12.1 %collective-permute-start.10 = (bf16[1024,128]{1,0:T(8,128)(2,1)S(1)}, bf16[1024,128]{1,0:T(8,128)(2,1)S(1)}, u32[]{:S(2)}, u32[]{:S(2)}) collective-permute-start(bf16[1024,128]{1,0:T(8,128)(2,1)S(1)} %get-tuple-element.60), channel_id=1, source_target_pairs={{0,3},{1,0},{2,1},{3,2},{4,7},{5,4},{6,5},{7,6},{8,11},{9,8},{10,9... | collective-permute-start | bytes 786440 | tf_op jit(solution)/shard_map/ppermute | solution.py:409
  22.1 1.8 %collective-permute-start.6 = (bf16[3,176,128]{2,1,0:T(8,128)(2,1)S(1)}, bf16[3,176,128]{2,1,0:T(8,128)(2,1)S(1)}, u32[]{:S(2)}, u32[]{:S(2)}) collective-permute-start(bf16[3,176,128]{2,1,0:T(8,128)(2,1)S(1)} %collective-permute-done.3.hp2), channel_id=1, source_target_pairs={{0,4},{4,0},{8,12},{12,8},{16,20},{20,16},{24,28},{28,24},{32,36},... | collective-permute-start | bytes 405512 | tf_op jit(solution)/shard_map/ppermute | solution.py:414
  23.0 1.4 %collective-permute-start.7 = (bf16[3,176,128]{2,1,0:T(8,128)(2,1)S(1)}, bf16[3,176,128]{2,1,0:T(8,128)(2,1)S(1)}, u32[]{:S(2)}, u32[]{:S(2)}) collective-permute-start(bf16[3,176,128]{2,1,0:T(8,128)(2,1)S(1)} %collective-permute-done.4.hp3), channel_id=1, source_target_pairs={{0,4},{4,0},{8,12},{12,8},{16,20},{20,16},{24,28},{28,24},{32,36},... | collective-permute-start | bytes 405512 | tf_op jit(solution)/shard_map/ppermute | solution.py:414
  33.2 2.3 %collective-permute-start.11 = (bf16[1024,128]{1,0:T(8,128)(2,1)S(1)}, bf16[1024,128]{1,0:T(8,128)(2,1)S(1)}, u32[]{:S(2)}, u32[]{:S(2)}) collective-permute-start(bf16[1024,128]{1,0:T(8,128)(2,1)S(1)} %collective-permute-done.8.ho1), channel_id=1, source_target_pairs={{0,4},{4,0},{8,12},{12,8},{16,20},{20,16},{24,28},{28,24},{32,36},... | collective-permute-start | bytes 786440 | tf_op jit(solution)/shard_map/ppermute | solution.py:414
  34.3 1.5 %collective-permute-start.12 = (bf16[1024,128]{1,0:T(8,128)(2,1)S(1)}, bf16[1024,128]{1,0:T(8,128)(2,1)S(1)}, u32[]{:S(2)}, u32[]{:S(2)}) collective-permute-start(bf16[1024,128]{1,0:T(8,128)(2,1)S(1)} %collective-permute-done.9.ho2), channel_id=1, source_target_pairs={{0,4},{4,0},{8,12},{12,8},{16,20},{20,16},{24,28},{28,24},{32,36},... | collective-permute-start | bytes 786440 | tf_op jit(solution)/shard_map/ppermute | solution.py:414
  34.3 1.9 %collective-permute-start.13 = (bf16[1024,128]{1,0:T(8,128)(2,1)S(1)}, bf16[1024,128]{1,0:T(8,128)(2,1)S(1)}, u32[]{:S(2)}, u32[]{:S(2)}) collective-permute-start(bf16[1024,128]{1,0:T(8,128)(2,1)S(1)} %collective-permute-done.10.ho3), channel_id=1, source_target_pairs={{0,4},{4,0},{8,12},{12,8},{16,20},{20,16},{24,28},{28,24},{32,36},... | collective-permute-start | bytes 786440 | tf_op jit(solution)/shard_map/ppermute | solution.py:414
  48.0 5.3 %collective-permute-start.14 = (bf16[4,48,128]{2,1,0:T(8,128)(2,1)S(1)}, bf16[4,48,128]{2,1,0:T(8,128)(2,1)S(1)}, u32[]{:S(2)}, u32[]{:S(2)}) collective-permute-start(bf16[4,48,128]{2,1,0:T(8,128)(2,1)S(1)} %get-tuple-element.76), channel_id=1, source_target_pairs={{0,1},{1,2},{2,3},{3,0},{4,5},{5,6},{6,7},{7,4},{8,9},{9,10},{10,1... | collective-permute-start | bytes 147464 | tf_op jit(solution)/shard_map/ppermute | solution.py:409
  49.4 4.9 %collective-permute-start.15 = (bf16[4,48,128]{2,1,0:T(8,128)(2,1)S(1)}, bf16[4,48,128]{2,1,0:T(8,128)(2,1)S(1)}, u32[]{:S(2)}, u32[]{:S(2)}) collective-permute-start(bf16[4,48,128]{2,1,0:T(8,128)(2,1)S(1)} %get-tuple-element.77), channel_id=1, source_target_pairs={{0,2},{1,3},{2,0},{3,1},{4,6},{5,7},{6,4},{7,5},{8,10},{9,11},{10,... | collective-permute-start | bytes 147464 | tf_op jit(solution)/shard_map/ppermute | solution.py:409
  49.4 6.2 %collective-permute-start.16 = (bf16[4,48,128]{2,1,0:T(8,128)(2,1)S(1)}, bf16[4,48,128]{2,1,0:T(8,128)(2,1)S(1)}, u32[]{:S(2)}, u32[]{:S(2)}) collective-permute-start(bf16[4,48,128]{2,1,0:T(8,128)(2,1)S(1)} %get-tuple-element.78), channel_id=1, source_target_pairs={{0,3},{1,0},{2,1},{3,2},{4,7},{5,4},{6,5},{7,6},{8,11},{9,8},{10,9... | collective-permute-start | bytes 147464 | tf_op jit(solution)/shard_map/ppermute | solution.py:409
  51.9 4.7 %collective-permute-start.17 = (bf16[4,48,128]{2,1,0:T(8,128)(2,1)S(1)}, bf16[4,48,128]{2,1,0:T(8,128)(2,1)S(1)}, u32[]{:S(2)}, u32[]{:S(2)}) collective-permute-start(bf16[4,48,128]{2,1,0:T(8,128)(2,1)S(1)} %get-tuple-element.75.a0), channel_id=1, source_target_pairs={{0,4},{4,0},{8,12},{12,8},{16,20},{20,16},{24,28},{28,24},{32,36},... | collective-permute-start | bytes 147464 | tf_op jit(solution)/shard_map/ppermute | solution.py:414
  53.3 3.3 %collective-permute-start.18 = (bf16[4,48,128]{2,1,0:T(8,128)(2,1)S(1)}, bf16[4,48,128]{2,1,0:T(8,128)(2,1)S(1)}, u32[]{:S(2)}, u32[]{:S(2)}) collective-permute-start(bf16[4,48,128]{2,1,0:T(8,128)(2,1)S(1)} %collective-permute-done.14.a1), channel_id=1, source_target_pairs={{0,4},{4,0},{8,12},{12,8},{16,20},{20,16},{24,28},{28,24},{32,36},... | collective-permute-start | bytes 147464 | tf_op jit(solution)/shard_map/ppermute | solution.py:414
  54.3 2.3 %collective-permute-start.19 = (bf16[4,48,128]{2,1,0:T(8,128)(2,1)S(1)}, bf16[4,48,128]{2,1,0:T(8,128)(2,1)S(1)}, u32[]{:S(2)}, u32[]{:S(2)}) collective-permute-start(bf16[4,48,128]{2,1,0:T(8,128)(2,1)S(1)} %collective-permute-done.15.a2), channel_id=1, source_target_pairs={{0,4},{4,0},{8,12},{12,8},{16,20},{20,16},{24,28},{28,24},{32,36},... | collective-permute-start | bytes 147464 | tf_op jit(solution)/shard_map/ppermute | solution.py:414
  55.6 1.9 %collective-permute-start.20 = (bf16[4,48,128]{2,1,0:T(8,128)(2,1)S(1)}, bf16[4,48,128]{2,1,0:T(8,128)(2,1)S(1)}, u32[]{:S(2)}, u32[]{:S(2)}) collective-permute-start(bf16[4,48,128]{2,1,0:T(8,128)(2,1)S(1)} %collective-permute-done.16.a3), channel_id=1, source_target_pairs={{0,4},{4,0},{8,12},{12,8},{16,20},{20,16},{24,28},{28,24},{32,36},... | collective-permute-start | bytes 147464 | tf_op jit(solution)/shard_map/ppermute | solution.py:414
  59.0 20.6 %all-to-all-start = ((bf16[32,48,128]{2,1,0:T(8,128)(2,1)}), bf16[32,48,128]{2,1,0:T(8,128)(2,1)S(1)}, u32[]{:S(2)}, u32[]{:S(2)}) async-start(bf16[32,48,128]{2,1,0:T(8,128)(2,1)} %shard_map.136), calls=%async_computation | async-start | bytes 786432 | tf_op jit(solution)/shard_map/all_to_all | solution.py:546
  69.4 10.9 %collective-permute-start.24 = (bf16[4,160,128]{2,1,0:T(8,128)(2,1)S(1)}, bf16[4,160,128]{2,1,0:T(8,128)(2,1)S(1)}, u32[]{:S(2)}, u32[]{:S(2)}) collective-permute-start(bf16[4,160,128]{2,1,0:T(8,128)(2,1)S(1)} %get-tuple-element.81.a0), channel_id=1, source_target_pairs={{0,1},{1,2},{2,3},{3,0},{4,5},{5,6},{6,7},{7,4},{8,9},{9,10},{10,1... | collective-permute-start | bytes 491528 | tf_op jit(solution)/shard_map/ppermute | solution.py:409
  69.6 10.8 %collective-permute-start.25 = (bf16[4,160,128]{2,1,0:T(8,128)(2,1)S(1)}, bf16[4,160,128]{2,1,0:T(8,128)(2,1)S(1)}, u32[]{:S(2)}, u32[]{:S(2)}) collective-permute-start(bf16[4,160,128]{2,1,0:T(8,128)(2,1)S(1)} %get-tuple-element.81.a0), channel_id=1, source_target_pairs={{0,2},{1,3},{2,0},{3,1},{4,6},{5,7},{6,4},{7,5},{8,10},{9,11},{10,... | collective-permute-start | bytes 491528 | tf_op jit(solution)/shard_map/ppermute | solution.py:409
  72.2 8.2 %collective-permute-start.26 = (bf16[4,160,128]{2,1,0:T(8,128)(2,1)S(1)}, bf16[4,160,128]{2,1,0:T(8,128)(2,1)S(1)}, u32[]{:S(2)}, u32[]{:S(2)}) collective-permute-start(bf16[4,160,128]{2,1,0:T(8,128)(2,1)S(1)} %get-tuple-element.81.a0), channel_id=1, source_target_pairs={{0,3},{1,0},{2,1},{3,2},{4,7},{5,4},{6,5},{7,6},{8,11},{9,8},{10,9... | collective-permute-start | bytes 491528 | tf_op jit(solution)/shard_map/ppermute | solution.py:409
  80.5 4.7 %collective-permute-start.27 = (bf16[16,160,128]{2,1,0:T(8,128)(2,1)S(1)}, bf16[16,160,128]{2,1,0:T(8,128)(2,1)S(1)}, u32[]{:S(2)}, u32[]{:S(2)}) collective-permute-start(bf16[16,160,128]{2,1,0:T(8,128)(2,1)S(1)} %pad_maximum_fusion), channel_id=1, source_target_pairs={{0,4},{4,0},{8,12},{12,8},{16,20},{20,16},{24,28},{28,24},{32,36},... | collective-permute-start | bytes 1966088 | tf_op jit(solution)/shard_map/ppermute | solution.py:414
  81.6 5.5 %collective-permute-start.21 = (bf16[6,48,128]{2,1,0:T(8,128)(2,1)S(1)}, bf16[6,48,128]{2,1,0:T(8,128)(2,1)S(1)}, u32[]{:S(2)}, u32[]{:S(2)}) collective-permute-start(bf16[6,48,128]{2,1,0:T(8,128)(2,1)S(1)} %shard_map.137.b0), channel_id=1, source_target_pairs={{0,1},{1,2},{2,3},{3,0},{4,5},{5,6},{6,7},{7,4},{8,9},{9,10},{10,1... | collective-permute-start | bytes 221192 | tf_op jit(solution)/shard_map/ppermute | solution.py:409
  82.4 6.7 %collective-permute-start.22 = (bf16[6,48,128]{2,1,0:T(8,128)(2,1)S(1)}, bf16[6,48,128]{2,1,0:T(8,128)(2,1)S(1)}, u32[]{:S(2)}, u32[]{:S(2)}) collective-permute-start(bf16[6,48,128]{2,1,0:T(8,128)(2,1)S(1)} %shard_map.137.b0), channel_id=1, source_target_pairs={{0,2},{1,3},{2,0},{3,1},{4,6},{5,7},{6,4},{7,5},{8,10},{9,11},{10,... | collective-permute-start | bytes 221192 | tf_op jit(solution)/shard_map/ppermute | solution.py:409
  85.2 3.9 %collective-permute-start.23 = (bf16[6,48,128]{2,1,0:T(8,128)(2,1)S(1)}, bf16[6,48,128]{2,1,0:T(8,128)(2,1)S(1)}, u32[]{:S(2)}, u32[]{:S(2)}) collective-permute-start(bf16[6,48,128]{2,1,0:T(8,128)(2,1)S(1)} %shard_map.137.b0), channel_id=1, source_target_pairs={{0,3},{1,0},{2,1},{3,2},{4,7},{5,4},{6,5},{7,6},{8,11},{9,8},{10,9... | collective-permute-start | bytes 221192 | tf_op jit(solution)/shard_map/ppermute | solution.py:409
  (8 other events, 46.2 us)

commit v6 on v5

--- a/solution.py
+++ b/solution.py
@@ -505,7 +505,7 @@
     )
     halves = gathered(half)[1:]
     mel_late, noise_late = after(mel_audio, half), after(start_noise, half)
-    audio = (mel_audio, to_other(mel_late), start_noise, to_other(noise_late))
+    audio = (mel_late, to_other(mel_late), noise_late, to_other(noise_late))
     table, gram, context, noise, valid, scaled, values, keys, own_win = run_plan(
         plan, audio, w_input, e_rows
     )

time: 90 us -> 89.8 us (level); the launches traced: 90 us -> 88.2 us
  Pallas kernels: 31.1 us -> 22.1 us
  waiting for transfers between devices: 14.9 us -> 18.6 us
  starting transfers between devices: 41.9 us -> 45.4 us
    pallas_call x9, Pallas kernels: 31.1 us -> 22.1 us  [call(): pl.pallas_call(kernel, out_shape=outs, in_specs=[spec(k) for k in kinds],...]
    ppermute x15, waiting for transfers between devices: 4.64 us -> 8.37 us  [to_next(): return lax.ppermute(value, 'mp', [(i, (i + k) % N_MP) for i in range(N_MP)])]
    all_to_all x1, starting transfers between devices: 10.5 us -> 13.9 us  [shards(): got = lax.all_to_all(packed, 'dp', 0, 0, tiled=True)]
  transfers between devices with their start and end apart: 29 -> 29, of which waited for: 11 -> 11; matrix products, arithmetic and copies ran while one was open for 0% -> 0% of each run, Pallas kernels for 15% -> 11%
where the time goes in v6:
time: 89.8 us; the launch traced here: 88.2 us
  starting transfers between devices  45.4 us (51%)
  Pallas kernels  22.1 us (25%)
  waiting for transfers between devices  18.6 us (21%)
  local copies, waits for them, and re-layouts  1.13 us (1%)
  between operations  0.9 us (1%)
    pallas_call x9, Pallas kernels, call(): pl.pallas_call(kernel, out_shape=outs, in_specs=[spec(k) for k in kinds],...  22.1 us
    ppermute x15, starting transfers between devices, to_next(): return lax.ppermute(value, 'mp', [(i, (i + k) % N_MP) for i in range(N_MP)])  21 us
    all_to_all x1, starting transfers between devices, shards(): got = lax.all_to_all(packed, 'dp', 0, 0, tiled=True)  13.9 us
    ppermute x13, starting transfers between devices, to_other(): return lax.ppermute(value, 'dp', [(i, i ^ 1) for i in range(size)])  10.4 us
    ppermute x15, waiting for transfers between devices, to_next(): return lax.ppermute(value, 'mp', [(i, (i + k) % N_MP) for i in range(N_MP)])  8.37 us
    all_to_all x1, waiting for transfers between devices, shards(): got = lax.all_to_all(packed, 'dp', 0, 0, tiled=True)  6.61 us
    ppermute x13, waiting for transfers between devices, to_other(): return lax.ppermute(value, 'dp', [(i, i ^ 1) for i in range(size)])  3.64 us
  transfers between devices with their start and end apart: 29, of which 11 were waited for; matrix products, arithmetic and copies ran while one was open for 0% of the time, Pallas kernels for 11%

profile of v6, /device:TPU:1, one launch (start us, length us, event | category | flops | bytes accessed | tf_op | source)
XLA Modules:
  0.0 88.2 jit_solution(6008212003925663584)
XLA Ops:
  0.7 3.1 %shard_map.131 = (bf16[3,176,256]{2,1,0:T(8,128)(2,1)}, bf16[3,176,128]{2,1,0:T(8,128)(2,1)}) custom-call(bf16[160,1024]{1,0:T(8,128)(2,1)} %w_in.3, f32[16,1024]{1,0:T(8,128)} %constant.2.clone.e_rows_h.e_rows, f32[1,1024]{1,0:T(1,128)} %bitcast.7, bf16[3,1024,256]{2,1,0:T(8,128)(2,1)} %bitcast.6), custom_call_target="tpu_custom_call" | custom-call | tf_op jit(solution)/shard_map/pallas_call | solution.py:394
  3.8 1.5 %collective-permute-start = (bf16[4,80,2048]{2,1,0:T(8,128)(2,1)S(1)}, bf16[4,80,2048]{2,1,0:T(8,128)(2,1)S(1)}, u32[]{:S(2)}, u32[]{:S(2)}) collective-permute-start(bf16[4,80,2048]{2,1,0:T(8,128)(2,1)S(1)} %copy-done.1), channel_id=1, source_target_pairs={{0,4},{4,0},{8,12},{12,8},{16,20},{20,16},{24,28},{28,24},{32,36},... | collective-permute-start | bytes 3932168 | tf_op jit(solution)/shard_map/ppermute | solution.py:414
  5.4 1.7 %collective-permute-start.2 = (bf16[3,176,128]{2,1,0:T(8,128)(2,1)}, bf16[3,176,128]{2,1,0:T(8,128)(2,1)S(1)}, u32[]{:S(2)}, u32[]{:S(2)}) collective-permute-start(bf16[3,176,128]{2,1,0:T(8,128)(2,1)} %get-tuple-element.46), channel_id=1, source_target_pairs={{0,1},{1,2},{2,3},{3,0},{4,5},{5,6},{6,7},{7,4},{8,9},{9,10},{10,1... | collective-permute-start | bytes 405512 | tf_op jit(solution)/shard_map/ppermute | solution.py:409
  7.1 3.3 %collective-permute-start.3 = (bf16[3,176,128]{2,1,0:T(8,128)(2,1)}, bf16[3,176,128]{2,1,0:T(8,128)(2,1)S(1)}, u32[]{:S(2)}, u32[]{:S(2)}) collective-permute-start(bf16[3,176,128]{2,1,0:T(8,128)(2,1)} %get-tuple-element.46), channel_id=1, source_target_pairs={{0,2},{1,3},{2,0},{3,1},{4,6},{5,7},{6,4},{7,5},{8,10},{9,11},{10,... | collective-permute-start | bytes 405512 | tf_op jit(solution)/shard_map/ppermute | solution.py:409
  11.2 1.1 %copy-done.2 = bf16[4,80,1024]{2,1,0:T(8,128)(2,1)S(1)} copy-done((bf16[4,80,1024]{2,1,0:T(8,128)(2,1)S(1)}, bf16[4,80,1024]{2,1,0:T(8,128)(2,1)}, u32[]{:S(2)}) %copy-start.2) | copy-done | bytes 655384
  12.3 2.8 %shard_map.132 = (s32[80]{0:T(128)S(1)}, bf16[352,176]{1,0:T(8,128)(2,1)S(1)}, bf16[4,80,512]{2,1,0:T(8,128)(2,1)S(1)}, bf16[4,80,256]{2,1,0:T(8,128)(2,1)S(1)},...) custom-call(s32[512]{0:T(512)S(1)} %copy-done.7, ...), custom_call_target="tpu_custom_call" | custom-call | tf_op jit(solution)/shard_map/pallas_call | solution.py:394
  15.8 1.0 %collective-permute-done.3.hp2 = bf16[3,176,128]{2,1,0:T(8,128)(2,1)S(1)} collective-permute-done((bf16[3,176,128]{2,1,0:T(8,128)(2,1)}, bf16[3,176,128]{2,1,0:T(8,128)(2,1)S(1)}, u32[]{:S(2)}, u32[]{:S(2)}) %collective-permute-start.3) | collective-permute-done | bytes 135200 | tf_op jit(solution)/shard_map/ppermute | solution.py:409
  16.8 1.3 %collective-permute-start.5 = (bf16[3,176,128]{2,1,0:T(8,128)(2,1)S(1)}, bf16[3,176,128]{2,1,0:T(8,128)(2,1)S(1)}, u32[]{:S(2)}, u32[]{:S(2)}) collective-permute-start(bf16[3,176,128]{2,1,0:T(8,128)(2,1)S(1)} %collective-permute-done.2.hp1), channel_id=1, source_target_pairs={{0,4},{4,0},{8,12},{12,8},{16,20},{20,16},{24,28},{28,24},{32,36},... | collective-permute-start | bytes 405512 | tf_op jit(solution)/shard_map/ppermute | solution.py:414
  18.1 0.9 collective-permute-start.8
  19.0 2.1 %collective-permute-start.9 = (bf16[1024,128]{1,0:T(8,128)(2,1)S(1)}, bf16[1024,128]{1,0:T(8,128)(2,1)S(1)}, u32[]{:S(2)}, u32[]{:S(2)}) collective-permute-start(bf16[1024,128]{1,0:T(8,128)(2,1)S(1)} %get-tuple-element.60), channel_id=1, source_target_pairs={{0,2},{1,3},{2,0},{3,1},{4,6},{5,7},{6,4},{7,5},{8,10},{9,11},{10,... | collective-permute-start | bytes 786440 | tf_op jit(solution)/shard_map/ppermute | solution.py:409
  21.1 1.1 %collective-permute-start.10 = (bf16[1024,128]{1,0:T(8,128)(2,1)S(1)}, bf16[1024,128]{1,0:T(8,128)(2,1)S(1)}, u32[]{:S(2)}, u32[]{:S(2)}) collective-permute-start(bf16[1024,128]{1,0:T(8,128)(2,1)S(1)} %get-tuple-element.60), channel_id=1, source_target_pairs={{0,3},{1,0},{2,1},{3,2},{4,7},{5,4},{6,5},{7,6},{8,11},{9,8},{10,9... | collective-permute-start | bytes 786440 | tf_op jit(solution)/shard_map/ppermute | solution.py:409
  22.1 0.8 collective-permute-start.6
  23.0 1.0 %collective-permute-done.6.sp2 = bf16[3,176,128]{2,1,0:T(8,128)(2,1)S(1)} collective-permute-done((bf16[3,176,128]{2,1,0:T(8,128)(2,1)S(1)}, bf16[3,176,128]{2,1,0:T(8,128)(2,1)S(1)}, u32[]{:S(2)}, u32[]{:S(2)}) %collective-permute-start.6) | collective-permute-done | bytes 135200 | tf_op jit(solution)/shard_map/ppermute | solution.py:414
  24.3 4.0 %shard_map.134 = (bf16[1024,176]{1,0:T(8,128)(2,1)S(1)}, bf16[1024,176]{1,0:T(8,128)(2,1)S(1)}, bf16[176,1024]{1,0:T(8,128)(2,1)S(1)}, bf16[4,1200,256]{2,1,0:T(8,128)(2,1)S(1)}) custom-call(s32[80]{0:T(128)S(1)} %get-tuple-element.49.table, f32[4,8,512]{2,1,0:T(8,128)S(1)} %get-tuple-element.52.valid, bf16[4,176,256]{2,1,0:T(8,128)(2,1)S(1)} %get-tuple-element.54.scaled, ...), custom_call_target="tpu_custom_call" | custom-call | tf_op jit(solution)/shard_map/pallas_call | solution.py:394
  28.4 4.8 %collective-permute-done.9.ho2 = bf16[1024,128]{1,0:T(8,128)(2,1)S(1)} collective-permute-done((bf16[1024,128]{1,0:T(8,128)(2,1)S(1)}, bf16[1024,128]{1,0:T(8,128)(2,1)S(1)}, u32[]{:S(2)}, u32[]{:S(2)}) %collective-permute-start.9) | collective-permute-done | bytes 262176 | tf_op jit(solution)/shard_map/ppermute | solution.py:409
  33.2 1.1 %collective-permute-start.11 = (bf16[1024,128]{1,0:T(8,128)(2,1)S(1)}, bf16[1024,128]{1,0:T(8,128)(2,1)S(1)}, u32[]{:S(2)}, u32[]{:S(2)}) collective-permute-start(bf16[1024,128]{1,0:T(8,128)(2,1)S(1)} %collective-permute-done.8.ho1), channel_id=1, source_target_pairs={{0,4},{4,0},{8,12},{12,8},{16,20},{20,16},{24,28},{28,24},{32,36},... | collective-permute-start | bytes 786440 | tf_op jit(solution)/shard_map/ppermute | solution.py:414
  36.2 6.6 %shard_map.135 = (bf16[4,160,128]{2,1,0:T(8,128)(2,1)S(1)}, bf16[4,48,128]{2,1,0:T(8,128)(2,1)S(1)}, bf16[4,48,128]{2,1,0:T(8,128)(2,1)S(1)}, bf16[4,48,128]{2,1,0:T(8,128)(2,1)S(1)}, bf16[4,48,128]{2,1,0:T(8,128)(2,1)S(1)}) custom-call(s32[80]{0:T(128)S(1)} %get-tuple-element.49.table, bf16[4,80,512]{2,1,0:T(8,128)(2,1)S(1)} %get-tuple-element.50.context, ...), custom_call_target="tpu_custom_call" | custom-call | tf_op jit(solution)/shard_map/pallas_call | solution.py:394
  42.8 1.4 %collective-permute-start.14 = (bf16[4,48,128]{2,1,0:T(8,128)(2,1)S(1)}, bf16[4,48,128]{2,1,0:T(8,128)(2,1)S(1)}, u32[]{:S(2)}, u32[]{:S(2)}) collective-permute-start(bf16[4,48,128]{2,1,0:T(8,128)(2,1)S(1)} %get-tuple-element.76), channel_id=1, source_target_pairs={{0,1},{1,2},{2,3},{3,0},{4,5},{5,6},{6,7},{7,4},{8,9},{9,10},{10,1... | collective-permute-start | bytes 147464 | tf_op jit(solution)/shard_map/ppermute | solution.py:409
  44.2 2.2 %collective-permute-start.15 = (bf16[4,48,128]{2,1,0:T(8,128)(2,1)S(1)}, bf16[4,48,128]{2,1,0:T(8,128)(2,1)S(1)}, u32[]{:S(2)}, u32[]{:S(2)}) collective-permute-start(bf16[4,48,128]{2,1,0:T(8,128)(2,1)S(1)} %get-tuple-element.77), channel_id=1, source_target_pairs={{0,2},{1,3},{2,0},{3,1},{4,6},{5,7},{6,4},{7,5},{8,10},{9,11},{10,... | collective-permute-start | bytes 147464 | tf_op jit(solution)/shard_map/ppermute | solution.py:409
  46.9 1.2 %collective-permute-start.17 = (bf16[4,48,128]{2,1,0:T(8,128)(2,1)S(1)}, bf16[4,48,128]{2,1,0:T(8,128)(2,1)S(1)}, u32[]{:S(2)}, u32[]{:S(2)}) collective-permute-start(bf16[4,48,128]{2,1,0:T(8,128)(2,1)S(1)} %get-tuple-element.75.a0), channel_id=1, source_target_pairs={{0,4},{4,0},{8,12},{12,8},{16,20},{20,16},{24,28},{28,24},{32,36},... | collective-permute-start | bytes 147464 | tf_op jit(solution)/shard_map/ppermute | solution.py:414
  49.1 1.3 %collective-permute-start.19 = (bf16[4,48,128]{2,1,0:T(8,128)(2,1)S(1)}, bf16[4,48,128]{2,1,0:T(8,128)(2,1)S(1)}, u32[]{:S(2)}, u32[]{:S(2)}) collective-permute-start(bf16[4,48,128]{2,1,0:T(8,128)(2,1)S(1)} %collective-permute-done.15.a2), channel_id=1, source_target_pairs={{0,4},{4,0},{8,12},{12,8},{16,20},{20,16},{24,28},{28,24},{32,36},... | collective-permute-start | bytes 147464 | tf_op jit(solution)/shard_map/ppermute | solution.py:414
  50.4 1.0 %collective-permute-start.20 = (bf16[4,48,128]{2,1,0:T(8,128)(2,1)S(1)}, bf16[4,48,128]{2,1,0:T(8,128)(2,1)S(1)}, u32[]{:S(2)}, u32[]{:S(2)}) collective-permute-start(bf16[4,48,128]{2,1,0:T(8,128)(2,1)S(1)} %collective-permute-done.16.a3), channel_id=1, source_target_pairs={{0,4},{4,0},{8,12},{12,8},{16,20},{20,16},{24,28},{28,24},{32,36},... | collective-permute-start | bytes 147464 | tf_op jit(solution)/shard_map/ppermute | solution.py:414
  51.5 0.9 collective-permute-done.20.b3
  52.3 1.5 %shard_map.136 = bf16[32,48,128]{2,1,0:T(8,128)(2,1)} custom-call(s32[80]{0:T(128)S(1)} %get-tuple-element.49.table, bf16[4,48,128]{2,1,0:T(8,128)(2,1)S(1)} %get-tuple-element.75.a0, bf16[4,48,128]{2,1,0:T(8,128)(2,1)S(1)} %collective-permute-done.14.a1, bf16[4,48,128]{2,1,0:T(8,128)(2,1)S(1)} %collective-permute-done.15.a2, ...), custom_call_target="tpu_custom_call" | custom-call | tf_op jit(solution)/shard_map/pallas_call | solution.py:394
  53.8 13.9 %all-to-all-start = ((bf16[32,48,128]{2,1,0:T(8,128)(2,1)}), bf16[32,48,128]{2,1,0:T(8,128)(2,1)S(1)}, u32[]{:S(2)}, u32[]{:S(2)}) async-start(bf16[32,48,128]{2,1,0:T(8,128)(2,1)} %shard_map.136), calls=%async_computation | async-start | bytes 786432 | tf_op jit(solution)/shard_map/all_to_all | solution.py:546
  67.8 2.6 %collective-permute-start.25 = (bf16[4,160,128]{2,1,0:T(8,128)(2,1)S(1)}, bf16[4,160,128]{2,1,0:T(8,128)(2,1)S(1)}, u32[]{:S(2)}, u32[]{:S(2)}) collective-permute-start(bf16[4,160,128]{2,1,0:T(8,128)(2,1)S(1)} %get-tuple-element.81.a0), channel_id=1, source_target_pairs={{0,2},{1,3},{2,0},{3,1},{4,6},{5,7},{6,4},{7,5},{8,10},{9,11},{10,... | collective-permute-start | bytes 491528 | tf_op jit(solution)/shard_map/ppermute | solution.py:409
  71.3 6.6 %all-to-all-done.got = bf16[32,48,128]{2,1,0:T(8,128)(2,1)S(1)} async-done(((bf16[32,48,128]{2,1,0:T(8,128)(2,1)}), bf16[32,48,128]{2,1,0:T(8,128)(2,1)S(1)}, u32[]{:S(2)}, u32[]{:S(2)}) %all-to-all-start) | async-done | bytes 393248 | tf_op jit(solution)/shard_map/all_to_all | solution.py:546
  78.7 1.2 %collective-permute-start.27 = (bf16[16,160,128]{2,1,0:T(8,128)(2,1)S(1)}, bf16[16,160,128]{2,1,0:T(8,128)(2,1)S(1)}, u32[]{:S(2)}, u32[]{:S(2)}) collective-permute-start(bf16[16,160,128]{2,1,0:T(8,128)(2,1)S(1)} %pad_maximum_fusion), channel_id=1, source_target_pairs={{0,4},{4,0},{8,12},{12,8},{16,20},{20,16},{24,28},{28,24},{32,36},... | collective-permute-start | bytes 1966088 | tf_op jit(solution)/shard_map/ppermute | solution.py:414
  80.7 2.8 %collective-permute-start.22 = (bf16[6,48,128]{2,1,0:T(8,128)(2,1)S(1)}, bf16[6,48,128]{2,1,0:T(8,128)(2,1)S(1)}, u32[]{:S(2)}, u32[]{:S(2)}) collective-permute-start(bf16[6,48,128]{2,1,0:T(8,128)(2,1)S(1)} %shard_map.137.b0), channel_id=1, source_target_pairs={{0,2},{1,3},{2,0},{3,1},{4,6},{5,7},{6,4},{7,5},{8,10},{9,11},{10,... | collective-permute-start | bytes 221192 | tf_op jit(solution)/shard_map/ppermute | solution.py:409
  83.5 2.0 %shard_map.138 = f32[4,80,1024]{2,1,0:T(8,128)} custom-call(s32[80]{0:T(128)S(1)} %get-tuple-element.49.table, bf16[4,160,128]{2,1,0:T(8,128)(2,1)S(1)} %get-tuple-element.81.a0, bf16[4,160,128]{2,1,0:T(8,128)(2,1)S(1)} %collective-permute-done.24.a1, bf16[4,160,128]{2,1,0:T(8,128)(2,1)S(1)} %collective-permute-done.25.a2, ...), custom_call_target="tpu_custom_call" | custom-call | tf_op jit(solution)/shard_map/pallas_call | solution.py:394
  85.4 2.0 %collective-permute-done.22.b2 = bf16[6,48,128]{2,1,0:T(8,128)(2,1)S(1)} collective-permute-done((bf16[6,48,128]{2,1,0:T(8,128)(2,1)S(1)}, bf16[6,48,128]{2,1,0:T(8,128)(2,1)S(1)}, u32[]{:S(2)}, u32[]{:S(2)}) %collective-permute-start.22) | collective-permute-done | bytes 73760 | tf_op jit(solution)/shard_map/ppermute | solution.py:409
  87.4 0.8 shard_map.139
  (58 shorter events, 7.9 us)
Async XLA Ops:
  0.6 10.6 %copy-start.3 = (f32[16,1024]{1,0:T(8,128)S(1)}, f32[16,1024]{1,0:T(8,128)}, u32[]{:S(2)}) copy-start(f32[16,1024]{1,0:T(8,128)} %constant.2.clone.e_rows_h.e_rows) | copy-start | bytes 196612
  0.6 10.6 %copy-start = (bf16[160,1024]{1,0:T(8,128)(2,1)S(1)}, bf16[160,1024]{1,0:T(8,128)(2,1)}, u32[]{:S(2)}) copy-start(bf16[160,1024]{1,0:T(8,128)(2,1)} %w_in.3) | copy-start | bytes 983044
  3.8 7.4 %collective-permute-start = (bf16[4,80,2048]{2,1,0:T(8,128)(2,1)S(1)}, bf16[4,80,2048]{2,1,0:T(8,128)(2,1)S(1)}, u32[]{:S(2)}, u32[]{:S(2)}) collective-permute-start(bf16[4,80,2048]{2,1,0:T(8,128)(2,1)S(1)} %copy-done.1), channel_id=1, source_target_pairs={{0,4},{4,0},{8,12},{12,8},{16,20},{20,16},{24,28},{28,24},{32,36},... | collective-permute-start | bytes 3932168 | tf_op jit(solution)/shard_map/ppermute | solution.py:414
  5.3 5.8 %collective-permute-start.1 = (bf16[4,80,1024]{2,1,0:T(8,128)(2,1)}, bf16[4,80,1024]{2,1,0:T(8,128)(2,1)S(1)}, u32[]{:S(2)}, u32[]{:S(2)}) collective-permute-start(bf16[4,80,1024]{2,1,0:T(8,128)(2,1)} %noise_a), channel_id=1, source_target_pairs={{0,4},{4,0},{8,12},{12,8},{16,20},{20,16},{24,28},{28,24},{32,36},... | collective-permute-start | bytes 1966088 | tf_op jit(solution)/shard_map/ppermute | solution.py:414
  5.4 10.4 %collective-permute-start.2 = (bf16[3,176,128]{2,1,0:T(8,128)(2,1)}, bf16[3,176,128]{2,1,0:T(8,128)(2,1)S(1)}, u32[]{:S(2)}, u32[]{:S(2)}) collective-permute-start(bf16[3,176,128]{2,1,0:T(8,128)(2,1)} %get-tuple-element.46), channel_id=1, source_target_pairs={{0,1},{1,2},{2,3},{3,0},{4,5},{5,6},{6,7},{7,4},{8,9},{9,10},{10,1... | collective-permute-start | bytes 405512 | tf_op jit(solution)/shard_map/ppermute | solution.py:409
  7.1 9.7 %collective-permute-start.3 = (bf16[3,176,128]{2,1,0:T(8,128)(2,1)}, bf16[3,176,128]{2,1,0:T(8,128)(2,1)S(1)}, u32[]{:S(2)}, u32[]{:S(2)}) collective-permute-start(bf16[3,176,128]{2,1,0:T(8,128)(2,1)} %get-tuple-element.46), channel_id=1, source_target_pairs={{0,2},{1,3},{2,0},{3,1},{4,6},{5,7},{6,4},{7,5},{8,10},{9,11},{10,... | collective-permute-start | bytes 405512 | tf_op jit(solution)/shard_map/ppermute | solution.py:409
  10.5 6.4 %collective-permute-start.4 = (bf16[3,176,128]{2,1,0:T(8,128)(2,1)}, bf16[3,176,128]{2,1,0:T(8,128)(2,1)S(1)}, u32[]{:S(2)}, u32[]{:S(2)}) collective-permute-start(bf16[3,176,128]{2,1,0:T(8,128)(2,1)} %get-tuple-element.46), channel_id=1, source_target_pairs={{0,3},{1,0},{2,1},{3,2},{4,7},{5,4},{6,5},{7,6},{8,11},{9,8},{10,9... | collective-permute-start | bytes 405512 | tf_op jit(solution)/shard_map/ppermute | solution.py:409
  12.3 12.0 %copy-start.5 = (bf16[3,176,256]{2,1,0:T(8,128)(2,1)S(1)}, bf16[3,176,256]{2,1,0:T(8,128)(2,1)}, u32[]{:S(2)}) copy-start(bf16[3,176,256]{2,1,0:T(8,128)(2,1)} %get-tuple-element.58.wp0) | copy-start | bytes 811012
  16.8 6.1 %collective-permute-start.5 = (bf16[3,176,128]{2,1,0:T(8,128)(2,1)S(1)}, bf16[3,176,128]{2,1,0:T(8,128)(2,1)S(1)}, u32[]{:S(2)}, u32[]{:S(2)}) collective-permute-start(bf16[3,176,128]{2,1,0:T(8,128)(2,1)S(1)} %collective-permute-done.2.hp1), channel_id=1, source_target_pairs={{0,4},{4,0},{8,12},{12,8},{16,20},{20,16},{24,28},{28,24},{32,36},... | collective-permute-start | bytes 405512 | tf_op jit(solution)/shard_map/ppermute | solution.py:414
  18.1 10.3 %collective-permute-start.8 = (bf16[1024,128]{1,0:T(8,128)(2,1)S(1)}, bf16[1024,128]{1,0:T(8,128)(2,1)S(1)}, u32[]{:S(2)}, u32[]{:S(2)}) collective-permute-start(bf16[1024,128]{1,0:T(8,128)(2,1)S(1)} %get-tuple-element.60), channel_id=1, source_target_pairs={{0,1},{1,2},{2,3},{3,0},{4,5},{5,6},{6,7},{7,4},{8,9},{9,10},{10,1... | collective-permute-start | bytes 786440 | tf_op jit(solution)/shard_map/ppermute | solution.py:409
  19.0 14.2 %collective-permute-start.9 = (bf16[1024,128]{1,0:T(8,128)(2,1)S(1)}, bf16[1024,128]{1,0:T(8,128)(2,1)S(1)}, u32[]{:S(2)}, u32[]{:S(2)}) collective-permute-start(bf16[1024,128]{1,0:T(8,128)(2,1)S(1)} %get-tuple-element.60), channel_id=1, source_target_pairs={{0,2},{1,3},{2,0},{3,1},{4,6},{5,7},{6,4},{7,5},{8,10},{9,11},{10,... | collective-permute-start | bytes 786440 | tf_op jit(solution)/shard_map/ppermute | solution.py:409
  21.1 12.1 %collective-permute-start.10 = (bf16[1024,128]{1,0:T(8,128)(2,1)S(1)}, bf16[1024,128]{1,0:T(8,128)(2,1)S(1)}, u32[]{:S(2)}, u32[]{:S(2)}) collective-permute-start(bf16[1024,128]{1,0:T(8,128)(2,1)S(1)} %get-tuple-element.60), channel_id=1, source_target_pairs={{0,3},{1,0},{2,1},{3,2},{4,7},{5,4},{6,5},{7,6},{8,11},{9,8},{10,9... | collective-permute-start | bytes 786440 | tf_op jit(solution)/shard_map/ppermute | solution.py:409
  22.1 1.8 %collective-permute-start.6 = (bf16[3,176,128]{2,1,0:T(8,128)(2,1)S(1)}, bf16[3,176,128]{2,1,0:T(8,128)(2,1)S(1)}, u32[]{:S(2)}, u32[]{:S(2)}) collective-permute-start(bf16[3,176,128]{2,1,0:T(8,128)(2,1)S(1)} %collective-permute-done.3.hp2), channel_id=1, source_target_pairs={{0,4},{4,0},{8,12},{12,8},{16,20},{20,16},{24,28},{28,24},{32,36},... | collective-permute-start | bytes 405512 | tf_op jit(solution)/shard_map/ppermute | solution.py:414
  23.0 1.4 %collective-permute-start.7 = (bf16[3,176,128]{2,1,0:T(8,128)(2,1)S(1)}, bf16[3,176,128]{2,1,0:T(8,128)(2,1)S(1)}, u32[]{:S(2)}, u32[]{:S(2)}) collective-permute-start(bf16[3,176,128]{2,1,0:T(8,128)(2,1)S(1)} %collective-permute-done.4.hp3), channel_id=1, source_target_pairs={{0,4},{4,0},{8,12},{12,8},{16,20},{20,16},{24,28},{28,24},{32,36},... | collective-permute-start | bytes 405512 | tf_op jit(solution)/shard_map/ppermute | solution.py:414
  33.2 2.3 %collective-permute-start.11 = (bf16[1024,128]{1,0:T(8,128)(2,1)S(1)}, bf16[1024,128]{1,0:T(8,128)(2,1)S(1)}, u32[]{:S(2)}, u32[]{:S(2)}) collective-permute-start(bf16[1024,128]{1,0:T(8,128)(2,1)S(1)} %collective-permute-done.8.ho1), channel_id=1, source_target_pairs={{0,4},{4,0},{8,12},{12,8},{16,20},{20,16},{24,28},{28,24},{32,36},... | collective-permute-start | bytes 786440 | tf_op jit(solution)/shard_map/ppermute | solution.py:414
  34.3 1.5 %collective-permute-start.12 = (bf16[1024,128]{1,0:T(8,128)(2,1)S(1)}, bf16[1024,128]{1,0:T(8,128)(2,1)S(1)}, u32[]{:S(2)}, u32[]{:S(2)}) collective-permute-start(bf16[1024,128]{1,0:T(8,128)(2,1)S(1)} %collective-permute-done.9.ho2), channel_id=1, source_target_pairs={{0,4},{4,0},{8,12},{12,8},{16,20},{20,16},{24,28},{28,24},{32,36},... | collective-permute-start | bytes 786440 | tf_op jit(solution)/shard_map/ppermute | solution.py:414
  34.3 1.9 %collective-permute-start.13 = (bf16[1024,128]{1,0:T(8,128)(2,1)S(1)}, bf16[1024,128]{1,0:T(8,128)(2,1)S(1)}, u32[]{:S(2)}, u32[]{:S(2)}) collective-permute-start(bf16[1024,128]{1,0:T(8,128)(2,1)S(1)} %collective-permute-done.10.ho3), channel_id=1, source_target_pairs={{0,4},{4,0},{8,12},{12,8},{16,20},{20,16},{24,28},{28,24},{32,36},... | collective-permute-start | bytes 786440 | tf_op jit(solution)/shard_map/ppermute | solution.py:414
  42.8 5.3 %collective-permute-start.14 = (bf16[4,48,128]{2,1,0:T(8,128)(2,1)S(1)}, bf16[4,48,128]{2,1,0:T(8,128)(2,1)S(1)}, u32[]{:S(2)}, u32[]{:S(2)}) collective-permute-start(bf16[4,48,128]{2,1,0:T(8,128)(2,1)S(1)} %get-tuple-element.76), channel_id=1, source_target_pairs={{0,1},{1,2},{2,3},{3,0},{4,5},{5,6},{6,7},{7,4},{8,9},{9,10},{10,1... | collective-permute-start | bytes 147464 | tf_op jit(solution)/shard_map/ppermute | solution.py:409
  44.2 4.9 %collective-permute-start.15 = (bf16[4,48,128]{2,1,0:T(8,128)(2,1)S(1)}, bf16[4,48,128]{2,1,0:T(8,128)(2,1)S(1)}, u32[]{:S(2)}, u32[]{:S(2)}) collective-permute-start(bf16[4,48,128]{2,1,0:T(8,128)(2,1)S(1)} %get-tuple-element.77), channel_id=1, source_target_pairs={{0,2},{1,3},{2,0},{3,1},{4,6},{5,7},{6,4},{7,5},{8,10},{9,11},{10,... | collective-permute-start | bytes 147464 | tf_op jit(solution)/shard_map/ppermute | solution.py:409
  46.4 4.0 %collective-permute-start.16 = (bf16[4,48,128]{2,1,0:T(8,128)(2,1)S(1)}, bf16[4,48,128]{2,1,0:T(8,128)(2,1)S(1)}, u32[]{:S(2)}, u32[]{:S(2)}) collective-permute-start(bf16[4,48,128]{2,1,0:T(8,128)(2,1)S(1)} %get-tuple-element.78), channel_id=1, source_target_pairs={{0,3},{1,0},{2,1},{3,2},{4,7},{5,4},{6,5},{7,6},{8,11},{9,8},{10,9... | collective-permute-start | bytes 147464 | tf_op jit(solution)/shard_map/ppermute | solution.py:409
  46.9 4.5 %collective-permute-start.17 = (bf16[4,48,128]{2,1,0:T(8,128)(2,1)S(1)}, bf16[4,48,128]{2,1,0:T(8,128)(2,1)S(1)}, u32[]{:S(2)}, u32[]{:S(2)}) collective-permute-start(bf16[4,48,128]{2,1,0:T(8,128)(2,1)S(1)} %get-tuple-element.75.a0), channel_id=1, source_target_pairs={{0,4},{4,0},{8,12},{12,8},{16,20},{20,16},{24,28},{28,24},{32,36},... | collective-permute-start | bytes 147464 | tf_op jit(solution)/shard_map/ppermute | solution.py:414
  48.1 3.3 %collective-permute-start.18 = (bf16[4,48,128]{2,1,0:T(8,128)(2,1)S(1)}, bf16[4,48,128]{2,1,0:T(8,128)(2,1)S(1)}, u32[]{:S(2)}, u32[]{:S(2)}) collective-permute-start(bf16[4,48,128]{2,1,0:T(8,128)(2,1)S(1)} %collective-permute-done.14.a1), channel_id=1, source_target_pairs={{0,4},{4,0},{8,12},{12,8},{16,20},{20,16},{24,28},{28,24},{32,36},... | collective-permute-start | bytes 147464 | tf_op jit(solution)/shard_map/ppermute | solution.py:414
  49.1 2.3 %collective-permute-start.19 = (bf16[4,48,128]{2,1,0:T(8,128)(2,1)S(1)}, bf16[4,48,128]{2,1,0:T(8,128)(2,1)S(1)}, u32[]{:S(2)}, u32[]{:S(2)}) collective-permute-start(bf16[4,48,128]{2,1,0:T(8,128)(2,1)S(1)} %collective-permute-done.15.a2), channel_id=1, source_target_pairs={{0,4},{4,0},{8,12},{12,8},{16,20},{20,16},{24,28},{28,24},{32,36},... | collective-permute-start | bytes 147464 | tf_op jit(solution)/shard_map/ppermute | solution.py:414
  50.4 1.9 %collective-permute-start.20 = (bf16[4,48,128]{2,1,0:T(8,128)(2,1)S(1)}, bf16[4,48,128]{2,1,0:T(8,128)(2,1)S(1)}, u32[]{:S(2)}, u32[]{:S(2)}) collective-permute-start(bf16[4,48,128]{2,1,0:T(8,128)(2,1)S(1)} %collective-permute-done.16.a3), channel_id=1, source_target_pairs={{0,4},{4,0},{8,12},{12,8},{16,20},{20,16},{24,28},{28,24},{32,36},... | collective-permute-start | bytes 147464 | tf_op jit(solution)/shard_map/ppermute | solution.py:414
  53.8 24.1 %all-to-all-start = ((bf16[32,48,128]{2,1,0:T(8,128)(2,1)}), bf16[32,48,128]{2,1,0:T(8,128)(2,1)S(1)}, u32[]{:S(2)}, u32[]{:S(2)}) async-start(bf16[32,48,128]{2,1,0:T(8,128)(2,1)} %shard_map.136), calls=%async_computation | async-start | bytes 786432 | tf_op jit(solution)/shard_map/all_to_all | solution.py:546
  67.7 10.9 %collective-permute-start.24 = (bf16[4,160,128]{2,1,0:T(8,128)(2,1)S(1)}, bf16[4,160,128]{2,1,0:T(8,128)(2,1)S(1)}, u32[]{:S(2)}, u32[]{:S(2)}) collective-permute-start(bf16[4,160,128]{2,1,0:T(8,128)(2,1)S(1)} %get-tuple-element.81.a0), channel_id=1, source_target_pairs={{0,1},{1,2},{2,3},{3,0},{4,5},{5,6},{6,7},{7,4},{8,9},{9,10},{10,1... | collective-permute-start | bytes 491528 | tf_op jit(solution)/shard_map/ppermute | solution.py:409
  67.8 10.8 %collective-permute-start.25 = (bf16[4,160,128]{2,1,0:T(8,128)(2,1)S(1)}, bf16[4,160,128]{2,1,0:T(8,128)(2,1)S(1)}, u32[]{:S(2)}, u32[]{:S(2)}) collective-permute-start(bf16[4,160,128]{2,1,0:T(8,128)(2,1)S(1)} %get-tuple-element.81.a0), channel_id=1, source_target_pairs={{0,2},{1,3},{2,0},{3,1},{4,6},{5,7},{6,4},{7,5},{8,10},{9,11},{10,... | collective-permute-start | bytes 491528 | tf_op jit(solution)/shard_map/ppermute | solution.py:409
  70.4 8.2 %collective-permute-start.26 = (bf16[4,160,128]{2,1,0:T(8,128)(2,1)S(1)}, bf16[4,160,128]{2,1,0:T(8,128)(2,1)S(1)}, u32[]{:S(2)}, u32[]{:S(2)}) collective-permute-start(bf16[4,160,128]{2,1,0:T(8,128)(2,1)S(1)} %get-tuple-element.81.a0), channel_id=1, source_target_pairs={{0,3},{1,0},{2,1},{3,2},{4,7},{5,4},{6,5},{7,6},{8,11},{9,8},{10,9... | collective-permute-start | bytes 491528 | tf_op jit(solution)/shard_map/ppermute | solution.py:409
  78.7 4.7 %collective-permute-start.27 = (bf16[16,160,128]{2,1,0:T(8,128)(2,1)S(1)}, bf16[16,160,128]{2,1,0:T(8,128)(2,1)S(1)}, u32[]{:S(2)}, u32[]{:S(2)}) collective-permute-start(bf16[16,160,128]{2,1,0:T(8,128)(2,1)S(1)} %pad_maximum_fusion), channel_id=1, source_target_pairs={{0,4},{4,0},{8,12},{12,8},{16,20},{20,16},{24,28},{28,24},{32,36},... | collective-permute-start | bytes 1966088 | tf_op jit(solution)/shard_map/ppermute | solution.py:414
  79.9 5.5 %collective-permute-start.21 = (bf16[6,48,128]{2,1,0:T(8,128)(2,1)S(1)}, bf16[6,48,128]{2,1,0:T(8,128)(2,1)S(1)}, u32[]{:S(2)}, u32[]{:S(2)}) collective-permute-start(bf16[6,48,128]{2,1,0:T(8,128)(2,1)S(1)} %shard_map.137.b0), channel_id=1, source_target_pairs={{0,1},{1,2},{2,3},{3,0},{4,5},{5,6},{6,7},{7,4},{8,9},{9,10},{10,1... | collective-permute-start | bytes 221192 | tf_op jit(solution)/shard_map/ppermute | solution.py:409
  80.7 6.7 %collective-permute-start.22 = (bf16[6,48,128]{2,1,0:T(8,128)(2,1)S(1)}, bf16[6,48,128]{2,1,0:T(8,128)(2,1)S(1)}, u32[]{:S(2)}, u32[]{:S(2)}) collective-permute-start(bf16[6,48,128]{2,1,0:T(8,128)(2,1)S(1)} %shard_map.137.b0), channel_id=1, source_target_pairs={{0,2},{1,3},{2,0},{3,1},{4,6},{5,7},{6,4},{7,5},{8,10},{9,11},{10,... | collective-permute-start | bytes 221192 | tf_op jit(solution)/shard_map/ppermute | solution.py:409
  83.5 3.9 %collective-permute-start.23 = (bf16[6,48,128]{2,1,0:T(8,128)(2,1)S(1)}, bf16[6,48,128]{2,1,0:T(8,128)(2,1)S(1)}, u32[]{:S(2)}, u32[]{:S(2)}) collective-permute-start(bf16[6,48,128]{2,1,0:T(8,128)(2,1)S(1)} %shard_map.137.b0), channel_id=1, source_target_pairs={{0,3},{1,0},{2,1},{3,2},{4,7},{5,4},{6,5},{7,6},{8,11},{9,8},{10,9... | collective-permute-start | bytes 221192 | tf_op jit(solution)/shard_map/ppermute | solution.py:409
  (8 other events, 44.4 us)
